TPU v7x, 32 devices: a whole 2x2x4 slice. The times are simulated.
32 devices in a mesh: grp: 2 (over x), seq: 4 (over y, core), head: 4 (over z).
Axes of the slice: x: 2, y: 2, z: 4, core: 2. Of those that a mesh axis runs over, the one named last changes fastest.
Arguments:
- queries: bfloat16 [256, 4096], P(('grp', 'seq'), 'head'), parts along dimension 0, may hold values from -6 to 6
- root_keys: bfloat16 [8192, 4096], P(('grp', 'seq'), 'head'), parts along dimension 0, may hold values from -6 to 6
- root_values: bfloat16 [8192, 4096], P(('grp', 'seq'), 'head'), parts along dimension 0, may hold values from -6 to 6
- branch_keys: bfloat16 [8192, 4096], P(('grp', 'seq'), 'head'), parts along dimension 0, may hold values from -6 to 6
- branch_values: bfloat16 [8192, 4096], P(('grp', 'seq'), 'head'), parts along dimension 0, may hold values from -6 to 6
- branch_lengths: int32 [8], P(('grp', 'seq')), parts along dimension 0, may hold values from 1 to 1024, 2560 in all
- branch_ids: int32 [256], P('grp'), parts along dimension 0, may hold values from 0 to 3
- slopes: float32 [32], P('head'), may hold values from 0.0001953125 to 0.08
Outputs:
- attended: bfloat16 [256, 4096], P(('grp', 'seq'), 'head'), parts along dimension 0
There are 2 independent parts, one for each index of `grp`. A program takes and returns all parts, laid end to end along the dimension named above; an argument that names none is the same for every part. Nothing has to cross between parts.
Inputs may be any that keep to these rules, and one draw needn't show every extreme that they name: `branch_lengths`: the longest branch holds exactly 1024 live positions; each holds at least one.
All inputs are finite; a program needn't handle non-finite values. No bound on the sum of `branch_lengths` on one device may be relied on, other than what follows from the above.
Results may differ from a plain program's by a relative error of at most 0.0041.
Values may be sent and summed in bfloat16 or wider, within the bound.
No kernel may reach another device: no remote copies, remote signals or barrier semaphores. Data moves between devices by JAX's collectives and lax.ppermute only.
A program may use at most 128 MiB of HBM per device.

v0:
```python
import jax
import jax.numpy as jnp
from jax import lax
from jax.sharding import PartitionSpec as P


def combined_all(array, axis, combine):
    everything = jax.tree.map(lambda part: lax.all_gather(part, axis), array)
    initial = jax.tree.map(lambda part: part[0], everything)

    def step(k, so_far):
        return combine(so_far, jax.tree.map(lambda part: part[k], everything))

    return lax.fori_loop(1, lax.axis_size(axis), step, initial)


def join(first, second):
    top = jnp.maximum(first[0], second[0])
    left = jnp.exp(first[0] - top)
    right = jnp.exp(second[0] - top)
    head_size = first[2].shape[-1] // first[0].shape[-1]
    total = left * first[1] + right * second[1]
    mixed = (
        jnp.repeat(left, head_size, axis=-1) * first[2]
        + jnp.repeat(right, head_size, axis=-1) * second[2]
    )
    return (top, total, mixed)


def shards(
    queries, root_keys, root_values, branch_keys, branch_values, branch_lengths, branch_ids, slopes
):
    seq_count = lax.axis_size("seq")
    seq_index = lax.axis_index("seq")
    heads_dev = slopes.shape[0]
    head_size = queries.shape[1] // heads_dev
    root_dev = root_keys.shape[0]
    branch_len = branch_keys.shape[0]
    query_dev = queries.shape[0]
    scale = 1.0 / head_size**0.5
    dims = (((1,), (1,)), ((), ()))
    every_query = lax.all_gather(queries, "seq", axis=0, tiled=True)
    span = root_dev * seq_count + branch_len
    root_pos = (seq_index * root_dev + jnp.arange(root_dev)).astype(jnp.float32) - span
    offset = jnp.arange(branch_len)
    branch_pos = offset.astype(jnp.float32) - branch_len
    match = (branch_ids[:, None] == seq_index) & (offset < branch_lengths[0])[None, :]
    tops = []
    totals = []
    mixes = []
    for head in range(heads_dev):
        cols = slice(head * head_size, (head + 1) * head_size)
        query = every_query[:, cols]
        scores = (
            lax.dot_general(query, root_keys[:, cols], dims, preferred_element_type=jnp.float32)
            * scale
            + slopes[head] * root_pos[None, :]
        )
        top_root = jnp.max(scores, axis=1)
        weights = jnp.exp(scores - top_root[:, None])
        total_root = jnp.sum(weights, axis=1)
        out_root = jnp.dot(
            weights.astype(jnp.bfloat16), root_values[:, cols], preferred_element_type=jnp.float32
        )
        bscores = (
            lax.dot_general(query, branch_keys[:, cols], dims, preferred_element_type=jnp.float32)
            * scale
            + slopes[head] * branch_pos[None, :]
        )
        top_branch = jnp.max(jnp.where(match, bscores, -jnp.inf), axis=1)
        bweights = jnp.where(match, jnp.exp(bscores - top_branch[:, None]), 0.0)
        total_branch = jnp.sum(bweights, axis=1)
        out_branch = jnp.dot(
            bweights.astype(jnp.bfloat16),
            branch_values[:, cols],
            preferred_element_type=jnp.float32,
        )
        top = jnp.maximum(top_root, top_branch)
        factor_root = jnp.exp(top_root - top)
        factor_branch = jnp.exp(top_branch - top)
        tops.append(top)
        totals.append(factor_root * total_root + factor_branch * total_branch)
        mixes.append(factor_root[:, None] * out_root + factor_branch[:, None] * out_branch)
    top_all = jnp.stack(tops, axis=1)
    total_all = jnp.stack(totals, axis=1)
    mix_all = jnp.concatenate(mixes, axis=1)
    merged = combined_all((top_all, total_all, mix_all), "seq", join)
    own_total = lax.dynamic_slice_in_dim(merged[1], seq_index * query_dev, query_dev, 0)
    own_mix = lax.dynamic_slice_in_dim(merged[2], seq_index * query_dev, query_dev, 0)
    return (own_mix / jnp.repeat(own_total, head_size, axis=-1)).astype(jnp.bfloat16)


def solution(mesh):
    in_specs = (
        P(("grp", "seq"), "head"),
        P(("grp", "seq"), "head"),
        P(("grp", "seq"), "head"),
        P(("grp", "seq"), "head"),
        P(("grp", "seq"), "head"),
        P(("grp", "seq")),
        P("grp"),
        P("head"),
    )
    out_specs = P(("grp", "seq"), "head")
    return jax.shard_map(shards, mesh=mesh, in_specs=in_specs, out_specs=out_specs, check_vma=False)
```

profile of v0, /device:TPU:0, one launch (start us, length us, event | category | flops | bytes accessed | tf_op | source)
XLA Modules:
  0.0 81.4 jit_solution(12630164083880661991)
XLA Ops:
  7.3 0.7 broadcast_compare_fusion
  8.0 1.6 %fusion.245 = (f32[1]{0:T(128)}, f32[1]{0:T(128)}, f32[1]{0:T(128)}, f32[1]{0:T(128)}, f32[1]{0:T(128)}, /*index=5*/f32[1]{0:T(128)}, f32[1]{0:T(128)}, f32[1]{0:T(128)}) fusion(f32[8]{0:T(128)} %param.17), kind=kLoop, calls=%fused_computation.352 | loop fusion | bytes 64 | tf_op jit(solution)/shard_map/slice | solution.py:57
  9.6 0.7 fusion.187
  10.3 0.7 fusion.182
  11.0 0.6 fusion.183
  11.6 0.6 fusion.184
  12.2 0.6 fusion.185
  12.8 0.6 fusion.186
  13.5 0.6 fusion.180
  14.1 0.6 fusion.181
  14.7 7.4 %all_gather.21 = bf16[128,1024]{1,0:T(8,128)(2,1)S(1)} all-gather(bf16[32,1024]{1,0:T(8,128)(2,1)} %param.10), channel_id=1, replica_groups=mesh['grp'=2,'seq'=4,'head'=4] {'seq'}, dimensions={0}, use_global_device_ids=true | all-gather | bytes 327680 | tf_op jit(solution)/shard_map/all_gather | solution.py:42
  22.1 1.2 %fusion.4 = f32[128,1024]{1,0:T(8,128)S(1)} fusion(f32[1024]{0:T(1024)S(1)} %get-tuple-element.294, bf16[1024,1024]{1,0:T(8,128)(2,1)} %param.13, bf16[128,1024]{1,0:T(8,128)(2,1)S(1)} %all_gather.21), kind=kOutput, calls=%fused_computation.42 | convolution fusion | flops 33816576 | bytes 823296 | tf_op jit(solution)/shard_map/dot_general | solution.py:66
  23.3 1.4 %fusion.6 = f32[128,1024]{1,0:T(8,128)S(1)} fusion(f32[1024]{0:T(1024)S(1)} %get-tuple-element.292, bf16[1024,1024]{1,0:T(8,128)(2,1)} %param.13, bf16[128,1024]{1,0:T(8,128)(2,1)S(1)} %all_gather.21), kind=kOutput, calls=%fused_computation.44 | convolution fusion | flops 33816576 | bytes 823296 | tf_op jit(solution)/shard_map/dot_general | solution.py:66
  26.1 1.4 %copy-done.17 = bf16[1024,1024]{1,0:T(8,128)(2,1)S(1)} copy-done((bf16[1024,1024]{1,0:T(8,128)(2,1)S(1)}, bf16[1024,1024]{1,0:T(8,128)(2,1)}, u32[]{:S(2)}) %copy-start.17) | copy-done | bytes 2097176
  27.7 0.3 fusion.252
  28.1 0.3 fusion.251
  28.4 0.3 fusion.250
  28.8 0.3 fusion.249
  29.1 0.3 fusion.248
  29.4 0.3 fusion.247
  30.1 1.8 %fusion.42 = (f32[128]{0:T(128)S(1)}, f32[128]{0:T(128)S(1)}, f32[128]{0:T(128)S(1)}, f32[128]{0:T(128)S(1)}, f32[128]{0:T(128)S(1)}, /*index=5*/f32[128]{0:T(12...) fusion(pred[1024]{0:T(1024)(128)(4,1)S(1)} %iota_compare_fusion, ...), kind=kOutput, calls=%fused_computation.96 | convolution fusion | flops 36043776 | bytes 4498944 | tf_op jit(solution)/shard_map/dot_general | solution.py:66
  32.0 0.3 convolution_multiply_fusion.30
  32.3 0.3 convolution_multiply_fusion.28
  32.7 0.4 convolution_multiply_fusion.26
  33.1 0.3 convolution_multiply_fusion.24
  33.5 0.4 convolution_multiply_fusion.22
  33.9 0.4 convolution_multiply_fusion.20
  34.3 0.3 convolution_multiply_fusion.18
  34.6 0.3 convolution_multiply_fusion.16
  35.1 1.0 %fusion.20 = f32[128,1024]{0,1:T(8,128)} fusion(f32[128,128]{0,1:T(8,128)S(1)} %convolution_multiply_fusion.30, f32[128,1024]{1,0:T(8,128)S(1)} %get-tuple-element.267, bf16[1024,1024]{1,0:T(8,128)(2,1)S(1)} %copy-done.18, f32[128]{0:T(128)S(1)} %get-tuple-element.266, f32[128]{0:T(128)S(1)} %get-tuple-element.239), kind=kOutput, calls=%fused_computation.74 | convolution fusion | flops 33849344 | bytes 918528 | tf_op jit(solution)/shard_map/dot_general | solution.py:62
  36.0 1.0 %fusion.22 = f32[128,1024]{0,1:T(8,128)} fusion(f32[128,1024]{0,1:T(8,128)} %fusion.20, f32[128,128]{0,1:T(8,128)S(1)} %convolution_multiply_fusion.28, f32[128,1024]{1,0:T(8,128)S(1)} %get-tuple-element.269, bf16[1024,1024]{1,0:T(8,128)(2,1)S(1)} %copy-done.18, f32[128]{0:T(128)S(1)} %get-tuple-element.268, f32[128]{0:T(128)S(1)} %get-tuple-element.237), kind=kOutput, calls=%fused_computation.76 | convolution fusion | flops 33849344 | bytes 918528 | tf_op jit(solution)/shard_map/dot_general | solution.py:62
  37.0 1.0 %fusion.24 = f32[128,1024]{0,1:T(8,128)} fusion(f32[128,1024]{0,1:T(8,128)} %fusion.22, f32[128,128]{0,1:T(8,128)S(1)} %convolution_multiply_fusion.26, f32[128,1024]{1,0:T(8,128)S(1)} %get-tuple-element.271, bf16[1024,1024]{1,0:T(8,128)(2,1)S(1)} %copy-done.18, f32[128]{0:T(128)S(1)} %get-tuple-element.270, f32[128]{0:T(128)S(1)} %get-tuple-element.235), kind=kOutput, calls=%fused_computation.78 | convolution fusion | flops 33849344 | bytes 918528 | tf_op jit(solution)/shard_map/dot_general | solution.py:62
  37.9 1.0 %fusion.26 = f32[128,1024]{0,1:T(8,128)} fusion(f32[128,1024]{0,1:T(8,128)} %fusion.24, f32[128,128]{0,1:T(8,128)S(1)} %convolution_multiply_fusion.24, f32[128,1024]{1,0:T(8,128)S(1)} %get-tuple-element.273, bf16[1024,1024]{1,0:T(8,128)(2,1)S(1)} %copy-done.18, f32[128]{0:T(128)S(1)} %get-tuple-element.272, f32[128]{0:T(128)S(1)} %get-tuple-element.233), kind=kOutput, calls=%fused_computation.80 | convolution fusion | flops 33849344 | bytes 918528 | tf_op jit(solution)/shard_map/dot_general | solution.py:62
  38.9 0.9 %fusion.28 = f32[128,1024]{0,1:T(8,128)} fusion(f32[128,1024]{0,1:T(8,128)} %fusion.26, f32[128,128]{0,1:T(8,128)S(1)} %convolution_multiply_fusion.22, f32[128,1024]{1,0:T(8,128)S(1)} %get-tuple-element.275, bf16[1024,1024]{1,0:T(8,128)(2,1)S(1)} %copy-done.18, f32[128]{0:T(128)S(1)} %get-tuple-element.274, f32[128]{0:T(128)S(1)} %get-tuple-element.231), kind=kOutput, calls=%fused_computation.82 | convolution fusion | flops 33849344 | bytes 918528 | tf_op jit(solution)/shard_map/dot_general | solution.py:62
  39.8 1.0 %fusion.30 = f32[128,1024]{0,1:T(8,128)} fusion(f32[128,1024]{0,1:T(8,128)} %fusion.28, f32[128,128]{0,1:T(8,128)S(1)} %convolution_multiply_fusion.20, f32[128,1024]{1,0:T(8,128)S(1)} %get-tuple-element.277, bf16[1024,1024]{1,0:T(8,128)(2,1)S(1)} %copy-done.18, f32[128]{0:T(128)S(1)} %get-tuple-element.276, f32[128]{0:T(128)S(1)} %get-tuple-element.229), kind=kOutput, calls=%fused_computation.84 | convolution fusion | flops 33849344 | bytes 918528 | tf_op jit(solution)/shard_map/dot_general | solution.py:62
  40.8 1.0 %fusion.32 = f32[128,1024]{0,1:T(8,128)} fusion(f32[128,1024]{0,1:T(8,128)} %fusion.30, f32[128,128]{0,1:T(8,128)S(1)} %convolution_multiply_fusion.18, f32[128,1024]{1,0:T(8,128)S(1)} %get-tuple-element.279, bf16[1024,1024]{1,0:T(8,128)(2,1)S(1)} %copy-done.18, f32[128]{0:T(128)S(1)} %get-tuple-element.278, f32[128]{0:T(128)S(1)} %get-tuple-element.227), kind=kOutput, calls=%fused_computation.86 | convolution fusion | flops 33849344 | bytes 918528 | tf_op jit(solution)/shard_map/dot_general | solution.py:62
  41.7 1.0 %fusion.34 = f32[128,1024]{0,1:T(8,128)} fusion(f32[128,1024]{0,1:T(8,128)} %fusion.32, f32[128,128]{0,1:T(8,128)S(1)} %convolution_multiply_fusion.16, f32[128,1024]{1,0:T(8,128)S(1)} %get-tuple-element.281, bf16[1024,1024]{1,0:T(8,128)(2,1)S(1)} %copy-done.18, f32[128]{0:T(128)S(1)} %get-tuple-element.280, f32[128]{0:T(128)S(1)} %get-tuple-element.225), kind=kOutput, calls=%fused_computation.88 | convolution fusion | flops 33849344 | bytes 918528 | tf_op jit(solution)/shard_map/dot_general | solution.py:62
  45.0 2.4 %fusion.74 = (f32[128]{0:T(128)S(1)}, f32[128]{0:T(128)S(1)}, f32[128]{0:T(128)S(1)}, f32[128]{0:T(128)S(1)}, f32[128]{0:T(128)S(1)}, /*index=5*/f32[128]{0:T(128)S(1)}, f32[128]{0:T(128)S(1)}, f32[128]{0:T(128)S(1)}) fusion(f32[128,1024]{1,0:T(8,128)} %copy-done.19, f32[128]{0:T(128)S(1)} %get-tuple-element.199, pred[1024]{0:T(1024)(128)(4,1)S(1)} %iota_compare_fusion, ...), kind=kLoop, calls=%fused_computation.136 | loop fusion | flops 3275776 | bytes 4203648 | tf_op jit(solution)/shard_map/reduce_sum | solution.py:72
  47.6 5.2 %all-gather = f32[512,8]{0,1:T(8,128)S(1)} all-gather(f32[128,8]{0,1:T(8,128)S(1)} %stack.4), channel_id=2, replica_groups=mesh['grp'=2,'seq'=4,'head'=4] {'seq'}, dimensions={0}, use_global_device_ids=true | all-gather | bytes 20480 | tf_op jit(solution)/shard_map/all_gather | solution.py:8
  52.8 5.2 %all-gather.1 = f32[512,8]{0,1:T(8,128)S(1)} all-gather(f32[128,8]{0,1:T(8,128)S(1)} %stack.5), channel_id=3, replica_groups=mesh['grp'=2,'seq'=4,'head'=4] {'seq'}, dimensions={0}, use_global_device_ids=true | all-gather | bytes 20480 | tf_op jit(solution)/shard_map/all_gather | solution.py:8
  58.0 9.1 %all-gather.5.cloned.1.call-done = f32[512,1024]{0,1:T(8,128)} async-done(((f32[128,1024]{0,1:T(8,128)}), f32[512,1024]{0,1:T(8,128)}) %all-gather.5.cloned.1.call-update) | async-done | bytes 2097168 | tf_op jit(solution)/shard_map/all_gather | solution.py:8
  67.1 1.1 %slice.225 = f32[128,1024]{0,1:T(8,128)S(1)} slice(f32[512,1024]{0,1:T(8,128)} %all-gather.5.cloned.1.call-done), slice={[0:128], [0:1024]} | slice | bytes 1048576 | tf_op jit(solution)/shard_map/slice | solution.py:9
  68.4 1.9 %copy.14 = f32[512,1024]{1,0:T(8,128)S(1)} copy(f32[512,1024]{0,1:T(8,128)} %all-gather.5.cloned.1.call-done) | data formatting | bytes 4194304 | tf_op jit(solution)/shard_map/while | solution.py:14
  70.3 3.3 %while.19 = (s32[]{:T(128)}, f32[128,8]{0,1:T(8,128)S(1)}, f32[128,8]{0,1:T(8,128)S(1)}, f32[128,1024]{1,0:T(8,128)S(1)}, f32[4,128,8]{1,2,0:T(8,128)S(1)}, /*in...) while((s32[]{:T(128)}, f32[128,8]{0,1:T(8,128)S(1)}, ...), condition=%wide.region_33.34_spmd, body=%wide.region_32.33_spmd.sunk | while | flops 399365 | bytes 3727503 | solution.py:14
  71.0 0.5 fusion.257
  72.1 0.5 fusion.257
  73.2 0.5 fusion.257
  73.9 0.7 fusion.163
  (98 shorter events, 6.7 us)
Async XLA Ops:
  6.5 18.2 %copy-start.16 = (bf16[1024,1024]{1,0:T(8,128)(2,1)S(1)}, bf16[1024,1024]{1,0:T(8,128)(2,1)}, u32[]{:S(2)}) copy-start(bf16[1024,1024]{1,0:T(8,128)(2,1)} %param.13) | copy-start | bytes 6291460
  6.5 60.6 %all-gather.5.cloned.1.call-start = ((), (), s32[]{:S(2)}) async-start(), calls=%async_computation | async-start | bytes 2621440 | tf_op jit(solution)/shard_map/all_gather | solution.py:8
  23.3 8.7 %copy-start.4 = (f32[128,1024]{1,0:T(8,128)}, f32[128,1024]{1,0:T(8,128)S(1)}, u32[]{:S(2)}) copy-start(f32[128,1024]{1,0:T(8,128)S(1)} %fusion.4) | copy-start | bytes 1572868
  24.7 7.7 %copy-start.6 = (f32[128,1024]{1,0:T(8,128)}, f32[128,1024]{1,0:T(8,128)S(1)}, u32[]{:S(2)}) copy-start(f32[128,1024]{1,0:T(8,128)S(1)} %fusion.6) | copy-start | bytes 1572868
  24.7 2.7 %copy-start.17 = (bf16[1024,1024]{1,0:T(8,128)(2,1)S(1)}, bf16[1024,1024]{1,0:T(8,128)(2,1)}, u32[]{:S(2)}) copy-start(bf16[1024,1024]{1,0:T(8,128)(2,1)} %param.11) | copy-start | bytes 6291460
  25.0 7.8 %copy-start.8 = (f32[128,1024]{1,0:T(8,128)}, f32[128,1024]{1,0:T(8,128)S(1)}, u32[]{:S(2)}) copy-start(f32[128,1024]{1,0:T(8,128)S(1)} %fusion.8) | copy-start | bytes 1572868
  25.2 7.9 %copy-start.10 = (f32[128,1024]{1,0:T(8,128)}, f32[128,1024]{1,0:T(8,128)S(1)}, u32[]{:S(2)}) copy-start(f32[128,1024]{1,0:T(8,128)S(1)} %fusion.10) | copy-start | bytes 1572868
  25.5 8.0 %copy-start.12 = (f32[128,1024]{1,0:T(8,128)}, f32[128,1024]{1,0:T(8,128)S(1)}, u32[]{:S(2)}) copy-start(f32[128,1024]{1,0:T(8,128)S(1)} %fusion.12) | copy-start | bytes 1572868
  25.8 8.1 %copy-start.14 = (f32[128,1024]{1,0:T(8,128)}, f32[128,1024]{1,0:T(8,128)S(1)}, u32[]{:S(2)}) copy-start(f32[128,1024]{1,0:T(8,128)S(1)} %fusion.14) | copy-start | bytes 1572868
  26.0 8.2 %copy-start.15 = (f32[128,1024]{1,0:T(8,128)}, f32[128,1024]{1,0:T(8,128)S(1)}, u32[]{:S(2)}) copy-start(f32[128,1024]{1,0:T(8,128)S(1)} %fusion.16) | copy-start | bytes 1572868
  29.8 6.3 %copy-start = (f32[128,1024]{1,0:T(8,128)}, f32[128,1024]{1,0:T(8,128)S(1)}, u32[]{:S(2)}) copy-start(f32[128,1024]{1,0:T(8,128)S(1)} %get-tuple-element.269) | copy-start | bytes 1572868
  30.1 4.9 %copy-start.2 = (f32[128,1024]{1,0:T(8,128)}, f32[128,1024]{1,0:T(8,128)S(1)}, u32[]{:S(2)}) copy-start(f32[128,1024]{1,0:T(8,128)S(1)} %get-tuple-element.267) | copy-start | bytes 1572868
  30.1 1.9 %copy-start.20 = (bf16[1024,1024]{1,0:T(8,128)(2,1)S(1)}, bf16[1024,1024]{1,0:T(8,128)(2,1)}, u32[]{:S(2)}) copy-start(bf16[1024,1024]{1,0:T(8,128)(2,1)} %param.14) | copy-start | bytes 6291460
  31.9 2.7 %copy-start.19 = (f32[128,1024]{1,0:T(8,128)}, f32[128,1024]{1,0:T(8,128)S(1)}, u32[]{:S(2)}) copy-start(f32[128,1024]{1,0:T(8,128)S(1)} %get-tuple-element.265) | copy-start | bytes 1572868
  33.5 1.6 %copy-start.18 = (bf16[1024,1024]{1,0:T(8,128)(2,1)S(1)}, bf16[1024,1024]{1,0:T(8,128)(2,1)}, u32[]{:S(2)}) copy-start(bf16[1024,1024]{1,0:T(8,128)(2,1)} %param.12) | copy-start | bytes 6291460
  43.0 1.2 %copy-start.1 = (f32[128,1024]{1,0:T(8,128)S(1)}, f32[128,1024]{1,0:T(8,128)}, u32[]{:S(2)}) copy-start(f32[128,1024]{1,0:T(8,128)} %copy-done) | copy-start | bytes 1572868
  43.0 1.5 %copy-start.3 = (f32[128,1024]{1,0:T(8,128)S(1)}, f32[128,1024]{1,0:T(8,128)}, u32[]{:S(2)}) copy-start(f32[128,1024]{1,0:T(8,128)} %copy-done.2) | copy-start | bytes 1572868
  43.0 1.7 %copy-start.5 = (f32[128,1024]{1,0:T(8,128)S(1)}, f32[128,1024]{1,0:T(8,128)}, u32[]{:S(2)}) copy-start(f32[128,1024]{1,0:T(8,128)} %copy-done.4) | copy-start | bytes 1572868
  43.0 1.7 %copy-start.7 = (f32[128,1024]{1,0:T(8,128)S(1)}, f32[128,1024]{1,0:T(8,128)}, u32[]{:S(2)}) copy-start(f32[128,1024]{1,0:T(8,128)} %copy-done.6) | copy-start | bytes 1572868
  43.0 1.7 %copy-start.9 = (f32[128,1024]{1,0:T(8,128)S(1)}, f32[128,1024]{1,0:T(8,128)}, u32[]{:S(2)}) copy-start(f32[128,1024]{1,0:T(8,128)} %copy-done.8) | copy-start | bytes 1572868
  43.0 1.8 %copy-start.11 = (f32[128,1024]{1,0:T(8,128)S(1)}, f32[128,1024]{1,0:T(8,128)}, u32[]{:S(2)}) copy-start(f32[128,1024]{1,0:T(8,128)} %copy-done.10) | copy-start | bytes 1572868
  43.0 1.9 %copy-start.13 = (f32[128,1024]{1,0:T(8,128)S(1)}, f32[128,1024]{1,0:T(8,128)}, u32[]{:S(2)}) copy-start(f32[128,1024]{1,0:T(8,128)} %copy-done.12) | copy-start | bytes 1572868
Sparse Core Ops, SparseCore 0:
  42.8 24.2 all-gather.4
where the time goes:
time: 82 us; the launch traced here: 81.4 us
  matrix products  18.7 us (23%)
  blocking collectives  17.8 us (22%)
  between operations  14.8 us (18%)
  other arithmetic  12.2 us (15%)
  waiting for transfers between devices  9.11 us (11%)
  local copies, waits for them, and re-layouts  8.67 us (11%)
    all_gather x2, blocking collectives, combined_all(): everything = jax.tree.map(lambda part: lax.all_gather(part, axis), array)  10.4 us
    all_gather x1, waiting for transfers between devices, combined_all(): everything = jax.tree.map(lambda part: lax.all_gather(part, axis), array)  9.09 us
    dot_general x8, matrix products, shards(): jnp.dot(weights.astype(jnp.bfloat16), root_values[:, cols], preferred_ele...  7.64 us
    all_gather x1, blocking collectives, shards(): every_query = lax.all_gather(queries, 'seq', axis=0, tiled=True)  7.43 us
    dot_general x8, matrix products, shards(): lax.dot_general(query, branch_keys[:, cols], dims, preferred_element_type...  5.6 us
    mul x8, other arithmetic, shards(): slopes[head] * branch_pos[None, :]  4.99 us
    dot_general x8, matrix products, shards(): jnp.dot(bweights.astype(jnp.bfloat16), branch_values[:, cols], preferred_...  2.79 us
    dot_general x8, matrix products, shards(): lax.dot_general(query, root_keys[:, cols], dims, preferred_element_type=j...  2.69 us
  transfers between devices with their start and end apart: 1, of which 1 were waited for; matrix products, arithmetic and copies ran while one was open for 5% of the time, Pallas kernels for 0%

commit v1 on v0

v1 whole, which is shorter than its diff:
```python
import functools
import math

import jax
import jax.numpy as jnp
from jax import lax
from jax.experimental import pallas as pl
from jax.experimental.pallas import tpu as pltpu
from jax.sharding import PartitionSpec as P

LOG2E = math.log2(math.e)
DEAD = -1e30
LANES = 128
HBM = pl.BlockSpec(memory_space=pltpu.HBM)
SMEM = pl.BlockSpec(memory_space=pltpu.SMEM)
VMEM = pl.BlockSpec(memory_space=pltpu.VMEM)


def load_kernel(chunks, root_k, root_v, branch_k, branch_v, root_kt, root_vv, branch_kt, branch_vv, held, sems):
    rows = root_k.shape[0] // chunks
    copies = []
    for i, (src, slot) in enumerate(((root_k, 0), (branch_k, 1))):
        for j in range(chunks):
            part = pl.ds(j * rows, rows)
            copies.append(pltpu.make_async_copy(src.at[part], held.at[slot, part], sems.at[i * chunks + j]))
    values = [
        pltpu.make_async_copy(root_v, root_vv, sems.at[2 * chunks]),
        pltpu.make_async_copy(branch_v, branch_vv, sems.at[2 * chunks + 1]),
    ]
    for copy in copies + values:
        copy.start()
    for slot, out in ((0, root_kt), (1, branch_kt)):
        for j in range(chunks):
            copies[slot * chunks + j].wait()
            part = slice(j * rows, (j + 1) * rows)
            for col in range(0, root_k.shape[1], LANES):
                out[col : col + LANES, part] = held[slot, part, col : col + LANES].T
    for copy in values:
        copy.wait()


def load(root_k, root_v, branch_k, branch_v):
    chunks = 4
    keys, width = root_k.shape
    return pl.pallas_call(
        functools.partial(load_kernel, chunks),
        out_shape=(
            jax.ShapeDtypeStruct((width, keys), root_k.dtype),
            jax.ShapeDtypeStruct((keys, width), root_k.dtype),
            jax.ShapeDtypeStruct((width, keys), root_k.dtype),
            jax.ShapeDtypeStruct((keys, width), root_k.dtype),
        ),
        in_specs=[HBM] * 4,
        out_specs=[VMEM] * 4,
        scratch_shapes=[
            pltpu.VMEM((2, keys, width), root_k.dtype),
            pltpu.SemaphoreType.DMA((2 * chunks + 2,)),
        ],
        compiler_params=pltpu.CompilerParams(vmem_limit_bytes=44 << 20),
        cost_estimate=pl.CostEstimate(flops=0, bytes_accessed=8 * keys * width, transcendentals=0),
        name="load",
    )(root_k, root_v, branch_k, branch_v)


def attend_kernel(shifts, wide, slopes, lengths, ids, *refs):
    blocks, (root_kt, root_v, branch_kt, branch_v) = refs[: len(shifts)], refs[len(shifts) : len(shifts) + 4]
    outs = refs[len(shifts) + 4 + wide :]
    me = lax.axis_index("seq")
    count = lax.axis_size("seq")
    heads = slopes.shape[0]
    rows = blocks[0].shape[0]
    width = blocks[0].shape[1]
    size = width // heads
    keys = root_kt.shape[1]
    every = rows * len(shifts)
    factor = LOG2E / math.sqrt(size)
    spot = lax.broadcasted_iota(jnp.int32, (1, keys), 1)
    place = spot.astype(jnp.float32)
    root_pos = (place + (me * keys).astype(jnp.float32)) - float(keys * count + branch_v.shape[0])
    branch_pos = place - float(branch_v.shape[0])
    dead = jnp.where(spot < lengths[0], 0.0, DEAD)
    all_ids = jnp.broadcast_to(ids[...].reshape(1, -1), (rows, ids.shape[0]))
    lane = lax.broadcasted_iota(jnp.int32, all_ids.shape, 1)
    sub = lax.broadcasted_iota(jnp.int32, all_ids.shape, 0)
    own = []
    for shift in shifts:
        at = lane == sub + jnp.bitwise_xor(me, shift) * rows
        own.append(jnp.sum(jnp.where(at & (all_ids == me), 1.0, 0.0), axis=1, keepdims=True))
    own = jnp.concatenate(own, axis=0) > 0.5
    own = jnp.concatenate([own, own], axis=0)
    zero = jnp.zeros((every, size), blocks[0].dtype)
    units = [(head, part) for head in range(0, heads, 2) for part in (0, 1)]

    def scores(unit):
        head, part = unit
        first = jnp.concatenate([b[:, head * size : (head + 1) * size] for b in blocks], axis=0)
        second = jnp.concatenate([b[:, (head + 1) * size : (head + 2) * size] for b in blocks], axis=0)
        left = jnp.concatenate(
            [jnp.concatenate([first, zero], axis=1), jnp.concatenate([zero, second], axis=1)], axis=0
        )
        key = (root_kt, branch_kt)[part][head * size : (head + 2) * size, :]
        return jnp.dot(left, key, preferred_element_type=jnp.float32)

    ahead = scores(units[0])
    column = lax.broadcasted_iota(jnp.int32, (every, LANES), 1)
    level = jnp.zeros((every, LANES), jnp.float32)
    seen = []
    for i, (head, part) in enumerate(units):
        raw = ahead
        if i + 1 < len(units):
            ahead = scores(units[i + 1])
        shaped = []
        for k in range(2):
            slope = slopes[head + k] * LOG2E
            bias = slope * root_pos if part == 0 else slope * branch_pos + dead
            shaped.append(raw[k * every : (k + 1) * every] * factor + bias)
        shaped = jnp.concatenate(shaped, axis=0)
        top = jnp.max(shaped, axis=1, keepdims=True)
        weight = jnp.exp2(shaped - top)
        total = jnp.sum(weight, axis=1, keepdims=True)
        value = (root_v, branch_v)[part][:, head * size : (head + 2) * size]
        mixed = jnp.dot(weight.astype(value.dtype), value, preferred_element_type=jnp.float32)
        mixed = jnp.concatenate([mixed[:every, :size], mixed[every:, size:]], axis=0)
        seen.append((top, total, mixed))
        if part == 1:
            (top_r, total_r, mixed_r), (top_b, total_b, mixed_b) = seen
            seen = []
            top = jnp.maximum(top_r, jnp.where(own, top_b, DEAD))
            scale_r = jnp.exp2(top_r - top)
            scale_b = jnp.where(own, jnp.exp2(top_b - top), 0.0)
            total = scale_r * total_r + scale_b * total_b
            mixed = (scale_r * mixed_r + scale_b * mixed_b) / total
            log = top + jnp.log2(total)
            for k in range(2):
                cols = slice((head + k) * size, (head + k + 1) * size)
                half = log[k * every : (k + 1) * every]
                level = jnp.where(lax.rem(column, heads) == head + k, half, level)
                for j, out in enumerate(outs):
                    at = slice(k * every + j * rows, k * every + (j + 1) * rows)
                    out[:, cols] = mixed[at].astype(out.dtype)
    if True:
        high = level.astype(jnp.bfloat16).astype(jnp.float32)
        middle = (level - high).astype(jnp.bfloat16).astype(jnp.float32)
        low = level - high - middle
        coded = jnp.where(column < heads, high, jnp.where(column < 2 * heads, middle, low))
    else:
        coded = level
    coded = jnp.where(column < 3 * heads, coded, 0.0)
    for j, out in enumerate(outs):
        out[:, width:] = coded[j * rows : (j + 1) * rows].astype(out.dtype)


def attend(shifts, blocks, slopes, lengths, ids, caches, after):
    rows, width = blocks[0].shape
    keys = caches[0].shape[1]
    return pl.pallas_call(
        functools.partial(attend_kernel, tuple(shifts), len(after)),
        out_shape=tuple(jax.ShapeDtypeStruct((rows, width + LANES), jnp.bfloat16) for _ in shifts),
        in_specs=[SMEM, SMEM, VMEM] + [VMEM] * len(blocks) + [VMEM] * 4 + [pl.BlockSpec(memory_space=pl.ANY)] * len(after),
        out_specs=[VMEM] * len(shifts),
        compiler_params=pltpu.CompilerParams(vmem_limit_bytes=24 << 20),
        cost_estimate=pl.CostEstimate(
            flops=8 * rows * len(shifts) * width * keys,
            bytes_accessed=8 * keys * width,
            transcendentals=2 * rows * len(shifts) * keys * slopes.shape[0],
        ),
        name="attend",
    )(slopes, lengths, ids, *blocks, *caches, *after)


def spread_logs(heads, size, coded):
    row = lax.broadcasted_iota(jnp.int32, (LANES, heads * size), 0)
    col = lax.broadcasted_iota(jnp.int32, (LANES, heads * size), 1)
    spread = jnp.where((lax.rem(row, heads) == col // size) & (row < 3 * heads), 1.0, 0.0).astype(coded.dtype)
    return jnp.dot(coded, spread, preferred_element_type=jnp.float32)


def merge_kernel(heads, last, *refs):
    parts, outs = (refs[:-1], refs[-1:]) if last else (refs[:-2], refs[-2:])
    width = outs[0].shape[1]
    logs, values = [], []
    for i, ref in enumerate(parts):
        if last and i == 0:
            continue
        if last and i == 1:
            logs.append(ref[...])
            values.append(parts[0][...])
        else:
            logs.append(spread_logs(heads, width // heads, ref[:, width:]))
            values.append(ref[:, :width].astype(jnp.float32))
    top = functools.reduce(jnp.maximum, logs)
    scales = [jnp.exp2(log - top) for log in logs]
    total = functools.reduce(jnp.add, scales)
    mixed = functools.reduce(jnp.add, [scale * value for scale, value in zip(scales, values)]) / total
    if last:
        outs[0][...] = mixed.astype(outs[0].dtype)
    else:
        outs[0][...] = mixed
        outs[1][...] = top + jnp.log2(total)


def merge(heads, parts, rows, width, last):
    whole = jax.ShapeDtypeStruct((rows, width), jnp.float32)
    return pl.pallas_call(
        functools.partial(merge_kernel, heads, last),
        out_shape=jax.ShapeDtypeStruct((rows, width), jnp.bfloat16) if last else (whole, whole),
        in_specs=[VMEM] * len(parts),
        out_specs=VMEM if last else (VMEM, VMEM),
        compiler_params=pltpu.CompilerParams(vmem_limit_bytes=8 << 20),
        cost_estimate=pl.CostEstimate(flops=0, bytes_accessed=4 << 20, transcendentals=0),
        name="merge",
    )(*parts)


def shards(queries, root_keys, root_values, branch_keys, branch_values, branch_lengths, branch_ids, slopes):
    count = lax.axis_size("seq")
    rows, width = queries.shape

    def swap(array, shift):
        return lax.ppermute(array, "seq", [(i, i ^ shift) for i in range(count)])

    near, far = (0, 1), tuple(range(2, count))
    blocks = {0: queries}
    for shift in range(2, count, 2):
        blocks[shift] = swap(queries, shift)
    blocks[1] = swap(queries, 1)
    for shift in range(2, count, 2):
        blocks[shift + 1] = swap(blocks[shift], 1)
    caches = load(root_keys, root_values, branch_keys, branch_values)
    sent = attend(far, [blocks[s] for s in far], slopes, branch_lengths, branch_ids, caches, ())
    got = [swap(array, shift) for array, shift in zip(sent, far)]
    kept, passed = attend(near, [blocks[s] for s in near], slopes, branch_lengths, branch_ids, caches, sent[:1])
    mixed, logs = merge(slopes.shape[0], got, rows, width, False)
    return merge(slopes.shape[0], [mixed, logs, kept, swap(passed, 1)], rows, width, True)


def solution(mesh):
    in_specs = (
        P(("grp", "seq"), "head"),
        P(("grp", "seq"), "head"),
        P(("grp", "seq"), "head"),
        P(("grp", "seq"), "head"),
        P(("grp", "seq"), "head"),
        P(("grp", "seq")),
        P("grp"),
        P("head"),
    )
    out_specs = P(("grp", "seq"), "head")
    return jax.shard_map(shards, mesh=mesh, in_specs=in_specs, out_specs=out_specs, check_vma=False)
```

time: 82 us -> 20.7 us (0.25)
  matrix products: 18.7 us -> 0 us
  blocking collectives: 17.8 us -> 0 us
  between operations: 14.8 us -> 0.74 us
  other arithmetic: 12.2 us -> 0 us
  Pallas kernels: 0 us -> 10.4 us
  local copies, waits for them, and re-layouts: 8.67 us -> 0.01 us
  starting transfers between devices: 0.01 us -> 5.75 us
  waiting for transfers between devices: 9.11 us -> 3.69 us
    dot_general x32 -> x0, matrix products: 18.7 us -> none  [the longest x8 7.64 us: shards(): jnp.dot(weights.astype(jnp.bfloat16), root_values[:, cols], preferred_ele...]
    all_gather x3 -> x0, blocking collectives: 17.8 us -> none  [the longest x2 10.4 us: combined_all(): everything = jax.tree.map(lambda part: lax.all_gather(part, axis), array)]
    pallas_call x0 -> x5, Pallas kernels: none -> 10.4 us  [the longest x2 5.69 us: attend(): pl.pallas_call(functools.partial(attend_kernel, tuple(shifts), len(after)...]
    all_gather x1 -> x0, waiting for transfers between devices: 9.09 us -> none  [combined_all(): everything = jax.tree.map(lambda part: lax.all_gather(part, axis), array)]
    ppermute x0 -> x6, starting transfers between devices: none -> 5.75 us  [swap(): return lax.ppermute(array, 'seq', [(i, i ^ shift) for i in range(count)])]
    mul x8 -> x0, other arithmetic: 4.99 us -> none  [shards(): slopes[head] * branch_pos[None, :]]
    reduce_sum x9 -> x0, other arithmetic: 4.27 us -> none  [the longest x1 2.44 us: shards(): total_branch = jnp.sum(bweights, axis=1)]
    ppermute x0 -> x6, waiting for transfers between devices: none -> 3.69 us  [swap(): return lax.ppermute(array, 'seq', [(i, i ^ shift) for i in range(count)])]
  transfers between devices with their start and end apart: 1 -> 6, of which waited for: 1 -> 2; matrix products, arithmetic and copies ran while one was open for 5% -> 0% of each run, Pallas kernels for 0% -> 46%
where the time goes in v1:
time: 20.7 us; the launch traced here: 20.6 us
  Pallas kernels  10.4 us (50%)
  starting transfers between devices  5.75 us (28%)
  waiting for transfers between devices  3.69 us (18%)
  between operations  0.74 us (4%)
    ppermute x6, starting transfers between devices, swap(): return lax.ppermute(array, 'seq', [(i, i ^ shift) for i in range(count)])  5.75 us
    pallas_call x2, Pallas kernels, attend(): pl.pallas_call(functools.partial(attend_kernel, tuple(shifts), len(after)...  5.69 us
    ppermute x6, waiting for transfers between devices, swap(): return lax.ppermute(array, 'seq', [(i, i ^ shift) for i in range(count)])  3.69 us
    pallas_call x1, Pallas kernels, load(): pl.pallas_call(functools.partial(load_kernel, chunks), out_shape=(jax.Sha...  3.58 us
    pallas_call x2, Pallas kernels, merge(): pl.pallas_call(functools.partial(merge_kernel, heads, last), out_shape=ja...  1.11 us
  transfers between devices with their start and end apart: 6, of which 2 were waited for; matrix products, arithmetic and copies ran while one was open for 0% of the time, Pallas kernels for 46%

profile of v1, /device:TPU:0, one launch (start us, length us, event | category | flops | bytes accessed | tf_op | source)
XLA Modules:
  0.0 20.6 jit_solution(13124257841550755982)
XLA Ops:
  0.0 3.0 %collective-permute-start = (bf16[32,1024]{1,0:T(8,128)(2,1)}, bf16[32,1024]{1,0:T(8,128)(2,1)S(1)}, u32[]{:S(2)}, u32[]{:S(2)}) collective-permute-start(bf16[32,1024]{1,0:T(8,128)(2,1)} %refs_0_.1), channel_id=1, source_target_pairs={{0,8},{4,12},{8,0},{12,4},{1,9},{5,13},{9,1},{13,5},{2,10},{6,14},... | collective-permute-start | bytes 196616 | tf_op jit(solution)/shard_map/ppermute | solution.py:220
  3.0 2.5 %collective-permute-done.refs_0_ = bf16[32,1024]{1,0:T(8,128)(2,1)S(1)} collective-permute-done((bf16[32,1024]{1,0:T(8,128)(2,1)}, bf16[32,1024]{1,0:T(8,128)(2,1)S(1)}, u32[]{:S(2)}, u32[]{:S(2)}) %collective-permute-start) | collective-permute-done | bytes 65568 | tf_op jit(solution)/shard_map/ppermute | solution.py:220
  5.4 0.0 collective-permute-start.1
  5.4 0.5 %collective-permute-start.4 = (bf16[32,1024]{1,0:T(8,128)(2,1)}, bf16[32,1024]{1,0:T(8,128)(2,1)S(1)}, u32[]{:S(2)}, u32[]{:S(2)}) collective-permute-start(bf16[32,1024]{1,0:T(8,128)(2,1)} %refs_0_.1), channel_id=1, source_target_pairs={{0,4},{4,0},{8,12},{12,8},{1,5},{5,1},{9,13},{13,9},{2,6},{6,2},{1... | collective-permute-start | bytes 196616 | tf_op jit(solution)/shard_map/ppermute | solution.py:220
  6.6 0.0 copy-start.1
  6.6 0.0 copy-start.2
  6.6 3.6 %load.1 = (bf16[1024,1024]{1,0:T(8,128)(2,1)S(1)}, bf16[1024,1024]{1,0:T(8,128)(2,1)S(1)}, bf16[1024,1024]{1,0:T(8,128)(2,1)S(1)}, bf16[1024,1024]{1,0:T(8,128)(2,1)S(1)}) custom-call(bf16[1024,1024]{1,0:T(8,128)(2,1)} %root_k.1, bf16[1024,1024]{1,0:T(8,128)(2,1)} %root_v.1, bf16[1024,1024]{1,0:T(8,128)(2,1)} %branch_k.1, bf16[1024,1024]{1,0:T(8,128)(2,1)} %branch_v.1), custom_call_target="tpu_custom_call" | custom-call | bytes 8388608 | tf_op jit(solution)/shard_map/load/pallas_call | solution.py:45
  10.2 0.0 collective-permute-done.1.refs_1_
  10.2 0.0 copy-done.1
  10.2 0.0 copy-done.2
  10.2 0.0 copy-start
  10.2 2.8 %attend.2 = (bf16[32,1152]{1,0:T(8,128)(2,1)S(1)}, bf16[32,1152]{1,0:T(8,128)(2,1)S(1)}) custom-call(f32[8]{0:T(128)S(1)} %copy-done.1, s32[1]{0:T(128)S(6)} %copy.9.lengths, s32[128]{0:T(128)S(1)} %copy-done.2, bf16[32,1024]{1,0:T(8,128)(2,1)S(1)} %collective-permute-done.refs_0_, bf16[32,1024]{1,0:T(8,128)(2,1)S(1)} %collective-permute-done.1.refs_1_, ...), custom_call_target="tpu_custom_call" | custom-call | flops 536870912 | bytes 8388608 | tf_op jit(solution)/shard_map/attend/pallas_call | solution.py:156
  13.1 1.7 %collective-permute-start.3 = (bf16[32,1152]{1,0:T(8,128)(2,1)S(1)}, bf16[32,1152]{1,0:T(8,128)(2,1)S(1)}, u32[]{:S(2)}, u32[]{:S(2)}) collective-permute-start(bf16[32,1152]{1,0:T(8,128)(2,1)S(1)} %get-tuple-element.20), channel_id=1, source_target_pairs={{0,12},{4,8},{8,4},{12,0},{1,13},{5,9},{9,5},{13,1},{2,14},{6,10},... | collective-permute-start | bytes 221192 | tf_op jit(solution)/shard_map/ppermute | solution.py:220
  14.8 0.5 %collective-permute-start.2 = (bf16[32,1152]{1,0:T(8,128)(2,1)S(1)}, bf16[32,1152]{1,0:T(8,128)(2,1)S(1)}, u32[]{:S(2)}, u32[]{:S(2)}) collective-permute-start(bf16[32,1152]{1,0:T(8,128)(2,1)S(1)} %get-tuple-element.19.refs_6_), channel_id=1, source_target_pairs={{0,8},{4,12},{8,0},{12,4},{1,9},{5,13},{9,1},{13,5},{2,10},{6,14},... | collective-permute-start | bytes 221192 | tf_op jit(solution)/shard_map/ppermute | solution.py:220
  15.3 0.0 collective-permute-done.4.refs_1_
  15.3 0.0 copy-done
  15.3 2.9 %attend.3 = (bf16[32,1152]{1,0:T(8,128)(2,1)S(1)}, bf16[32,1152]{1,0:T(8,128)(2,1)S(1)}) custom-call(f32[8]{0:T(128)S(1)} %copy-done.1, s32[1]{0:T(128)S(6)} %copy.9.lengths, s32[128]{0:T(128)S(1)} %copy-done.2, bf16[32,1024]{1,0:T(8,128)(2,1)S(1)} %copy-done, bf16[32,1024]{1,0:T(8,128)(2,1)S(1)} %collective-permute-done.4.refs_1_, ...), custom_call_target="tpu_custom_call" | custom-call | flops 536870912 | bytes 8388608 | tf_op jit(solution)/shard_map/attend/pallas_call | solution.py:156
  18.1 0.1 collective-permute-start.5
  18.2 0.0 collective-permute-done.3.refs_1_
  18.2 1.2 %collective-permute-done.2.refs_0_ = bf16[32,1152]{1,0:T(8,128)(2,1)S(1)} collective-permute-done((bf16[32,1152]{1,0:T(8,128)(2,1)S(1)}, bf16[32,1152]{1,0:T(8,128)(2,1)S(1)}, u32[]{:S(2)}, u32[]{:S(2)}) %collective-permute-start.2) | collective-permute-done | bytes 73760 | tf_op jit(solution)/shard_map/ppermute | solution.py:220
  19.5 0.2 %merge.2 = (f32[32,1024]{1,0:T(8,128)S(1)}, f32[32,1024]{1,0:T(8,128)S(1)}) custom-call(bf16[32,1152]{1,0:T(8,128)(2,1)S(1)} %collective-permute-done.2.refs_0_, bf16[32,1152]{1,0:T(8,128)(2,1)S(1)} %collective-permute-done.3.refs_1_), custom_call_target="tpu_custom_call" | custom-call | bytes 4194304 | tf_op jit(solution)/shard_map/merge/pallas_call | solution.py:204
  19.7 0.0 collective-permute-done.5.refs_3_
  19.7 0.9 %merge.3 = bf16[32,1024]{1,0:T(8,128)(2,1)} custom-call(f32[32,1024]{1,0:T(8,128)S(1)} %get-tuple-element.21.refs_0_, f32[32,1024]{1,0:T(8,128)S(1)} %get-tuple-element.22.refs_1_, bf16[32,1152]{1,0:T(8,128)(2,1)S(1)} %get-tuple-element.23.refs_2_, bf16[32,1152]{1,0:T(8,128)(2,1)S(1)} %collective-permute-done.5.refs_3_), custom_call_target="tpu_custom_call" | custom-call | bytes 4194304 | tf_op jit(solution)/shard_map/merge/pallas_call | solution.py:204
Async XLA Ops:
  0.0 5.4 %collective-permute-start = (bf16[32,1024]{1,0:T(8,128)(2,1)}, bf16[32,1024]{1,0:T(8,128)(2,1)S(1)}, u32[]{:S(2)}, u32[]{:S(2)}) collective-permute-start(bf16[32,1024]{1,0:T(8,128)(2,1)} %refs_0_.1), channel_id=1, source_target_pairs={{0,8},{4,12},{8,0},{12,4},{1,9},{5,13},{9,1},{13,5},{2,10},{6,14},... | collective-permute-start | bytes 196616 | tf_op jit(solution)/shard_map/ppermute | solution.py:220
  5.4 4.8 %collective-permute-start.1 = (bf16[32,1024]{1,0:T(8,128)(2,1)S(1)}, bf16[32,1024]{1,0:T(8,128)(2,1)S(1)}, u32[]{:S(2)}, u32[]{:S(2)}) collective-permute-start(bf16[32,1024]{1,0:T(8,128)(2,1)S(1)} %collective-permute-done.refs_0_), channel_id=1, source_target_pairs={{0,4},{4,0},{8,12},{12,8},{1,5},{5,1},{9,13},{13,9},{2,6},{6,2},{1... | collective-permute-start | bytes 196616 | tf_op jit(solution)/shard_map/ppermute | solution.py:220
  5.4 9.8 %collective-permute-start.4 = (bf16[32,1024]{1,0:T(8,128)(2,1)}, bf16[32,1024]{1,0:T(8,128)(2,1)S(1)}, u32[]{:S(2)}, u32[]{:S(2)}) collective-permute-start(bf16[32,1024]{1,0:T(8,128)(2,1)} %refs_0_.1), channel_id=1, source_target_pairs={{0,4},{4,0},{8,12},{12,8},{1,5},{5,1},{9,13},{13,9},{2,6},{6,2},{1... | collective-permute-start | bytes 196616 | tf_op jit(solution)/shard_map/ppermute | solution.py:220
  6.6 3.6 %copy-start.1 = (f32[8]{0:T(128)S(1)}, f32[8]{0:T(128)}, u32[]{:S(2)}) copy-start(f32[8]{0:T(128)} %slopes.3) | copy-start | bytes 100
  6.6 3.6 %copy-start.2 = (s32[128]{0:T(128)S(1)}, s32[128]{0:T(128)}, u32[]{:S(2)}) copy-start(s32[128]{0:T(128)} %ids.3) | copy-start | bytes 1540
  10.2 5.0 %copy-start = (bf16[32,1024]{1,0:T(8,128)(2,1)S(1)}, bf16[32,1024]{1,0:T(8,128)(2,1)}, u32[]{:S(2)}) copy-start(bf16[32,1024]{1,0:T(8,128)(2,1)} %refs_0_.1) | copy-start | bytes 196612
  13.1 5.1 %collective-permute-start.3 = (bf16[32,1152]{1,0:T(8,128)(2,1)S(1)}, bf16[32,1152]{1,0:T(8,128)(2,1)S(1)}, u32[]{:S(2)}, u32[]{:S(2)}) collective-permute-start(bf16[32,1152]{1,0:T(8,128)(2,1)S(1)} %get-tuple-element.20), channel_id=1, source_target_pairs={{0,12},{4,8},{8,4},{12,0},{1,13},{5,9},{9,5},{13,1},{2,14},{6,10},... | collective-permute-start | bytes 221192 | tf_op jit(solution)/shard_map/ppermute | solution.py:220
  14.8 4.7 %collective-permute-start.2 = (bf16[32,1152]{1,0:T(8,128)(2,1)S(1)}, bf16[32,1152]{1,0:T(8,128)(2,1)S(1)}, u32[]{:S(2)}, u32[]{:S(2)}) collective-permute-start(bf16[32,1152]{1,0:T(8,128)(2,1)S(1)} %get-tuple-element.19.refs_6_), channel_id=1, source_target_pairs={{0,8},{4,12},{8,0},{12,4},{1,9},{5,13},{9,1},{13,5},{2,10},{6,14},... | collective-permute-start | bytes 221192 | tf_op jit(solution)/shard_map/ppermute | solution.py:220
  18.1 1.6 %collective-permute-start.5 = (bf16[32,1152]{1,0:T(8,128)(2,1)S(1)}, bf16[32,1152]{1,0:T(8,128)(2,1)S(1)}, u32[]{:S(2)}, u32[]{:S(2)}) collective-permute-start(bf16[32,1152]{1,0:T(8,128)(2,1)S(1)} %get-tuple-element.24), channel_id=1, source_target_pairs={{0,4},{4,0},{8,12},{12,8},{1,5},{5,1},{9,13},{13,9},{2,6},{6,2},{1... | collective-permute-start | bytes 221192 | tf_op jit(solution)/shard_map/ppermute | solution.py:220

commit v2 on v1

--- a/solution.py
+++ b/solution.py
@@ -62,32 +62,53 @@
     )(root_k, root_v, branch_k, branch_v)
 
 
-def attend_kernel(shifts, wide, slopes, lengths, ids, *refs):
-    blocks, (root_kt, root_v, branch_kt, branch_v) = refs[: len(shifts)], refs[len(shifts) : len(shifts) + 4]
-    outs = refs[len(shifts) + 4 + wide :]
+def column(vector, rows, start):
+    wide = jnp.broadcast_to(vector.reshape(1, -1), (rows, vector.shape[0]))
+    lane = lax.broadcasted_iota(jnp.int32, wide.shape, 1)
+    sub = lax.broadcasted_iota(jnp.int32, wide.shape, 0)
+    return jnp.sum(jnp.where(lane == sub + start, wide, jnp.zeros_like(wide)), axis=1, keepdims=True)
+
+
+def tables_kernel(rows, slopes, lengths, ids, after, bias, mine):
     me = lax.axis_index("seq")
     count = lax.axis_size("seq")
     heads = slopes.shape[0]
-    rows = blocks[0].shape[0]
-    width = blocks[0].shape[1]
+    keys = bias.shape[1]
+    slope = column(slopes[...], heads, 0) * LOG2E
+    spot = lax.broadcasted_iota(jnp.int32, (1, keys), 1)
+    place = spot.astype(jnp.float32)
+    bias[:heads] = slope * (place + (me * keys - keys * (count + 1)).astype(jnp.float32))
+    dead = jnp.where(spot < lengths[...].reshape(1, 1), 0.0, DEAD)
+    bias[heads:] = slope * (place - float(keys)) + dead
+    mark = jnp.where(ids[...] == me, 1.0, 0.0)
+    for shift in range(count):
+        at = column(mark, rows, jnp.bitwise_xor(me, shift) * rows)
+        mine[shift * rows : (shift + 1) * rows, :] = jnp.broadcast_to(at, (rows, LANES))
+
+
+def tables(slopes, lengths, ids, rows, keys, after):
+    return pl.pallas_call(
+        functools.partial(tables_kernel, rows),
+        out_shape=(
+            jax.ShapeDtypeStruct((2 * slopes.shape[0], keys), jnp.float32),
+            jax.ShapeDtypeStruct((ids.shape[0], LANES), jnp.float32),
+        ),
+        in_specs=[VMEM] * 3 + [pl.BlockSpec(memory_space=pl.ANY)],
+        out_specs=[VMEM] * 2,
+        compiler_params=pltpu.CompilerParams(vmem_limit_bytes=8 << 20),
+        name="tables",
+    )(slopes, lengths, ids, after)
+
+
+def attend_kernel(shifts, heads, skipped, *refs):
+    blocks, caches = refs[: len(shifts)], refs[len(shifts) : len(shifts) + 6]
+    root_kt, root_v, branch_kt, branch_v, bias, mine = caches
+    outs = refs[len(shifts) + 6 + skipped :]
+    rows, width = blocks[0].shape
     size = width // heads
-    keys = root_kt.shape[1]
     every = rows * len(shifts)
     factor = LOG2E / math.sqrt(size)
-    spot = lax.broadcasted_iota(jnp.int32, (1, keys), 1)
-    place = spot.astype(jnp.float32)
-    root_pos = (place + (me * keys).astype(jnp.float32)) - float(keys * count + branch_v.shape[0])
-    branch_pos = place - float(branch_v.shape[0])
-    dead = jnp.where(spot < lengths[0], 0.0, DEAD)
-    all_ids = jnp.broadcast_to(ids[...].reshape(1, -1), (rows, ids.shape[0]))
-    lane = lax.broadcasted_iota(jnp.int32, all_ids.shape, 1)
-    sub = lax.broadcasted_iota(jnp.int32, all_ids.shape, 0)
-    own = []
-    for shift in shifts:
-        at = lane == sub + jnp.bitwise_xor(me, shift) * rows
-        own.append(jnp.sum(jnp.where(at & (all_ids == me), 1.0, 0.0), axis=1, keepdims=True))
-    own = jnp.concatenate(own, axis=0) > 0.5
-    own = jnp.concatenate([own, own], axis=0)
+    own = jnp.concatenate([mine[shift * rows : (shift + 1) * rows, :1] for shift in shifts] * 2, axis=0) > 0.5
     zero = jnp.zeros((every, size), blocks[0].dtype)
     units = [(head, part) for head in range(0, heads, 2) for part in (0, 1)]
 
@@ -102,7 +123,7 @@
         return jnp.dot(left, key, preferred_element_type=jnp.float32)
 
     ahead = scores(units[0])
-    column = lax.broadcasted_iota(jnp.int32, (every, LANES), 1)
+    lane = lax.broadcasted_iota(jnp.int32, (every, LANES), 1)
     level = jnp.zeros((every, LANES), jnp.float32)
     seen = []
     for i, (head, part) in enumerate(units):
@@ -111,9 +132,8 @@
             ahead = scores(units[i + 1])
         shaped = []
         for k in range(2):
-            slope = slopes[head + k] * LOG2E
-            bias = slope * root_pos if part == 0 else slope * branch_pos + dead
-            shaped.append(raw[k * every : (k + 1) * every] * factor + bias)
+            row = part * heads + head + k
+            shaped.append(raw[k * every : (k + 1) * every] * factor + bias[row : row + 1, :])
         shaped = jnp.concatenate(shaped, axis=0)
         top = jnp.max(shaped, axis=1, keepdims=True)
         weight = jnp.exp2(shaped - top)
@@ -129,43 +149,41 @@
             scale_r = jnp.exp2(top_r - top)
             scale_b = jnp.where(own, jnp.exp2(top_b - top), 0.0)
             total = scale_r * total_r + scale_b * total_b
-            mixed = (scale_r * mixed_r + scale_b * mixed_b) / total
+            inverse = 1.0 / total
+            mixed = (scale_r * inverse) * mixed_r + (scale_b * inverse) * mixed_b
             log = top + jnp.log2(total)
             for k in range(2):
                 cols = slice((head + k) * size, (head + k + 1) * size)
                 half = log[k * every : (k + 1) * every]
-                level = jnp.where(lax.rem(column, heads) == head + k, half, level)
+                level = jnp.where(lax.rem(lane, heads) == head + k, half, level)
                 for j, out in enumerate(outs):
                     at = slice(k * every + j * rows, k * every + (j + 1) * rows)
                     out[:, cols] = mixed[at].astype(out.dtype)
-    if True:
-        high = level.astype(jnp.bfloat16).astype(jnp.float32)
-        middle = (level - high).astype(jnp.bfloat16).astype(jnp.float32)
-        low = level - high - middle
-        coded = jnp.where(column < heads, high, jnp.where(column < 2 * heads, middle, low))
-    else:
-        coded = level
-    coded = jnp.where(column < 3 * heads, coded, 0.0)
+    high = level.astype(jnp.bfloat16).astype(jnp.float32)
+    middle = (level - high).astype(jnp.bfloat16).astype(jnp.float32)
+    low = level - high - middle
+    coded = jnp.where(lane < heads, high, jnp.where(lane < 2 * heads, middle, low))
+    coded = jnp.where(lane < 3 * heads, coded, 0.0)
     for j, out in enumerate(outs):
         out[:, width:] = coded[j * rows : (j + 1) * rows].astype(out.dtype)
 
 
-def attend(shifts, blocks, slopes, lengths, ids, caches, after):
+def attend(shifts, blocks, heads, caches, after):
     rows, width = blocks[0].shape
     keys = caches[0].shape[1]
     return pl.pallas_call(
-        functools.partial(attend_kernel, tuple(shifts), len(after)),
+        functools.partial(attend_kernel, tuple(shifts), heads, len(after)),
         out_shape=tuple(jax.ShapeDtypeStruct((rows, width + LANES), jnp.bfloat16) for _ in shifts),
-        in_specs=[SMEM, SMEM, VMEM] + [VMEM] * len(blocks) + [VMEM] * 4 + [pl.BlockSpec(memory_space=pl.ANY)] * len(after),
+        in_specs=[VMEM] * (len(blocks) + len(caches)) + [pl.BlockSpec(memory_space=pl.ANY)] * len(after),
         out_specs=[VMEM] * len(shifts),
         compiler_params=pltpu.CompilerParams(vmem_limit_bytes=24 << 20),
         cost_estimate=pl.CostEstimate(
             flops=8 * rows * len(shifts) * width * keys,
             bytes_accessed=8 * keys * width,
-            transcendentals=2 * rows * len(shifts) * keys * slopes.shape[0],
+            transcendentals=2 * rows * len(shifts) * keys * heads,
         ),
         name="attend",
-    )(slopes, lengths, ids, *blocks, *caches, *after)
+    )(*blocks, *caches, *after)
 
 
 def spread_logs(heads, size, coded):
@@ -220,18 +238,15 @@
         return lax.ppermute(array, "seq", [(i, i ^ shift) for i in range(count)])
 
     near, far = (0, 1), tuple(range(2, count))
-    blocks = {0: queries}
-    for shift in range(2, count, 2):
-        blocks[shift] = swap(queries, shift)
-    blocks[1] = swap(queries, 1)
-    for shift in range(2, count, 2):
-        blocks[shift + 1] = swap(blocks[shift], 1)
+    blocks = {0: queries} | {shift: swap(queries, shift) for shift in far + near[1:]}
+    heads = slopes.shape[0]
     caches = load(root_keys, root_values, branch_keys, branch_values)
-    sent = attend(far, [blocks[s] for s in far], slopes, branch_lengths, branch_ids, caches, ())
+    caches += tables(slopes, branch_lengths, branch_ids, rows, root_keys.shape[0], caches[0])
+    sent = attend(far, [blocks[s] for s in far], heads, caches, ())
     got = [swap(array, shift) for array, shift in zip(sent, far)]
-    kept, passed = attend(near, [blocks[s] for s in near], slopes, branch_lengths, branch_ids, caches, sent[:1])
-    mixed, logs = merge(slopes.shape[0], got, rows, width, False)
-    return merge(slopes.shape[0], [mixed, logs, kept, swap(passed, 1)], rows, width, True)
+    kept, passed = attend(near, [blocks[s] for s in near], heads, caches, sent[:1])
+    mixed, logs = merge(heads, got, rows, width, False)
+    return merge(heads, [mixed, logs, kept, swap(passed, 1)], rows, width, True)
 
 
 def solution(mesh):

time: 20.7 us -> 17 us (0.82)
  waiting for transfers between devices: 3.69 us -> 1.97 us
  Pallas kernels: 10.4 us -> 8.85 us
  starting transfers between devices: 5.75 us -> 5.28 us
    ppermute x6, waiting for transfers between devices: 3.69 us -> 1.97 us  [swap(): return lax.ppermute(array, 'seq', [(i, i ^ shift) for i in range(count)])]
    pallas_call x2 -> x3, Pallas kernels: 5.69 us -> 4.15 us  [the longest x2 4.04 us: attend(): pl.pallas_call(functools.partial(attend_kernel, tuple(shifts), heads, len...]
    ppermute x6, starting transfers between devices: 5.75 us -> 5.28 us  [swap(): return lax.ppermute(array, 'seq', [(i, i ^ shift) for i in range(count)])]
  transfers between devices with their start and end apart: 6 -> 6, of which waited for: 2 -> 1; matrix products, arithmetic and copies ran while one was open for 0% -> 0% of each run, Pallas kernels for 46% -> 47%
where the time goes in v2:
time: 17 us; the launch traced here: 16.9 us
  Pallas kernels  8.85 us (52%)
  starting transfers between devices  5.28 us (31%)
  waiting for transfers between devices  1.97 us (12%)
  between operations  0.77 us (5%)
    ppermute x6, starting transfers between devices, swap(): return lax.ppermute(array, 'seq', [(i, i ^ shift) for i in range(count)])  5.28 us
    pallas_call x2, Pallas kernels, attend(): pl.pallas_call(functools.partial(attend_kernel, tuple(shifts), heads, len...  4.04 us
    pallas_call x1, Pallas kernels, load(): pl.pallas_call(functools.partial(load_kernel, chunks), out_shape=(jax.Sha...  3.58 us
    ppermute x6, waiting for transfers between devices, swap(): return lax.ppermute(array, 'seq', [(i, i ^ shift) for i in range(count)])  1.97 us
    pallas_call x2, Pallas kernels, merge(): pl.pallas_call(functools.partial(merge_kernel, heads, last), out_shape=ja...  1.11 us
  transfers between devices with their start and end apart: 6, of which 1 were waited for; matrix products, arithmetic and copies ran while one was open for 0% of the time, Pallas kernels for 47%

profile of v2, /device:TPU:0, one launch (start us, length us, event | category | flops | bytes accessed | tf_op | source)
XLA Modules:
  0.0 16.9 jit_solution(1208308483476091285)
XLA Ops:
  0.0 2.4 %collective-permute-start.1 = (bf16[32,1024]{1,0:T(8,128)(2,1)}, bf16[32,1024]{1,0:T(8,128)(2,1)S(1)}, u32[]{:S(2)}, u32[]{:S(2)}) collective-permute-start(bf16[32,1024]{1,0:T(8,128)(2,1)} %refs_0_.1), channel_id=1, source_target_pairs={{0,12},{4,8},{8,4},{12,0},{1,13},{5,9},{9,5},{13,1},{2,14},{6,10},... | collective-permute-start | bytes 196616 | tf_op jit(solution)/shard_map/ppermute | solution.py:238
  2.4 0.6 %collective-permute-start = (bf16[32,1024]{1,0:T(8,128)(2,1)}, bf16[32,1024]{1,0:T(8,128)(2,1)S(1)}, u32[]{:S(2)}, u32[]{:S(2)}) collective-permute-start(bf16[32,1024]{1,0:T(8,128)(2,1)} %refs_0_.1), channel_id=1, source_target_pairs={{0,8},{4,12},{8,0},{12,4},{1,9},{5,13},{9,1},{13,5},{2,10},{6,14},... | collective-permute-start | bytes 196616 | tf_op jit(solution)/shard_map/ppermute | solution.py:238
  3.0 0.1 collective-permute-start.4
  3.7 0.0 copy-start.1
  3.7 0.0 copy-start.2
  3.8 3.6 %load.1 = (bf16[1024,1024]{1,0:T(8,128)(2,1)S(1)}, bf16[1024,1024]{1,0:T(8,128)(2,1)S(1)}, bf16[1024,1024]{1,0:T(8,128)(2,1)S(1)}, bf16[1024,1024]{1,0:T(8,128)(2,1)S(1)}) custom-call(bf16[1024,1024]{1,0:T(8,128)(2,1)} %root_k.1, bf16[1024,1024]{1,0:T(8,128)(2,1)} %root_v.1, bf16[1024,1024]{1,0:T(8,128)(2,1)} %branch_k.1, bf16[1024,1024]{1,0:T(8,128)(2,1)} %branch_v.1), custom_call_target="tpu_custom_call" | custom-call | bytes 8388608 | tf_op jit(solution)/shard_map/load/pallas_call | solution.py:45
  7.3 0.0 copy-done.1
  7.4 0.0 copy-done.2
  7.4 0.1 tables.1
  7.5 0.0 collective-permute-done.1.refs_1_
  7.5 0.0 collective-permute-done.refs_0_
  7.5 0.0 copy-start
  7.5 2.0 %attend.2 = (bf16[32,1152]{1,0:T(8,128)(2,1)S(1)}, bf16[32,1152]{1,0:T(8,128)(2,1)S(1)}) custom-call(bf16[32,1024]{1,0:T(8,128)(2,1)S(1)} %collective-permute-done.refs_0_, bf16[32,1024]{1,0:T(8,128)(2,1)S(1)} %collective-permute-done.1.refs_1_, bf16[1024,1024]{1,0:T(8,128)(2,1)S(1)} %get-tuple-element.17.after.refs_2_, ...), custom_call_target="tpu_custom_call" | custom-call | flops 536870912 | bytes 8388608 | tf_op jit(solution)/shard_map/attend/pallas_call | solution.py:174
  9.5 1.5 %collective-permute-start.3 = (bf16[32,1152]{1,0:T(8,128)(2,1)S(1)}, bf16[32,1152]{1,0:T(8,128)(2,1)S(1)}, u32[]{:S(2)}, u32[]{:S(2)}) collective-permute-start(bf16[32,1152]{1,0:T(8,128)(2,1)S(1)} %get-tuple-element.24), channel_id=1, source_target_pairs={{0,12},{4,8},{8,4},{12,0},{1,13},{5,9},{9,5},{13,1},{2,14},{6,10},... | collective-permute-start | bytes 221192 | tf_op jit(solution)/shard_map/ppermute | solution.py:238
  11.1 0.6 %collective-permute-start.2 = (bf16[32,1152]{1,0:T(8,128)(2,1)S(1)}, bf16[32,1152]{1,0:T(8,128)(2,1)S(1)}, u32[]{:S(2)}, u32[]{:S(2)}) collective-permute-start(bf16[32,1152]{1,0:T(8,128)(2,1)S(1)} %get-tuple-element.23.refs_8_), channel_id=1, source_target_pairs={{0,8},{4,12},{8,0},{12,4},{1,9},{5,13},{9,1},{13,5},{2,10},{6,14},... | collective-permute-start | bytes 221192 | tf_op jit(solution)/shard_map/ppermute | solution.py:238
  11.7 0.0 collective-permute-done.4.refs_1_
  11.7 0.0 copy-done
  11.7 2.0 %attend.3 = (bf16[32,1152]{1,0:T(8,128)(2,1)S(1)}, bf16[32,1152]{1,0:T(8,128)(2,1)S(1)}) custom-call(bf16[32,1024]{1,0:T(8,128)(2,1)S(1)} %copy-done, bf16[32,1024]{1,0:T(8,128)(2,1)S(1)} %collective-permute-done.4.refs_1_, bf16[1024,1024]{1,0:T(8,128)(2,1)S(1)} %get-tuple-element.17.after.refs_2_, bf16[1024,1024]{1,0:T(8,128)(2,1)S(1)} %get-tuple-element.18.refs_3_, ...), custom_call_target="tpu_custom_call" | custom-call | flops 536870912 | bytes 8388608 | tf_op jit(solution)/shard_map/attend/pallas_call | solution.py:174
  13.7 0.1 collective-permute-start.5
  13.8 0.0 collective-permute-done.3.refs_1_
  13.8 2.0 %collective-permute-done.2.refs_0_ = bf16[32,1152]{1,0:T(8,128)(2,1)S(1)} collective-permute-done((bf16[32,1152]{1,0:T(8,128)(2,1)S(1)}, bf16[32,1152]{1,0:T(8,128)(2,1)S(1)}, u32[]{:S(2)}, u32[]{:S(2)}) %collective-permute-start.2) | collective-permute-done | bytes 73760 | tf_op jit(solution)/shard_map/ppermute | solution.py:238
  15.8 0.2 %merge.2 = (f32[32,1024]{1,0:T(8,128)S(1)}, f32[32,1024]{1,0:T(8,128)S(1)}) custom-call(bf16[32,1152]{1,0:T(8,128)(2,1)S(1)} %collective-permute-done.2.refs_0_, bf16[32,1152]{1,0:T(8,128)(2,1)S(1)} %collective-permute-done.3.refs_1_), custom_call_target="tpu_custom_call" | custom-call | bytes 4194304 | tf_op jit(solution)/shard_map/merge/pallas_call | solution.py:222
  16.0 0.0 collective-permute-done.5.refs_3_
  16.0 0.9 %merge.3 = bf16[32,1024]{1,0:T(8,128)(2,1)} custom-call(f32[32,1024]{1,0:T(8,128)S(1)} %get-tuple-element.25.refs_0_, f32[32,1024]{1,0:T(8,128)S(1)} %get-tuple-element.26.refs_1_, bf16[32,1152]{1,0:T(8,128)(2,1)S(1)} %get-tuple-element.27.refs_2_, bf16[32,1152]{1,0:T(8,128)(2,1)S(1)} %collective-permute-done.5.refs_3_), custom_call_target="tpu_custom_call" | custom-call | bytes 4194304 | tf_op jit(solution)/shard_map/merge/pallas_call | solution.py:222
Async XLA Ops:
  0.0 7.5 %collective-permute-start.1 = (bf16[32,1024]{1,0:T(8,128)(2,1)}, bf16[32,1024]{1,0:T(8,128)(2,1)S(1)}, u32[]{:S(2)}, u32[]{:S(2)}) collective-permute-start(bf16[32,1024]{1,0:T(8,128)(2,1)} %refs_0_.1), channel_id=1, source_target_pairs={{0,12},{4,8},{8,4},{12,0},{1,13},{5,9},{9,5},{13,1},{2,14},{6,10},... | collective-permute-start | bytes 196616 | tf_op jit(solution)/shard_map/ppermute | solution.py:238
  2.4 5.1 %collective-permute-start = (bf16[32,1024]{1,0:T(8,128)(2,1)}, bf16[32,1024]{1,0:T(8,128)(2,1)S(1)}, u32[]{:S(2)}, u32[]{:S(2)}) collective-permute-start(bf16[32,1024]{1,0:T(8,128)(2,1)} %refs_0_.1), channel_id=1, source_target_pairs={{0,8},{4,12},{8,0},{12,4},{1,9},{5,13},{9,1},{13,5},{2,10},{6,14},... | collective-permute-start | bytes 196616 | tf_op jit(solution)/shard_map/ppermute | solution.py:238
  3.0 8.7 %collective-permute-start.4 = (bf16[32,1024]{1,0:T(8,128)(2,1)}, bf16[32,1024]{1,0:T(8,128)(2,1)S(1)}, u32[]{:S(2)}, u32[]{:S(2)}) collective-permute-start(bf16[32,1024]{1,0:T(8,128)(2,1)} %refs_0_.1), channel_id=1, source_target_pairs={{0,4},{4,0},{8,12},{12,8},{1,5},{5,1},{9,13},{13,9},{2,6},{6,2},{1... | collective-permute-start | bytes 196616 | tf_op jit(solution)/shard_map/ppermute | solution.py:238
  3.7 3.6 %copy-start.1 = (f32[8]{0:T(128)S(1)}, f32[8]{0:T(128)}, u32[]{:S(2)}) copy-start(f32[8]{0:T(128)} %slopes.1) | copy-start | bytes 100
  3.7 3.6 %copy-start.2 = (s32[128]{0:T(128)S(1)}, s32[128]{0:T(128)}, u32[]{:S(2)}) copy-start(s32[128]{0:T(128)} %ids.1) | copy-start | bytes 1540
  7.5 4.2 %copy-start = (bf16[32,1024]{1,0:T(8,128)(2,1)S(1)}, bf16[32,1024]{1,0:T(8,128)(2,1)}, u32[]{:S(2)}) copy-start(bf16[32,1024]{1,0:T(8,128)(2,1)} %refs_0_.1) | copy-start | bytes 196612
  9.5 4.2 %collective-permute-start.3 = (bf16[32,1152]{1,0:T(8,128)(2,1)S(1)}, bf16[32,1152]{1,0:T(8,128)(2,1)S(1)}, u32[]{:S(2)}, u32[]{:S(2)}) collective-permute-start(bf16[32,1152]{1,0:T(8,128)(2,1)S(1)} %get-tuple-element.24), channel_id=1, source_target_pairs={{0,12},{4,8},{8,4},{12,0},{1,13},{5,9},{9,5},{13,1},{2,14},{6,10},... | collective-permute-start | bytes 221192 | tf_op jit(solution)/shard_map/ppermute | solution.py:238
  11.1 4.7 %collective-permute-start.2 = (bf16[32,1152]{1,0:T(8,128)(2,1)S(1)}, bf16[32,1152]{1,0:T(8,128)(2,1)S(1)}, u32[]{:S(2)}, u32[]{:S(2)}) collective-permute-start(bf16[32,1152]{1,0:T(8,128)(2,1)S(1)} %get-tuple-element.23.refs_8_), channel_id=1, source_target_pairs={{0,8},{4,12},{8,0},{12,4},{1,9},{5,13},{9,1},{13,5},{2,10},{6,14},... | collective-permute-start | bytes 221192 | tf_op jit(solution)/shard_map/ppermute | solution.py:238
  13.7 2.3 %collective-permute-start.5 = (bf16[32,1152]{1,0:T(8,128)(2,1)S(1)}, bf16[32,1152]{1,0:T(8,128)(2,1)S(1)}, u32[]{:S(2)}, u32[]{:S(2)}) collective-permute-start(bf16[32,1152]{1,0:T(8,128)(2,1)S(1)} %get-tuple-element.28), channel_id=1, source_target_pairs={{0,4},{4,0},{8,12},{12,8},{1,5},{5,1},{9,13},{13,9},{2,6},{6,2},{1... | collective-permute-start | bytes 221192 | tf_op jit(solution)/shard_map/ppermute | solution.py:238

commit v3 on v2

--- a/solution.py
+++ b/solution.py
@@ -11,8 +11,9 @@
 LOG2E = math.log2(math.e)
 DEAD = -1e30
 LANES = 128
+SUBLANES = 8
+ANY = pl.BlockSpec(memory_space=pl.ANY)
 HBM = pl.BlockSpec(memory_space=pltpu.HBM)
-SMEM = pl.BlockSpec(memory_space=pltpu.SMEM)
 VMEM = pl.BlockSpec(memory_space=pltpu.VMEM)
 
 
@@ -93,18 +94,23 @@
             jax.ShapeDtypeStruct((2 * slopes.shape[0], keys), jnp.float32),
             jax.ShapeDtypeStruct((ids.shape[0], LANES), jnp.float32),
         ),
-        in_specs=[VMEM] * 3 + [pl.BlockSpec(memory_space=pl.ANY)],
+        in_specs=[VMEM] * 3 + [ANY],
         out_specs=[VMEM] * 2,
         compiler_params=pltpu.CompilerParams(vmem_limit_bytes=8 << 20),
         name="tables",
     )(slopes, lengths, ids, after)
 
 
-def attend_kernel(shifts, heads, skipped, *refs):
+def period(rows):
+    return LANES // (rows // SUBLANES)
+
+
+def attend_kernel(shifts, skipped, *refs):
     blocks, caches = refs[: len(shifts)], refs[len(shifts) : len(shifts) + 6]
     root_kt, root_v, branch_kt, branch_v, bias, mine = caches
     outs = refs[len(shifts) + 6 + skipped :]
     rows, width = blocks[0].shape
+    heads = bias.shape[0] // 2
     size = width // heads
     every = rows * len(shifts)
     factor = LOG2E / math.sqrt(size)
@@ -124,6 +130,7 @@
 
     ahead = scores(units[0])
     lane = lax.broadcasted_iota(jnp.int32, (every, LANES), 1)
+    place = lax.rem(lane, period(rows))
     level = jnp.zeros((every, LANES), jnp.float32)
     seen = []
     for i, (head, part) in enumerate(units):
@@ -153,28 +160,36 @@
             mixed = (scale_r * inverse) * mixed_r + (scale_b * inverse) * mixed_b
             log = top + jnp.log2(total)
             for k in range(2):
-                cols = slice((head + k) * size, (head + k + 1) * size)
                 half = log[k * every : (k + 1) * every]
-                level = jnp.where(lax.rem(lane, heads) == head + k, half, level)
+                level = jnp.where(lax.rem(place, heads) == head + k, half, level)
                 for j, out in enumerate(outs):
                     at = slice(k * every + j * rows, k * every + (j + 1) * rows)
-                    out[:, cols] = mixed[at].astype(out.dtype)
+                    out[(head + k) * rows : (head + k + 1) * rows, :] = mixed[at].astype(out.dtype)
     high = level.astype(jnp.bfloat16).astype(jnp.float32)
     middle = (level - high).astype(jnp.bfloat16).astype(jnp.float32)
     low = level - high - middle
-    coded = jnp.where(lane < heads, high, jnp.where(lane < 2 * heads, middle, low))
-    coded = jnp.where(lane < 3 * heads, coded, 0.0)
+    coded = jnp.where(place < heads, high, jnp.where(place < 2 * heads, middle, low))
+    coded = jnp.where(place < 3 * heads, coded, 0.0)
+    group = lax.broadcasted_iota(jnp.int32, (SUBLANES, LANES), 1) // period(rows)
     for j, out in enumerate(outs):
-        out[:, width:] = coded[j * rows : (j + 1) * rows].astype(out.dtype)
-
-
-def attend(shifts, blocks, heads, caches, after):
+        packed = jnp.zeros((SUBLANES, LANES), jnp.float32)
+        for g in range(rows // SUBLANES):
+            start = j * rows + g * SUBLANES
+            packed = jnp.where(group == g, coded[start : start + SUBLANES], packed)
+        packed = jnp.concatenate([packed, jnp.zeros_like(packed)], axis=0)
+        out[heads * rows :, :] = packed.astype(out.dtype)
+
+
+def attend(shifts, blocks, caches, after):
     rows, width = blocks[0].shape
     keys = caches[0].shape[1]
-    return pl.pallas_call(
-        functools.partial(attend_kernel, tuple(shifts), heads, len(after)),
-        out_shape=tuple(jax.ShapeDtypeStruct((rows, width + LANES), jnp.bfloat16) for _ in shifts),
-        in_specs=[VMEM] * (len(blocks) + len(caches)) + [pl.BlockSpec(memory_space=pl.ANY)] * len(after),
+    heads = caches[4].shape[0] // 2
+    return pl.pallas_call(
+        functools.partial(attend_kernel, tuple(shifts), len(after)),
+        out_shape=tuple(
+            jax.ShapeDtypeStruct((heads * rows + 2 * SUBLANES, width // heads), jnp.bfloat16) for _ in shifts
+        ),
+        in_specs=[VMEM] * (len(blocks) + len(caches)) + [ANY] * len(after),
         out_specs=[VMEM] * len(shifts),
         compiler_params=pltpu.CompilerParams(vmem_limit_bytes=24 << 20),
         cost_estimate=pl.CostEstimate(
@@ -186,46 +201,57 @@
     )(*blocks, *caches, *after)
 
 
-def spread_logs(heads, size, coded):
-    row = lax.broadcasted_iota(jnp.int32, (LANES, heads * size), 0)
-    col = lax.broadcasted_iota(jnp.int32, (LANES, heads * size), 1)
-    spread = jnp.where((lax.rem(row, heads) == col // size) & (row < 3 * heads), 1.0, 0.0).astype(coded.dtype)
-    return jnp.dot(coded, spread, preferred_element_type=jnp.float32)
-
-
-def merge_kernel(heads, last, *refs):
-    parts, outs = (refs[:-1], refs[-1:]) if last else (refs[:-2], refs[-2:])
-    width = outs[0].shape[1]
-    logs, values = [], []
-    for i, ref in enumerate(parts):
-        if last and i == 0:
-            continue
-        if last and i == 1:
-            logs.append(ref[...])
-            values.append(parts[0][...])
-        else:
-            logs.append(spread_logs(heads, width // heads, ref[:, width:]))
-            values.append(ref[:, :width].astype(jnp.float32))
+def hold_kernel(*refs):
+    pass
+
+
+def hold(arrays):
+    return pl.pallas_call(
+        hold_kernel,
+        out_shape=tuple(jax.ShapeDtypeStruct(array.shape, array.dtype) for array in arrays),
+        in_specs=[ANY] * len(arrays),
+        out_specs=[ANY] * len(arrays),
+        input_output_aliases={i: i for i in range(len(arrays))},
+        compiler_params=pltpu.CompilerParams(vmem_limit_bytes=1 << 20),
+        cost_estimate=pl.CostEstimate(flops=0, bytes_accessed=4 << 20, transcendentals=0),
+        name="hold",
+    )(*arrays)
+
+
+def merge_kernel(*refs):
+    out = refs[-1]
+    rows, width = out.shape
+    heads = (refs[0].shape[0] - 2 * SUBLANES) // rows
+    size = width // heads
+    lane = lax.rem(lax.broadcasted_iota(jnp.int32, (LANES, width), 0), period(rows))
+    head = lax.broadcasted_iota(jnp.int32, (LANES, width), 1) // size
+    spread = jnp.where((lax.rem(lane, heads) == head) & (lane < 3 * heads), 1.0, 0.0).astype(jnp.bfloat16)
+    group = lax.broadcasted_iota(jnp.int32, (SUBLANES, LANES), 1) // period(rows)
+    coded = []
+    for ref in refs[:-1]:
+        packed = ref[heads * rows :, :].astype(jnp.float32)[:SUBLANES]
+        coded += [jnp.where(group == g, packed, 0.0) for g in range(rows // SUBLANES)]
+    coded = jnp.concatenate(coded, axis=0).astype(jnp.bfloat16)
+    logs = jnp.dot(coded, spread, preferred_element_type=jnp.float32)
+    logs = [logs[j * rows : (j + 1) * rows] for j in range(len(refs) - 1)]
     top = functools.reduce(jnp.maximum, logs)
-    scales = [jnp.exp2(log - top) for log in logs]
-    total = functools.reduce(jnp.add, scales)
-    mixed = functools.reduce(jnp.add, [scale * value for scale, value in zip(scales, values)]) / total
-    if last:
-        outs[0][...] = mixed.astype(outs[0].dtype)
-    else:
-        outs[0][...] = mixed
-        outs[1][...] = top + jnp.log2(total)
-
-
-def merge(heads, parts, rows, width, last):
-    whole = jax.ShapeDtypeStruct((rows, width), jnp.float32)
-    return pl.pallas_call(
-        functools.partial(merge_kernel, heads, last),
-        out_shape=jax.ShapeDtypeStruct((rows, width), jnp.bfloat16) if last else (whole, whole),
+    total = jnp.zeros(out.shape, jnp.float32)
+    mixed = jnp.zeros(out.shape, jnp.float32)
+    for log, ref in zip(logs, refs[:-1]):
+        value = jnp.concatenate([ref[h * rows : (h + 1) * rows, :] for h in range(heads)], axis=1)
+        scale = jnp.exp2(log - top)
+        total += scale
+        mixed += scale * value.astype(jnp.float32)
+    out[...] = (mixed / total).astype(out.dtype)
+
+
+def merge(parts, rows, width):
+    return pl.pallas_call(
+        merge_kernel,
+        out_shape=jax.ShapeDtypeStruct((rows, width), jnp.bfloat16),
         in_specs=[VMEM] * len(parts),
-        out_specs=VMEM if last else (VMEM, VMEM),
+        out_specs=VMEM,
         compiler_params=pltpu.CompilerParams(vmem_limit_bytes=8 << 20),
-        cost_estimate=pl.CostEstimate(flops=0, bytes_accessed=4 << 20, transcendentals=0),
         name="merge",
     )(*parts)
 
@@ -237,16 +263,14 @@
     def swap(array, shift):
         return lax.ppermute(array, "seq", [(i, i ^ shift) for i in range(count)])
 
-    near, far = (0, 1), tuple(range(2, count))
+    near, far = (0, 1), tuple(reversed(range(2, count)))
     blocks = {0: queries} | {shift: swap(queries, shift) for shift in far + near[1:]}
-    heads = slopes.shape[0]
     caches = load(root_keys, root_values, branch_keys, branch_values)
     caches += tables(slopes, branch_lengths, branch_ids, rows, root_keys.shape[0], caches[0])
-    sent = attend(far, [blocks[s] for s in far], heads, caches, ())
-    got = [swap(array, shift) for array, shift in zip(sent, far)]
-    kept, passed = attend(near, [blocks[s] for s in near], heads, caches, sent[:1])
-    mixed, logs = merge(heads, got, rows, width, False)
-    return merge(heads, [mixed, logs, kept, swap(passed, 1)], rows, width, True)
+    sent = attend(far, [blocks[s] for s in far], caches, ())
+    got = hold([swap(array, shift) for array, shift in zip(sent, far)])
+    kept, passed = attend(near, [blocks[s] for s in near], caches, sent[:1])
+    return merge([kept, swap(passed, 1), *got], rows, width)
 
 
 def solution(mesh):

time: 17 us -> 16.9 us (level)
  transfers between devices with their start and end apart: 6 -> 6, of which waited for: 1 -> 2; matrix products, arithmetic and copies ran while one was open for 0% -> 0% of each run, Pallas kernels for 47% -> 46%
where the time goes in v3:
time: 16.9 us; the launch traced here: 16.8 us
  Pallas kernels  8.71 us (52%)
  starting transfers between devices  5.37 us (32%)
  waiting for transfers between devices  1.94 us (11%)
  between operations  0.74 us (4%)
    ppermute x6, starting transfers between devices, swap(): return lax.ppermute(array, 'seq', [(i, i ^ shift) for i in range(count)])  5.37 us
    pallas_call x2, Pallas kernels, attend(): pl.pallas_call(functools.partial(attend_kernel, tuple(shifts), len(after)...  4.08 us
    pallas_call x1, Pallas kernels, load(): pl.pallas_call(functools.partial(load_kernel, chunks), out_shape=(jax.Sha...  3.58 us
    ppermute x6, waiting for transfers between devices, swap(): return lax.ppermute(array, 'seq', [(i, i ^ shift) for i in range(count)])  1.94 us
    pallas_call x1, Pallas kernels, merge(): pl.pallas_call(merge_kernel, out_shape=jax.ShapeDtypeStruct((rows, width)...  0.94 us
  transfers between devices with their start and end apart: 6, of which 2 were waited for; matrix products, arithmetic and copies ran while one was open for 0% of the time, Pallas kernels for 46%

profile of v3, /device:TPU:0, one launch (start us, length us, event | category | flops | bytes accessed | tf_op | source)
XLA Modules:
  0.0 16.8 jit_solution(1772130673796191982)
XLA Ops:
  0.0 2.4 %collective-permute-start.1 = (bf16[32,1024]{1,0:T(8,128)(2,1)}, bf16[32,1024]{1,0:T(8,128)(2,1)S(1)}, u32[]{:S(2)}, u32[]{:S(2)}) collective-permute-start(bf16[32,1024]{1,0:T(8,128)(2,1)} %refs_0_.1), channel_id=1, source_target_pairs={{0,12},{4,8},{8,4},{12,0},{1,13},{5,9},{9,5},{13,1},{2,14},{6,10},... | collective-permute-start | bytes 196616 | tf_op jit(solution)/shard_map/ppermute | solution.py:264
  2.4 0.6 %collective-permute-start.2 = (bf16[32,1024]{1,0:T(8,128)(2,1)}, bf16[32,1024]{1,0:T(8,128)(2,1)S(1)}, u32[]{:S(2)}, u32[]{:S(2)}) collective-permute-start(bf16[32,1024]{1,0:T(8,128)(2,1)} %refs_0_.1), channel_id=1, source_target_pairs={{0,8},{4,12},{8,0},{12,4},{1,9},{5,13},{9,1},{13,5},{2,10},{6,14},... | collective-permute-start | bytes 196616 | tf_op jit(solution)/shard_map/ppermute | solution.py:264
  3.0 0.1 collective-permute-start
  3.7 0.0 copy-start.1
  3.7 0.0 copy-start.2
  3.8 3.6 %load.1 = (bf16[1024,1024]{1,0:T(8,128)(2,1)S(1)}, bf16[1024,1024]{1,0:T(8,128)(2,1)S(1)}, bf16[1024,1024]{1,0:T(8,128)(2,1)S(1)}, bf16[1024,1024]{1,0:T(8,128)(2,1)S(1)}) custom-call(bf16[1024,1024]{1,0:T(8,128)(2,1)} %root_k.1, bf16[1024,1024]{1,0:T(8,128)(2,1)} %root_v.1, bf16[1024,1024]{1,0:T(8,128)(2,1)} %branch_k.1, bf16[1024,1024]{1,0:T(8,128)(2,1)} %branch_v.1), custom_call_target="tpu_custom_call" | custom-call | bytes 8388608 | tf_op jit(solution)/shard_map/load/pallas_call | solution.py:46
  7.3 0.0 copy-done.1
  7.4 0.0 copy-done.2
  7.4 0.1 tables.1
  7.5 0.0 collective-permute-done.1.refs_0_
  7.5 0.0 collective-permute-done.2.refs_1_
  7.5 0.0 copy-start
  7.5 2.0 %attend.2 = (bf16[272,128]{1,0:T(8,128)(2,1)S(1)}, bf16[272,128]{1,0:T(8,128)(2,1)S(1)}) custom-call(bf16[32,1024]{1,0:T(8,128)(2,1)S(1)} %collective-permute-done.1.refs_0_, bf16[32,1024]{1,0:T(8,128)(2,1)S(1)} %collective-permute-done.2.refs_1_, bf16[1024,1024]{1,0:T(8,128)(2,1)S(1)} %get-tuple-element.17.after.refs_2_, ...), custom_call_target="tpu_custom_call" | custom-call | flops 536870912 | bytes 8388608 | tf_op jit(solution)/shard_map/attend/pallas_call | solution.py:187
  9.6 1.8 %collective-permute-start.5 = (bf16[272,128]{1,0:T(8,128)(2,1)S(1)}, bf16[272,128]{1,0:T(8,128)(2,1)S(1)}, u32[]{:S(2)}, u32[]{:S(2)}) collective-permute-start(bf16[272,128]{1,0:T(8,128)(2,1)S(1)} %get-tuple-element.26), channel_id=1, source_target_pairs={{0,8},{4,12},{8,0},{12,4},{1,9},{5,13},{9,1},{13,5},{2,10},{6,14},... | collective-permute-start | bytes 208904 | tf_op jit(solution)/shard_map/ppermute | solution.py:264
  11.4 0.0 collective-permute-start.4
  11.4 0.0 collective-permute-done.refs_1_
  11.4 0.0 copy-done
  11.4 2.0 %attend.3 = (bf16[272,128]{1,0:T(8,128)(2,1)S(1)}, bf16[272,128]{1,0:T(8,128)(2,1)S(1)}) custom-call(bf16[32,1024]{1,0:T(8,128)(2,1)S(1)} %copy-done, bf16[32,1024]{1,0:T(8,128)(2,1)S(1)} %collective-permute-done.refs_1_, bf16[1024,1024]{1,0:T(8,128)(2,1)S(1)} %get-tuple-element.17.after.refs_2_, bf16[1024,1024]{1,0:T(8,128)(2,1)S(1)} %get-tuple-element.18.refs_3_, ...), custom_call_target="tpu_custom_call" | custom-call | flops 536870912 | bytes 8388608 | tf_op jit(solution)/shard_map/attend/pallas_call | solution.py:187
  13.5 0.4 %collective-permute-start.3 = (bf16[272,128]{1,0:T(8,128)(2,1)S(1)}, bf16[272,128]{1,0:T(8,128)(2,1)S(1)}, u32[]{:S(2)}, u32[]{:S(2)}) collective-permute-start(bf16[272,128]{1,0:T(8,128)(2,1)S(1)} %get-tuple-element.25), channel_id=1, source_target_pairs={{0,4},{4,0},{8,12},{12,8},{1,5},{5,1},{9,13},{13,9},{2,6},{6,2},{1... | collective-permute-start | bytes 208904 | tf_op jit(solution)/shard_map/ppermute | solution.py:264
  13.9 0.2 %collective-permute-done.5.refs_1_ = bf16[272,128]{1,0:T(8,128)(2,1)S(1)} collective-permute-done((bf16[272,128]{1,0:T(8,128)(2,1)S(1)}, bf16[272,128]{1,0:T(8,128)(2,1)S(1)}, u32[]{:S(2)}, u32[]{:S(2)}) %collective-permute-start.5) | collective-permute-done | bytes 69664 | tf_op jit(solution)/shard_map/ppermute | solution.py:264
  14.2 1.7 %collective-permute-done.4.refs_0_ = bf16[272,128]{1,0:T(8,128)(2,1)S(1)} collective-permute-done((bf16[272,128]{1,0:T(8,128)(2,1)S(1)}, bf16[272,128]{1,0:T(8,128)(2,1)S(1)}, u32[]{:S(2)}, u32[]{:S(2)}) %collective-permute-start.4) | collective-permute-done | bytes 69664 | tf_op jit(solution)/shard_map/ppermute | solution.py:264
  15.8 0.0 collective-permute-done.3.refs_1_
  15.8 0.9 %merge.1 = bf16[32,1024]{1,0:T(8,128)(2,1)} custom-call(bf16[272,128]{1,0:T(8,128)(2,1)S(1)} %get-tuple-element.24.refs_0_, bf16[272,128]{1,0:T(8,128)(2,1)S(1)} %collective-permute-done.3.refs_1_, bf16[272,128]{1,0:T(8,128)(2,1)S(1)} %get-tuple-element.27.refs_2_, bf16[272,128]{1,0:T(8,128)(2,1)S(1)} %get-tuple-element.28.refs_3_), custom_call_target="tpu_custom_call" | custom-call | tf_op jit(solution)/shard_map/merge/pallas_call | solution.py:249
  (1 shorter events, 0.0 us)
Async XLA Ops:
  0.0 7.5 %collective-permute-start.1 = (bf16[32,1024]{1,0:T(8,128)(2,1)}, bf16[32,1024]{1,0:T(8,128)(2,1)S(1)}, u32[]{:S(2)}, u32[]{:S(2)}) collective-permute-start(bf16[32,1024]{1,0:T(8,128)(2,1)} %refs_0_.1), channel_id=1, source_target_pairs={{0,12},{4,8},{8,4},{12,0},{1,13},{5,9},{9,5},{13,1},{2,14},{6,10},... | collective-permute-start | bytes 196616 | tf_op jit(solution)/shard_map/ppermute | solution.py:264
  2.4 5.1 %collective-permute-start.2 = (bf16[32,1024]{1,0:T(8,128)(2,1)}, bf16[32,1024]{1,0:T(8,128)(2,1)S(1)}, u32[]{:S(2)}, u32[]{:S(2)}) collective-permute-start(bf16[32,1024]{1,0:T(8,128)(2,1)} %refs_0_.1), channel_id=1, source_target_pairs={{0,8},{4,12},{8,0},{12,4},{1,9},{5,13},{9,1},{13,5},{2,10},{6,14},... | collective-permute-start | bytes 196616 | tf_op jit(solution)/shard_map/ppermute | solution.py:264
  3.0 8.4 %collective-permute-start = (bf16[32,1024]{1,0:T(8,128)(2,1)}, bf16[32,1024]{1,0:T(8,128)(2,1)S(1)}, u32[]{:S(2)}, u32[]{:S(2)}) collective-permute-start(bf16[32,1024]{1,0:T(8,128)(2,1)} %refs_0_.1), channel_id=1, source_target_pairs={{0,4},{4,0},{8,12},{12,8},{1,5},{5,1},{9,13},{13,9},{2,6},{6,2},{1... | collective-permute-start | bytes 196616 | tf_op jit(solution)/shard_map/ppermute | solution.py:264
  3.7 3.6 %copy-start.1 = (f32[8]{0:T(128)S(1)}, f32[8]{0:T(128)}, u32[]{:S(2)}) copy-start(f32[8]{0:T(128)} %slopes.1) | copy-start | bytes 100
  3.7 3.6 %copy-start.2 = (s32[128]{0:T(128)S(1)}, s32[128]{0:T(128)}, u32[]{:S(2)}) copy-start(s32[128]{0:T(128)} %ids.1) | copy-start | bytes 1540
  7.5 3.9 %copy-start = (bf16[32,1024]{1,0:T(8,128)(2,1)S(1)}, bf16[32,1024]{1,0:T(8,128)(2,1)}, u32[]{:S(2)}) copy-start(bf16[32,1024]{1,0:T(8,128)(2,1)} %refs_0_.1) | copy-start | bytes 196612
  9.6 4.6 %collective-permute-start.5 = (bf16[272,128]{1,0:T(8,128)(2,1)S(1)}, bf16[272,128]{1,0:T(8,128)(2,1)S(1)}, u32[]{:S(2)}, u32[]{:S(2)}) collective-permute-start(bf16[272,128]{1,0:T(8,128)(2,1)S(1)} %get-tuple-element.26), channel_id=1, source_target_pairs={{0,8},{4,12},{8,0},{12,4},{1,9},{5,13},{9,1},{13,5},{2,10},{6,14},... | collective-permute-start | bytes 208904 | tf_op jit(solution)/shard_map/ppermute | solution.py:264
  11.4 4.5 %collective-permute-start.4 = (bf16[272,128]{1,0:T(8,128)(2,1)S(1)}, bf16[272,128]{1,0:T(8,128)(2,1)S(1)}, u32[]{:S(2)}, u32[]{:S(2)}) collective-permute-start(bf16[272,128]{1,0:T(8,128)(2,1)S(1)} %get-tuple-element.23.refs_8_), channel_id=1, source_target_pairs={{0,12},{4,8},{8,4},{12,0},{1,13},{5,9},{9,5},{13,1},{2,14},{6,10},... | collective-permute-start | bytes 208904 | tf_op jit(solution)/shard_map/ppermute | solution.py:264
  13.5 2.4 %collective-permute-start.3 = (bf16[272,128]{1,0:T(8,128)(2,1)S(1)}, bf16[272,128]{1,0:T(8,128)(2,1)S(1)}, u32[]{:S(2)}, u32[]{:S(2)}) collective-permute-start(bf16[272,128]{1,0:T(8,128)(2,1)S(1)} %get-tuple-element.25), channel_id=1, source_target_pairs={{0,4},{4,0},{8,12},{12,8},{1,5},{5,1},{9,13},{13,9},{2,6},{6,2},{1... | collective-permute-start | bytes 208904 | tf_op jit(solution)/shard_map/ppermute | solution.py:264

commit v4 on v3

--- a/solution.py
+++ b/solution.py
@@ -17,50 +17,49 @@
 VMEM = pl.BlockSpec(memory_space=pltpu.VMEM)
 
 
-def load_kernel(chunks, root_k, root_v, branch_k, branch_v, root_kt, root_vv, branch_kt, branch_vv, held, sems):
-    rows = root_k.shape[0] // chunks
+def load_kernel(chunks, turned, straight, skipped, *refs):
+    sources, outs = refs[: turned + straight], refs[turned + straight + skipped : 2 * (turned + straight) + skipped]
+    sems = refs[-1]
+    keys, width = sources[0].shape
+    rows = keys // chunks
     copies = []
-    for i, (src, slot) in enumerate(((root_k, 0), (branch_k, 1))):
+    for i in range(turned):
         for j in range(chunks):
             part = pl.ds(j * rows, rows)
-            copies.append(pltpu.make_async_copy(src.at[part], held.at[slot, part], sems.at[i * chunks + j]))
-    values = [
-        pltpu.make_async_copy(root_v, root_vv, sems.at[2 * chunks]),
-        pltpu.make_async_copy(branch_v, branch_vv, sems.at[2 * chunks + 1]),
-    ]
-    for copy in copies + values:
+            copies.append(
+                pltpu.make_async_copy(sources[i].at[part], refs[-2].at[i, part], sems.at[i * chunks + j])
+            )
+    for i in range(turned, turned + straight):
+        copies.append(pltpu.make_async_copy(sources[i], outs[i], sems.at[turned * chunks + i - turned]))
+    for copy in copies:
         copy.start()
-    for slot, out in ((0, root_kt), (1, branch_kt)):
+    for i in range(turned):
         for j in range(chunks):
-            copies[slot * chunks + j].wait()
+            copies[i * chunks + j].wait()
             part = slice(j * rows, (j + 1) * rows)
-            for col in range(0, root_k.shape[1], LANES):
-                out[col : col + LANES, part] = held[slot, part, col : col + LANES].T
-    for copy in values:
+            for col in range(0, width, LANES):
+                outs[i][col : col + LANES, part] = refs[-2][i, part, col : col + LANES].T
+    for copy in copies[turned * chunks :]:
         copy.wait()
 
 
-def load(root_k, root_v, branch_k, branch_v):
+def load(turned, straight, after, limit):
     chunks = 4
-    keys, width = root_k.shape
-    return pl.pallas_call(
-        functools.partial(load_kernel, chunks),
-        out_shape=(
-            jax.ShapeDtypeStruct((width, keys), root_k.dtype),
-            jax.ShapeDtypeStruct((keys, width), root_k.dtype),
-            jax.ShapeDtypeStruct((width, keys), root_k.dtype),
-            jax.ShapeDtypeStruct((keys, width), root_k.dtype),
-        ),
-        in_specs=[HBM] * 4,
-        out_specs=[VMEM] * 4,
-        scratch_shapes=[
-            pltpu.VMEM((2, keys, width), root_k.dtype),
-            pltpu.SemaphoreType.DMA((2 * chunks + 2,)),
-        ],
-        compiler_params=pltpu.CompilerParams(vmem_limit_bytes=44 << 20),
-        cost_estimate=pl.CostEstimate(flops=0, bytes_accessed=8 * keys * width, transcendentals=0),
+    arrays = (*turned, *straight)
+    keys, width = arrays[0].shape
+    kind = arrays[0].dtype
+    return pl.pallas_call(
+        functools.partial(load_kernel, chunks, len(turned), len(straight), len(after)),
+        out_shape=tuple(jax.ShapeDtypeStruct((width, keys), kind) for _ in turned)
+        + tuple(jax.ShapeDtypeStruct((keys, width), kind) for _ in straight),
+        in_specs=[HBM] * len(arrays) + [ANY] * len(after),
+        out_specs=(VMEM,) * len(arrays),
+        scratch_shapes=[pltpu.VMEM((len(turned), keys, width), kind)] * (len(turned) > 0)
+        + [pltpu.SemaphoreType.DMA((len(turned) * chunks + len(straight),))],
+        compiler_params=pltpu.CompilerParams(vmem_limit_bytes=limit << 20),
+        cost_estimate=pl.CostEstimate(flops=0, bytes_accessed=2 * len(arrays) * keys * width, transcendentals=0),
         name="load",
-    )(root_k, root_v, branch_k, branch_v)
+    )(*arrays, *after)
 
 
 def column(vector, rows, start):
@@ -205,17 +204,17 @@
     pass
 
 
-def hold(arrays):
+def hold(arrays, after=()):
     return pl.pallas_call(
         hold_kernel,
         out_shape=tuple(jax.ShapeDtypeStruct(array.shape, array.dtype) for array in arrays),
-        in_specs=[ANY] * len(arrays),
+        in_specs=[ANY] * (len(arrays) + len(after)),
         out_specs=[ANY] * len(arrays),
         input_output_aliases={i: i for i in range(len(arrays))},
         compiler_params=pltpu.CompilerParams(vmem_limit_bytes=1 << 20),
         cost_estimate=pl.CostEstimate(flops=0, bytes_accessed=4 << 20, transcendentals=0),
         name="hold",
-    )(*arrays)
+    )(*arrays, *after)
 
 
 def merge_kernel(*refs):
@@ -263,10 +262,16 @@
     def swap(array, shift):
         return lax.ppermute(array, "seq", [(i, i ^ shift) for i in range(count)])
 
-    near, far = (0, 1), tuple(reversed(range(2, count)))
-    blocks = {0: queries} | {shift: swap(queries, shift) for shift in far + near[1:]}
-    caches = load(root_keys, root_values, branch_keys, branch_values)
-    caches += tables(slopes, branch_lengths, branch_ids, rows, root_keys.shape[0], caches[0])
+    near, across = (0, 1), tuple(range(2, count, 2))
+    far = across + tuple(shift + 1 for shift in across)
+    blocks = {shift: swap(queries, shift) for shift in across}
+    blocks[0], blocks[1] = queries, swap(queries, 1)
+    root_kt, branch_kt, root_v = load((root_keys, branch_keys), (root_values,), (), 46)
+    arrived = hold([blocks[shift] for shift in across], (root_kt, blocks[1]))
+    for shift, block in zip(across, arrived):
+        blocks[shift], blocks[shift + 1] = block, swap(block, 1)
+    bias, mine = tables(slopes, branch_lengths, branch_ids, rows, root_keys.shape[0], root_kt)
+    caches = (root_kt, root_v, branch_kt, branch_values, bias, mine)
     sent = attend(far, [blocks[s] for s in far], caches, ())
     got = hold([swap(array, shift) for array, shift in zip(sent, far)])
     kept, passed = attend(near, [blocks[s] for s in near], caches, sent[:1])

time: 16.9 us -> 16.8 us (level)
  Pallas kernels: 8.71 us -> 8.08 us
  local copies, waits for them, and re-layouts: 0.01 us -> 0.29 us
  between operations: 0.74 us -> 0.91 us
    pallas_call x1, Pallas kernels: 3.58 us -> 2.96 us  [load(): pl.pallas_call(functools.partial(load_kernel, chunks, len(turned), len(st...]
    unnamed x6 -> x8, local copies, waits for them, and re-layouts: 0.01 us -> 0.29 us
  transfers between devices with their start and end apart: 6 -> 6, of which waited for: 2 -> 3; matrix products, arithmetic and copies ran while one was open for 0% -> 0% of each run, Pallas kernels for 46% -> 31%
where the time goes in v4:
time: 16.8 us; the launch traced here: 16.6 us
  Pallas kernels  8.08 us (48%)
  starting transfers between devices  5.27 us (31%)
  waiting for transfers between devices  2.06 us (12%)
  between operations  0.91 us (5%)
  local copies, waits for them, and re-layouts  0.29 us (2%)
    ppermute x6, starting transfers between devices, swap(): return lax.ppermute(array, 'seq', [(i, i ^ shift) for i in range(count)])  5.27 us
    pallas_call x2, Pallas kernels, attend(): pl.pallas_call(functools.partial(attend_kernel, tuple(shifts), len(after)...  4.07 us
    pallas_call x1, Pallas kernels, load(): pl.pallas_call(functools.partial(load_kernel, chunks, len(turned), len(st...  2.96 us
    ppermute x6, waiting for transfers between devices, swap(): return lax.ppermute(array, 'seq', [(i, i ^ shift) for i in range(count)])  2.06 us
    pallas_call x1, Pallas kernels, merge(): pl.pallas_call(merge_kernel, out_shape=jax.ShapeDtypeStruct((rows, width)...  0.94 us
  transfers between devices with their start and end apart: 6, of which 3 were waited for; matrix products, arithmetic and copies ran while one was open for 0% of the time, Pallas kernels for 31%

profile of v4, /device:TPU:0, one launch (start us, length us, event | category | flops | bytes accessed | tf_op | source)
XLA Modules:
  0.0 16.6 jit_solution(5520023494841221680)
XLA Ops:
  0.0 0.5 %collective-permute-start = (bf16[32,1024]{1,0:T(8,128)(2,1)}, bf16[32,1024]{1,0:T(8,128)(2,1)S(1)}, u32[]{:S(2)}, u32[]{:S(2)}) collective-permute-start(bf16[32,1024]{1,0:T(8,128)(2,1)} %refs_0_.3), channel_id=1, source_target_pairs={{0,4},{4,0},{8,12},{12,8},{1,5},{5,1},{9,13},{13,9},{2,6},{6,2},{1... | collective-permute-start | bytes 196616 | tf_op jit(solution)/shard_map/ppermute | solution.py:263
  0.5 2.5 %collective-permute-start.1 = (bf16[32,1024]{1,0:T(8,128)(2,1)}, bf16[32,1024]{1,0:T(8,128)(2,1)S(1)}, u32[]{:S(2)}, u32[]{:S(2)}) collective-permute-start(bf16[32,1024]{1,0:T(8,128)(2,1)} %refs_0_.3), channel_id=1, source_target_pairs={{0,8},{4,12},{8,0},{12,4},{1,9},{5,13},{9,1},{13,5},{2,10},{6,14},... | collective-permute-start | bytes 196616 | tf_op jit(solution)/shard_map/ppermute | solution.py:263
  3.0 3.0 %load.1 = (bf16[1024,1024]{1,0:T(8,128)(2,1)S(1)}, bf16[1024,1024]{1,0:T(8,128)(2,1)S(1)}, bf16[1024,1024]{1,0:T(8,128)(2,1)S(1)}) custom-call(bf16[1024,1024]{1,0:T(8,128)(2,1)} %refs_0_.2, bf16[1024,1024]{1,0:T(8,128)(2,1)} %refs_1_.1, bf16[1024,1024]{1,0:T(8,128)(2,1)} %refs_2_.1), custom_call_target="tpu_custom_call" | custom-call | bytes 6291456 | tf_op jit(solution)/shard_map/load/pallas_call | solution.py:51
  5.9 0.0 copy-start.2
  5.9 0.0 copy-start.3
  6.0 0.0 collective-permute-done.refs_2_.refs_1_
  6.0 0.0 collective-permute-done.1.refs_0_
  6.0 0.0 copy-start
  6.0 0.3 %collective-permute-start.2 = (bf16[32,1024]{1,0:T(8,128)(2,1)S(1)}, bf16[32,1024]{1,0:T(8,128)(2,1)S(1)}, u32[]{:S(2)}, u32[]{:S(2)}) collective-permute-start(bf16[32,1024]{1,0:T(8,128)(2,1)S(1)} %hold.2.refs_0_), channel_id=1, source_target_pairs={{0,4},{4,0},{8,12},{12,8},{1,5},{5,1},{9,13},{13,9},{2,6},{6,2},{1... | collective-permute-start | bytes 196616 | tf_op jit(solution)/shard_map/ppermute | solution.py:263
  7.1 0.0 copy-done.2
  7.1 0.0 copy-done.3
  7.1 0.1 tables.1
  7.2 0.1 collective-permute-done.2.refs_1_
  7.3 0.3 %copy-done = bf16[1024,1024]{1,0:T(8,128)(2,1)S(1)} copy-done((bf16[1024,1024]{1,0:T(8,128)(2,1)S(1)}, bf16[1024,1024]{1,0:T(8,128)(2,1)}, u32[]{:S(2)}) %copy-start) | copy-done | bytes 2097176
  7.6 0.0 copy-start.1
  7.6 2.0 %attend.2 = (bf16[272,128]{1,0:T(8,128)(2,1)S(1)}, bf16[272,128]{1,0:T(8,128)(2,1)S(1)}) custom-call(bf16[32,1024]{1,0:T(8,128)(2,1)S(1)} %hold.2.refs_0_, bf16[32,1024]{1,0:T(8,128)(2,1)S(1)} %collective-permute-done.2.refs_1_, bf16[1024,1024]{1,0:T(8,128)(2,1)S(1)} %get-tuple-element.16.after.refs_1_.refs_2_, ...), custom_call_target="tpu_custom_call" | custom-call | flops 536870912 | bytes 8388608 | tf_op jit(solution)/shard_map/attend/pallas_call | solution.py:186
  9.6 1.2 %collective-permute-start.5 = (bf16[272,128]{1,0:T(8,128)(2,1)S(1)}, bf16[272,128]{1,0:T(8,128)(2,1)S(1)}, u32[]{:S(2)}, u32[]{:S(2)}) collective-permute-start(bf16[272,128]{1,0:T(8,128)(2,1)S(1)} %get-tuple-element.24), channel_id=1, source_target_pairs={{0,12},{4,8},{8,4},{12,0},{1,13},{5,9},{9,5},{13,1},{2,14},{6,10},... | collective-permute-start | bytes 208904 | tf_op jit(solution)/shard_map/ppermute | solution.py:263
  10.8 0.7 %collective-permute-start.4 = (bf16[272,128]{1,0:T(8,128)(2,1)S(1)}, bf16[272,128]{1,0:T(8,128)(2,1)S(1)}, u32[]{:S(2)}, u32[]{:S(2)}) collective-permute-start(bf16[272,128]{1,0:T(8,128)(2,1)S(1)} %get-tuple-element.21.refs_8_), channel_id=1, source_target_pairs={{0,8},{4,12},{8,0},{12,4},{1,9},{5,13},{9,1},{13,5},{2,10},{6,14},... | collective-permute-start | bytes 208904 | tf_op jit(solution)/shard_map/ppermute | solution.py:263
  11.6 0.0 copy-done.1
  11.6 2.0 %attend.3 = (bf16[272,128]{1,0:T(8,128)(2,1)S(1)}, bf16[272,128]{1,0:T(8,128)(2,1)S(1)}) custom-call(bf16[32,1024]{1,0:T(8,128)(2,1)S(1)} %copy-done.1, bf16[32,1024]{1,0:T(8,128)(2,1)S(1)} %collective-permute-done.refs_2_.refs_1_, bf16[1024,1024]{1,0:T(8,128)(2,1)S(1)} %get-tuple-element.16.after.refs_1_.refs_2_, ...), custom_call_target="tpu_custom_call" | custom-call | flops 536870912 | bytes 8388608 | tf_op jit(solution)/shard_map/attend/pallas_call | solution.py:186
  13.6 0.1 collective-permute-start.3
  13.7 0.1 collective-permute-done.5.refs_1_
  13.8 1.8 %collective-permute-done.4.refs_0_ = bf16[272,128]{1,0:T(8,128)(2,1)S(1)} collective-permute-done((bf16[272,128]{1,0:T(8,128)(2,1)S(1)}, bf16[272,128]{1,0:T(8,128)(2,1)S(1)}, u32[]{:S(2)}, u32[]{:S(2)}) %collective-permute-start.4) | collective-permute-done | bytes 69664 | tf_op jit(solution)/shard_map/ppermute | solution.py:263
  15.7 0.0 collective-permute-done.3.refs_1_
  15.7 0.9 %merge.1 = bf16[32,1024]{1,0:T(8,128)(2,1)} custom-call(bf16[272,128]{1,0:T(8,128)(2,1)S(1)} %get-tuple-element.22.refs_0_, bf16[272,128]{1,0:T(8,128)(2,1)S(1)} %collective-permute-done.3.refs_1_, bf16[272,128]{1,0:T(8,128)(2,1)S(1)} %get-tuple-element.25.refs_2_, bf16[272,128]{1,0:T(8,128)(2,1)S(1)} %get-tuple-element.26.refs_3_), custom_call_target="tpu_custom_call" | custom-call | tf_op jit(solution)/shard_map/merge/pallas_call | solution.py:248
  (2 shorter events, 0.0 us)
Async XLA Ops:
  0.0 6.0 %collective-permute-start = (bf16[32,1024]{1,0:T(8,128)(2,1)}, bf16[32,1024]{1,0:T(8,128)(2,1)S(1)}, u32[]{:S(2)}, u32[]{:S(2)}) collective-permute-start(bf16[32,1024]{1,0:T(8,128)(2,1)} %refs_0_.3), channel_id=1, source_target_pairs={{0,4},{4,0},{8,12},{12,8},{1,5},{5,1},{9,13},{13,9},{2,6},{6,2},{1... | collective-permute-start | bytes 196616 | tf_op jit(solution)/shard_map/ppermute | solution.py:263
  0.5 5.5 %collective-permute-start.1 = (bf16[32,1024]{1,0:T(8,128)(2,1)}, bf16[32,1024]{1,0:T(8,128)(2,1)S(1)}, u32[]{:S(2)}, u32[]{:S(2)}) collective-permute-start(bf16[32,1024]{1,0:T(8,128)(2,1)} %refs_0_.3), channel_id=1, source_target_pairs={{0,8},{4,12},{8,0},{12,4},{1,9},{5,13},{9,1},{13,5},{2,10},{6,14},... | collective-permute-start | bytes 196616 | tf_op jit(solution)/shard_map/ppermute | solution.py:263
  5.9 1.2 %copy-start.2 = (f32[8]{0:T(128)S(1)}, f32[8]{0:T(128)}, u32[]{:S(2)}) copy-start(f32[8]{0:T(128)} %slopes.1) | copy-start | bytes 100
  5.9 1.2 %copy-start.3 = (s32[128]{0:T(128)S(1)}, s32[128]{0:T(128)}, u32[]{:S(2)}) copy-start(s32[128]{0:T(128)} %ids.1) | copy-start | bytes 1540
  6.0 1.6 %copy-start = (bf16[1024,1024]{1,0:T(8,128)(2,1)S(1)}, bf16[1024,1024]{1,0:T(8,128)(2,1)}, u32[]{:S(2)}) copy-start(bf16[1024,1024]{1,0:T(8,128)(2,1)} %refs_5_.3) | copy-start | bytes 6291460
  6.0 1.3 %collective-permute-start.2 = (bf16[32,1024]{1,0:T(8,128)(2,1)S(1)}, bf16[32,1024]{1,0:T(8,128)(2,1)S(1)}, u32[]{:S(2)}, u32[]{:S(2)}) collective-permute-start(bf16[32,1024]{1,0:T(8,128)(2,1)S(1)} %hold.2.refs_0_), channel_id=1, source_target_pairs={{0,4},{4,0},{8,12},{12,8},{1,5},{5,1},{9,13},{13,9},{2,6},{6,2},{1... | collective-permute-start | bytes 196616 | tf_op jit(solution)/shard_map/ppermute | solution.py:263
  7.6 4.0 %copy-start.1 = (bf16[32,1024]{1,0:T(8,128)(2,1)S(1)}, bf16[32,1024]{1,0:T(8,128)(2,1)}, u32[]{:S(2)}) copy-start(bf16[32,1024]{1,0:T(8,128)(2,1)} %refs_0_.3) | copy-start | bytes 196612
  9.6 4.2 %collective-permute-start.5 = (bf16[272,128]{1,0:T(8,128)(2,1)S(1)}, bf16[272,128]{1,0:T(8,128)(2,1)S(1)}, u32[]{:S(2)}, u32[]{:S(2)}) collective-permute-start(bf16[272,128]{1,0:T(8,128)(2,1)S(1)} %get-tuple-element.24), channel_id=1, source_target_pairs={{0,12},{4,8},{8,4},{12,0},{1,13},{5,9},{9,5},{13,1},{2,14},{6,10},... | collective-permute-start | bytes 208904 | tf_op jit(solution)/shard_map/ppermute | solution.py:263
  10.8 4.8 %collective-permute-start.4 = (bf16[272,128]{1,0:T(8,128)(2,1)S(1)}, bf16[272,128]{1,0:T(8,128)(2,1)S(1)}, u32[]{:S(2)}, u32[]{:S(2)}) collective-permute-start(bf16[272,128]{1,0:T(8,128)(2,1)S(1)} %get-tuple-element.21.refs_8_), channel_id=1, source_target_pairs={{0,8},{4,12},{8,0},{12,4},{1,9},{5,13},{9,1},{13,5},{2,10},{6,14},... | collective-permute-start | bytes 208904 | tf_op jit(solution)/shard_map/ppermute | solution.py:263
  13.6 2.1 %collective-permute-start.3 = (bf16[272,128]{1,0:T(8,128)(2,1)S(1)}, bf16[272,128]{1,0:T(8,128)(2,1)S(1)}, u32[]{:S(2)}, u32[]{:S(2)}) collective-permute-start(bf16[272,128]{1,0:T(8,128)(2,1)S(1)} %get-tuple-element.23), channel_id=1, source_target_pairs={{0,4},{4,0},{8,12},{12,8},{1,5},{5,1},{9,13},{13,9},{2,6},{6,2},{1... | collective-permute-start | bytes 208904 | tf_op jit(solution)/shard_map/ppermute | solution.py:263

commit v5 on v4

--- a/solution.py
+++ b/solution.py
@@ -69,7 +69,7 @@
     return jnp.sum(jnp.where(lane == sub + start, wide, jnp.zeros_like(wide)), axis=1, keepdims=True)
 
 
-def tables_kernel(rows, slopes, lengths, ids, after, bias, mine):
+def tables_kernel(rows, slopes, lengths, ids, after, brought, bias, mine):
     me = lax.axis_index("seq")
     count = lax.axis_size("seq")
     heads = slopes.shape[0]
@@ -86,18 +86,18 @@
         mine[shift * rows : (shift + 1) * rows, :] = jnp.broadcast_to(at, (rows, LANES))
 
 
-def tables(slopes, lengths, ids, rows, keys, after):
+def tables(slopes, lengths, ids, rows, keys, after, brought):
     return pl.pallas_call(
         functools.partial(tables_kernel, rows),
         out_shape=(
             jax.ShapeDtypeStruct((2 * slopes.shape[0], keys), jnp.float32),
             jax.ShapeDtypeStruct((ids.shape[0], LANES), jnp.float32),
         ),
-        in_specs=[VMEM] * 3 + [ANY],
+        in_specs=[VMEM] * 3 + [ANY, VMEM],
         out_specs=[VMEM] * 2,
         compiler_params=pltpu.CompilerParams(vmem_limit_bytes=8 << 20),
         name="tables",
-    )(slopes, lengths, ids, after)
+    )(slopes, lengths, ids, after, brought)
 
 
 def period(rows):
@@ -114,18 +114,17 @@
     every = rows * len(shifts)
     factor = LOG2E / math.sqrt(size)
     own = jnp.concatenate([mine[shift * rows : (shift + 1) * rows, :1] for shift in shifts] * 2, axis=0) > 0.5
-    zero = jnp.zeros((every, size), blocks[0].dtype)
     units = [(head, part) for head in range(0, heads, 2) for part in (0, 1)]
 
     def scores(unit):
         head, part = unit
-        first = jnp.concatenate([b[:, head * size : (head + 1) * size] for b in blocks], axis=0)
-        second = jnp.concatenate([b[:, (head + 1) * size : (head + 2) * size] for b in blocks], axis=0)
-        left = jnp.concatenate(
-            [jnp.concatenate([first, zero], axis=1), jnp.concatenate([zero, second], axis=1)], axis=0
-        )
-        key = (root_kt, branch_kt)[part][head * size : (head + 2) * size, :]
-        return jnp.dot(left, key, preferred_element_type=jnp.float32)
+        both = []
+        for k in (head, head + 1):
+            cols = slice(k * size, (k + 1) * size)
+            query = jnp.concatenate([b[:, cols] for b in blocks], axis=0)
+            key = (root_kt, branch_kt)[part][cols, :]
+            both.append(jnp.dot(query, key, preferred_element_type=jnp.float32))
+        return jnp.concatenate(both, axis=0)
 
     ahead = scores(units[0])
     lane = lax.broadcasted_iota(jnp.int32, (every, LANES), 1)
@@ -263,14 +262,14 @@
         return lax.ppermute(array, "seq", [(i, i ^ shift) for i in range(count)])
 
     near, across = (0, 1), tuple(range(2, count, 2))
-    far = across + tuple(shift + 1 for shift in across)
+    far = tuple(shift + 1 for shift in across) + across
     blocks = {shift: swap(queries, shift) for shift in across}
     blocks[0], blocks[1] = queries, swap(queries, 1)
     root_kt, branch_kt, root_v = load((root_keys, branch_keys), (root_values,), (), 46)
     arrived = hold([blocks[shift] for shift in across], (root_kt, blocks[1]))
     for shift, block in zip(across, arrived):
         blocks[shift], blocks[shift + 1] = block, swap(block, 1)
-    bias, mine = tables(slopes, branch_lengths, branch_ids, rows, root_keys.shape[0], root_kt)
+    bias, mine = tables(slopes, branch_lengths, branch_ids, rows, root_keys.shape[0], root_kt, branch_values)
     caches = (root_kt, root_v, branch_kt, branch_values, bias, mine)
     sent = attend(far, [blocks[s] for s in far], caches, ())
     got = hold([swap(array, shift) for array, shift in zip(sent, far)])

time: 16.8 us -> 16.5 us (0.982)
  waiting for transfers between devices: 2.06 us -> 1.52 us
  starting transfers between devices: 5.27 us -> 5.54 us
    ppermute x6, waiting for transfers between devices: 2.06 us -> 1.52 us  [swap(): return lax.ppermute(array, 'seq', [(i, i ^ shift) for i in range(count)])]
    ppermute x6, starting transfers between devices: 5.27 us -> 5.54 us  [swap(): return lax.ppermute(array, 'seq', [(i, i ^ shift) for i in range(count)])]
  transfers between devices with their start and end apart: 6 -> 6, of which waited for: 3 -> 2; matrix products, arithmetic and copies ran while one was open for 0% -> 0% of each run, Pallas kernels for 31% -> 31%
where the time goes in v5:
time: 16.5 us; the launch traced here: 16.3 us
  Pallas kernels  7.92 us (48%)
  starting transfers between devices  5.54 us (34%)
  waiting for transfers between devices  1.52 us (9%)
  between operations  0.93 us (6%)
  local copies, waits for them, and re-layouts  0.45 us (3%)
    ppermute x6, starting transfers between devices, swap(): return lax.ppermute(array, 'seq', [(i, i ^ shift) for i in range(count)])  5.54 us
    pallas_call x2, Pallas kernels, attend(): pl.pallas_call(functools.partial(attend_kernel, tuple(shifts), len(after)...  3.91 us
    pallas_call x1, Pallas kernels, load(): pl.pallas_call(functools.partial(load_kernel, chunks, len(turned), len(st...  2.96 us
    ppermute x6, waiting for transfers between devices, swap(): return lax.ppermute(array, 'seq', [(i, i ^ shift) for i in range(count)])  1.52 us
    pallas_call x1, Pallas kernels, merge(): pl.pallas_call(merge_kernel, out_shape=jax.ShapeDtypeStruct((rows, width)...  0.94 us
    unnamed x8, local copies, waits for them, and re-layouts  0.45 us
  transfers between devices with their start and end apart: 6, of which 2 were waited for; matrix products, arithmetic and copies ran while one was open for 0% of the time, Pallas kernels for 31%

profile of v5, /device:TPU:0, one launch (start us, length us, event | category | flops | bytes accessed | tf_op | source)
XLA Modules:
  0.0 16.3 jit_solution(13672510908135757466)
XLA Ops:
  0.0 0.5 %collective-permute-start = (bf16[32,1024]{1,0:T(8,128)(2,1)}, bf16[32,1024]{1,0:T(8,128)(2,1)S(1)}, u32[]{:S(2)}, u32[]{:S(2)}) collective-permute-start(bf16[32,1024]{1,0:T(8,128)(2,1)} %refs_0_.3), channel_id=1, source_target_pairs={{0,4},{4,0},{8,12},{12,8},{1,5},{5,1},{9,13},{13,9},{2,6},{6,2},{1... | collective-permute-start | bytes 196616 | tf_op jit(solution)/shard_map/ppermute | solution.py:262
  0.5 2.5 %collective-permute-start.1 = (bf16[32,1024]{1,0:T(8,128)(2,1)}, bf16[32,1024]{1,0:T(8,128)(2,1)S(1)}, u32[]{:S(2)}, u32[]{:S(2)}) collective-permute-start(bf16[32,1024]{1,0:T(8,128)(2,1)} %refs_0_.3), channel_id=1, source_target_pairs={{0,8},{4,12},{8,0},{12,4},{1,9},{5,13},{9,1},{13,5},{2,10},{6,14},... | collective-permute-start | bytes 196616 | tf_op jit(solution)/shard_map/ppermute | solution.py:262
  3.0 3.0 %load.1 = (bf16[1024,1024]{1,0:T(8,128)(2,1)S(1)}, bf16[1024,1024]{1,0:T(8,128)(2,1)S(1)}, bf16[1024,1024]{1,0:T(8,128)(2,1)S(1)}) custom-call(bf16[1024,1024]{1,0:T(8,128)(2,1)} %refs_0_.2, bf16[1024,1024]{1,0:T(8,128)(2,1)} %refs_1_.1, bf16[1024,1024]{1,0:T(8,128)(2,1)} %refs_2_.1), custom_call_target="tpu_custom_call" | custom-call | bytes 6291456 | tf_op jit(solution)/shard_map/load/pallas_call | solution.py:51
  5.9 0.0 copy-start
  5.9 0.0 copy-start.2
  6.0 0.0 copy-start.3
  6.0 0.0 collective-permute-done.refs_2_.refs_1_
  6.0 0.0 collective-permute-done.1.refs_0_
  6.0 0.3 %collective-permute-start.2 = (bf16[32,1024]{1,0:T(8,128)(2,1)S(1)}, bf16[32,1024]{1,0:T(8,128)(2,1)S(1)}, u32[]{:S(2)}, u32[]{:S(2)}) collective-permute-start(bf16[32,1024]{1,0:T(8,128)(2,1)S(1)} %hold.2.refs_1_), channel_id=1, source_target_pairs={{0,4},{4,0},{8,12},{12,8},{1,5},{5,1},{9,13},{13,9},{2,6},{6,2},{1... | collective-permute-start | bytes 196616 | tf_op jit(solution)/shard_map/ppermute | solution.py:262
  7.1 0.4 %copy-done = bf16[1024,1024]{1,0:T(8,128)(2,1)S(1)} copy-done((bf16[1024,1024]{1,0:T(8,128)(2,1)S(1)}, bf16[1024,1024]{1,0:T(8,128)(2,1)}, u32[]{:S(2)}) %copy-start) | copy-done | bytes 2097176
  7.5 0.0 copy-done.2
  7.5 0.0 copy-done.3
  7.5 0.1 tables.1
  7.7 0.0 collective-permute-done.2.refs_0_
  7.7 0.0 copy-start.1
  7.7 2.0 %attend.2 = (bf16[272,128]{1,0:T(8,128)(2,1)S(1)}, bf16[272,128]{1,0:T(8,128)(2,1)S(1)}) custom-call(bf16[32,1024]{1,0:T(8,128)(2,1)S(1)} %collective-permute-done.2.refs_0_, bf16[32,1024]{1,0:T(8,128)(2,1)S(1)} %hold.2.refs_1_, bf16[1024,1024]{1,0:T(8,128)(2,1)S(1)} %get-tuple-element.16.after.refs_1_.refs_2_, ...), custom_call_target="tpu_custom_call" | custom-call | flops 536870912 | bytes 8388608 | tf_op jit(solution)/shard_map/attend/pallas_call | solution.py:185
  9.7 1.3 %collective-permute-start.5 = (bf16[272,128]{1,0:T(8,128)(2,1)S(1)}, bf16[272,128]{1,0:T(8,128)(2,1)S(1)}, u32[]{:S(2)}, u32[]{:S(2)}) collective-permute-start(bf16[272,128]{1,0:T(8,128)(2,1)S(1)} %get-tuple-element.24), channel_id=1, source_target_pairs={{0,8},{4,12},{8,0},{12,4},{1,9},{5,13},{9,1},{13,5},{2,10},{6,14},... | collective-permute-start | bytes 208904 | tf_op jit(solution)/shard_map/ppermute | solution.py:262
  11.0 0.3 %collective-permute-start.4 = (bf16[272,128]{1,0:T(8,128)(2,1)S(1)}, bf16[272,128]{1,0:T(8,128)(2,1)S(1)}, u32[]{:S(2)}, u32[]{:S(2)}) collective-permute-start(bf16[272,128]{1,0:T(8,128)(2,1)S(1)} %get-tuple-element.21.refs_8_), channel_id=1, source_target_pairs={{0,12},{4,8},{8,4},{12,0},{1,13},{5,9},{9,5},{13,1},{2,14},{6,10},... | collective-permute-start | bytes 208904 | tf_op jit(solution)/shard_map/ppermute | solution.py:262
  11.3 0.0 copy-done.1
  11.3 2.0 %attend.3 = (bf16[272,128]{1,0:T(8,128)(2,1)S(1)}, bf16[272,128]{1,0:T(8,128)(2,1)S(1)}) custom-call(bf16[32,1024]{1,0:T(8,128)(2,1)S(1)} %copy-done.1, bf16[32,1024]{1,0:T(8,128)(2,1)S(1)} %collective-permute-done.refs_2_.refs_1_, bf16[1024,1024]{1,0:T(8,128)(2,1)S(1)} %get-tuple-element.16.after.refs_1_.refs_2_, ...), custom_call_target="tpu_custom_call" | custom-call | flops 536870912 | bytes 8388608 | tf_op jit(solution)/shard_map/attend/pallas_call | solution.py:185
  13.3 0.6 %collective-permute-start.3 = (bf16[272,128]{1,0:T(8,128)(2,1)S(1)}, bf16[272,128]{1,0:T(8,128)(2,1)S(1)}, u32[]{:S(2)}, u32[]{:S(2)}) collective-permute-start(bf16[272,128]{1,0:T(8,128)(2,1)S(1)} %get-tuple-element.23), channel_id=1, source_target_pairs={{0,4},{4,0},{8,12},{12,8},{1,5},{5,1},{9,13},{13,9},{2,6},{6,2},{1... | collective-permute-start | bytes 208904 | tf_op jit(solution)/shard_map/ppermute | solution.py:262
  13.9 0.3 %collective-permute-done.5.refs_1_ = bf16[272,128]{1,0:T(8,128)(2,1)S(1)} collective-permute-done((bf16[272,128]{1,0:T(8,128)(2,1)S(1)}, bf16[272,128]{1,0:T(8,128)(2,1)S(1)}, u32[]{:S(2)}, u32[]{:S(2)}) %collective-permute-start.5) | collective-permute-done | bytes 69664 | tf_op jit(solution)/shard_map/ppermute | solution.py:262
  14.2 1.2 %collective-permute-done.4.refs_0_ = bf16[272,128]{1,0:T(8,128)(2,1)S(1)} collective-permute-done((bf16[272,128]{1,0:T(8,128)(2,1)S(1)}, bf16[272,128]{1,0:T(8,128)(2,1)S(1)}, u32[]{:S(2)}, u32[]{:S(2)}) %collective-permute-start.4) | collective-permute-done | bytes 69664 | tf_op jit(solution)/shard_map/ppermute | solution.py:262
  15.4 0.0 collective-permute-done.3.refs_1_
  15.4 0.9 %merge.1 = bf16[32,1024]{1,0:T(8,128)(2,1)} custom-call(bf16[272,128]{1,0:T(8,128)(2,1)S(1)} %get-tuple-element.22.refs_0_, bf16[272,128]{1,0:T(8,128)(2,1)S(1)} %collective-permute-done.3.refs_1_, bf16[272,128]{1,0:T(8,128)(2,1)S(1)} %get-tuple-element.25.refs_2_, bf16[272,128]{1,0:T(8,128)(2,1)S(1)} %get-tuple-element.26.refs_3_), custom_call_target="tpu_custom_call" | custom-call | tf_op jit(solution)/shard_map/merge/pallas_call | solution.py:247
  (2 shorter events, 0.0 us)
Async XLA Ops:
  0.0 6.0 %collective-permute-start = (bf16[32,1024]{1,0:T(8,128)(2,1)}, bf16[32,1024]{1,0:T(8,128)(2,1)S(1)}, u32[]{:S(2)}, u32[]{:S(2)}) collective-permute-start(bf16[32,1024]{1,0:T(8,128)(2,1)} %refs_0_.3), channel_id=1, source_target_pairs={{0,4},{4,0},{8,12},{12,8},{1,5},{5,1},{9,13},{13,9},{2,6},{6,2},{1... | collective-permute-start | bytes 196616 | tf_op jit(solution)/shard_map/ppermute | solution.py:262
  0.5 5.5 %collective-permute-start.1 = (bf16[32,1024]{1,0:T(8,128)(2,1)}, bf16[32,1024]{1,0:T(8,128)(2,1)S(1)}, u32[]{:S(2)}, u32[]{:S(2)}) collective-permute-start(bf16[32,1024]{1,0:T(8,128)(2,1)} %refs_0_.3), channel_id=1, source_target_pairs={{0,8},{4,12},{8,0},{12,4},{1,9},{5,13},{9,1},{13,5},{2,10},{6,14},... | collective-permute-start | bytes 196616 | tf_op jit(solution)/shard_map/ppermute | solution.py:262
  5.9 1.6 %copy-start = (bf16[1024,1024]{1,0:T(8,128)(2,1)S(1)}, bf16[1024,1024]{1,0:T(8,128)(2,1)}, u32[]{:S(2)}) copy-start(bf16[1024,1024]{1,0:T(8,128)(2,1)} %refs_5_.3) | copy-start | bytes 6291460
  5.9 1.6 %copy-start.2 = (f32[8]{0:T(128)S(1)}, f32[8]{0:T(128)}, u32[]{:S(2)}) copy-start(f32[8]{0:T(128)} %slopes.1) | copy-start | bytes 100
  6.0 1.6 %copy-start.3 = (s32[128]{0:T(128)S(1)}, s32[128]{0:T(128)}, u32[]{:S(2)}) copy-start(s32[128]{0:T(128)} %ids.1) | copy-start | bytes 1540
  6.0 1.7 %collective-permute-start.2 = (bf16[32,1024]{1,0:T(8,128)(2,1)S(1)}, bf16[32,1024]{1,0:T(8,128)(2,1)S(1)}, u32[]{:S(2)}, u32[]{:S(2)}) collective-permute-start(bf16[32,1024]{1,0:T(8,128)(2,1)S(1)} %hold.2.refs_1_), channel_id=1, source_target_pairs={{0,4},{4,0},{8,12},{12,8},{1,5},{5,1},{9,13},{13,9},{2,6},{6,2},{1... | collective-permute-start | bytes 196616 | tf_op jit(solution)/shard_map/ppermute | solution.py:262
  7.7 3.6 %copy-start.1 = (bf16[32,1024]{1,0:T(8,128)(2,1)S(1)}, bf16[32,1024]{1,0:T(8,128)(2,1)}, u32[]{:S(2)}) copy-start(bf16[32,1024]{1,0:T(8,128)(2,1)} %refs_0_.3) | copy-start | bytes 196612
  9.7 4.5 %collective-permute-start.5 = (bf16[272,128]{1,0:T(8,128)(2,1)S(1)}, bf16[272,128]{1,0:T(8,128)(2,1)S(1)}, u32[]{:S(2)}, u32[]{:S(2)}) collective-permute-start(bf16[272,128]{1,0:T(8,128)(2,1)S(1)} %get-tuple-element.24), channel_id=1, source_target_pairs={{0,8},{4,12},{8,0},{12,4},{1,9},{5,13},{9,1},{13,5},{2,10},{6,14},... | collective-permute-start | bytes 208904 | tf_op jit(solution)/shard_map/ppermute | solution.py:262
  11.0 4.4 %collective-permute-start.4 = (bf16[272,128]{1,0:T(8,128)(2,1)S(1)}, bf16[272,128]{1,0:T(8,128)(2,1)S(1)}, u32[]{:S(2)}, u32[]{:S(2)}) collective-permute-start(bf16[272,128]{1,0:T(8,128)(2,1)S(1)} %get-tuple-element.21.refs_8_), channel_id=1, source_target_pairs={{0,12},{4,8},{8,4},{12,0},{1,13},{5,9},{9,5},{13,1},{2,14},{6,10},... | collective-permute-start | bytes 208904 | tf_op jit(solution)/shard_map/ppermute | solution.py:262
  13.3 2.1 %collective-permute-start.3 = (bf16[272,128]{1,0:T(8,128)(2,1)S(1)}, bf16[272,128]{1,0:T(8,128)(2,1)S(1)}, u32[]{:S(2)}, u32[]{:S(2)}) collective-permute-start(bf16[272,128]{1,0:T(8,128)(2,1)S(1)} %get-tuple-element.23), channel_id=1, source_target_pairs={{0,4},{4,0},{8,12},{12,8},{1,5},{5,1},{9,13},{13,9},{2,6},{6,2},{1... | collective-permute-start | bytes 208904 | tf_op jit(solution)/shard_map/ppermute | solution.py:262

commit v6 on v5

--- a/solution.py
+++ b/solution.py
@@ -203,7 +203,7 @@
     pass
 
 
-def hold(arrays, after=()):
+def hold(arrays, after=(), spent=4 << 20):
     return pl.pallas_call(
         hold_kernel,
         out_shape=tuple(jax.ShapeDtypeStruct(array.shape, array.dtype) for array in arrays),
@@ -211,47 +211,77 @@
         out_specs=[ANY] * len(arrays),
         input_output_aliases={i: i for i in range(len(arrays))},
         compiler_params=pltpu.CompilerParams(vmem_limit_bytes=1 << 20),
-        cost_estimate=pl.CostEstimate(flops=0, bytes_accessed=4 << 20, transcendentals=0),
+        cost_estimate=pl.CostEstimate(flops=0, bytes_accessed=spent, transcendentals=0),
         name="hold",
     )(*arrays, *after)
 
 
-def merge_kernel(*refs):
-    out = refs[-1]
-    rows, width = out.shape
-    heads = (refs[0].shape[0] - 2 * SUBLANES) // rows
-    size = width // heads
-    lane = lax.rem(lax.broadcasted_iota(jnp.int32, (LANES, width), 0), period(rows))
-    head = lax.broadcasted_iota(jnp.int32, (LANES, width), 1) // size
-    spread = jnp.where((lax.rem(lane, heads) == head) & (lane < 3 * heads), 1.0, 0.0).astype(jnp.bfloat16)
+def spread_of(rows, heads, size):
+    lane = lax.rem(lax.broadcasted_iota(jnp.int32, (LANES, heads * size), 0), period(rows))
+    head = lax.broadcasted_iota(jnp.int32, (LANES, heads * size), 1) // size
+    return jnp.where((lax.rem(lane, heads) == head) & (lane < 3 * heads), 1.0, 0.0).astype(jnp.bfloat16)
+
+
+def opened(refs, rows, heads, spread):
     group = lax.broadcasted_iota(jnp.int32, (SUBLANES, LANES), 1) // period(rows)
     coded = []
-    for ref in refs[:-1]:
+    for ref in refs:
         packed = ref[heads * rows :, :].astype(jnp.float32)[:SUBLANES]
         coded += [jnp.where(group == g, packed, 0.0) for g in range(rows // SUBLANES)]
     coded = jnp.concatenate(coded, axis=0).astype(jnp.bfloat16)
     logs = jnp.dot(coded, spread, preferred_element_type=jnp.float32)
-    logs = [logs[j * rows : (j + 1) * rows] for j in range(len(refs) - 1)]
-    top = functools.reduce(jnp.maximum, logs)
-    total = jnp.zeros(out.shape, jnp.float32)
-    mixed = jnp.zeros(out.shape, jnp.float32)
-    for log, ref in zip(logs, refs[:-1]):
-        value = jnp.concatenate([ref[h * rows : (h + 1) * rows, :] for h in range(heads)], axis=1)
-        scale = jnp.exp2(log - top)
-        total += scale
-        mixed += scale * value.astype(jnp.float32)
-    out[...] = (mixed / total).astype(out.dtype)
-
-
-def merge(parts, rows, width):
+    values = [jnp.concatenate([ref[h * rows : (h + 1) * rows, :] for h in range(heads)], axis=1) for ref in refs]
+    return [(value.astype(jnp.float32), logs[j * rows : (j + 1) * rows]) for j, value in enumerate(values)]
+
+
+def gather_kernel(rows, heads, *refs):
+    *messages, mixed, total, top, spread = refs
+    spread[...] = spread_of(rows, heads, messages[0].shape[1])
+    parts = opened(messages, rows, heads, spread[...])
+    level = functools.reduce(jnp.maximum, [log for _, log in parts])
+    scales = [jnp.exp2(log - level) for _, log in parts]
+    top[...] = level
+    total[...] = functools.reduce(jnp.add, scales)
+    mixed[...] = functools.reduce(jnp.add, [scale * value for scale, (value, _) in zip(scales, parts)])
+
+
+def gather(parts, rows, width):
+    wide = jax.ShapeDtypeStruct((rows, width), jnp.float32)
+    heads = width // parts[0].shape[1]
+    return pl.pallas_call(
+        functools.partial(gather_kernel, rows, heads),
+        out_shape=(wide, wide, wide, jax.ShapeDtypeStruct((LANES, width), jnp.bfloat16)),
+        in_specs=[VMEM] * len(parts),
+        out_specs=(VMEM,) * 4,
+        compiler_params=pltpu.CompilerParams(vmem_limit_bytes=8 << 20),
+        cost_estimate=pl.CostEstimate(flops=0, bytes_accessed=1 << 20, transcendentals=0),
+        name="gather",
+    )(*parts)
+
+
+def merge_kernel(mixed, total, top, spread, *refs):
+    out = refs[-1]
+    rows, width = out.shape
+    parts = opened(refs[:-1], rows, width // refs[0].shape[1], spread[...])
+    level = functools.reduce(jnp.maximum, [log for _, log in parts], top[...])
+    scale = jnp.exp2(top[...] - level)
+    whole, sums = scale * mixed[...], scale * total[...]
+    for value, log in parts:
+        scale = jnp.exp2(log - level)
+        whole += scale * value
+        sums += scale
+    out[...] = (whole / sums).astype(out.dtype)
+
+
+def merge(gathered, last, rows, width):
     return pl.pallas_call(
         merge_kernel,
         out_shape=jax.ShapeDtypeStruct((rows, width), jnp.bfloat16),
-        in_specs=[VMEM] * len(parts),
+        in_specs=[VMEM] * (4 + len(last)),
         out_specs=VMEM,
         compiler_params=pltpu.CompilerParams(vmem_limit_bytes=8 << 20),
         name="merge",
-    )(*parts)
+    )(*gathered, *last)
 
 
 def shards(queries, root_keys, root_values, branch_keys, branch_values, branch_lengths, branch_ids, slopes):
@@ -272,9 +302,11 @@
     bias, mine = tables(slopes, branch_lengths, branch_ids, rows, root_keys.shape[0], root_kt, branch_values)
     caches = (root_kt, root_v, branch_kt, branch_values, bias, mine)
     sent = attend(far, [blocks[s] for s in far], caches, ())
-    got = hold([swap(array, shift) for array, shift in zip(sent, far)])
+    got = [swap(array, shift) for array, shift in zip(sent, far)]
     kept, passed = attend(near, [blocks[s] for s in near], caches, sent[:1])
-    return merge([kept, swap(passed, 1), *got], rows, width)
+    gathered = gather([kept, *hold(got[1:])], rows, width)
+    (last,) = hold(got[:1], gathered[:1])
+    return merge(gathered, [last, swap(passed, 1)], rows, width)
 
 
 def solution(mesh):

time: 16.5 us -> 16.5 us (level)
  waiting for transfers between devices: 1.52 us -> 1.3 us
  Pallas kernels: 7.92 us -> 8.09 us
    ppermute x6, waiting for transfers between devices: 1.52 us -> 1.3 us  [swap(): return lax.ppermute(array, 'seq', [(i, i ^ shift) for i in range(count)])]
    pallas_call x0 -> x1, Pallas kernels: none -> 0.21 us  [gather(): pl.pallas_call(functools.partial(gather_kernel, rows, heads), out_shape=(...]
  transfers between devices with their start and end apart: 6 -> 6, of which waited for: 2 -> 2; matrix products, arithmetic and copies ran while one was open for 0% -> 0% of each run, Pallas kernels for 31% -> 32%
where the time goes in v6:
time: 16.5 us; the launch traced here: 16.3 us
  Pallas kernels  8.09 us (49%)
  starting transfers between devices  5.53 us (34%)
  waiting for transfers between devices  1.3 us (8%)
  between operations  0.93 us (6%)
  local copies, waits for them, and re-layouts  0.45 us (3%)
    ppermute x6, starting transfers between devices, swap(): return lax.ppermute(array, 'seq', [(i, i ^ shift) for i in range(count)])  5.53 us
    pallas_call x2, Pallas kernels, attend(): pl.pallas_call(functools.partial(attend_kernel, tuple(shifts), len(after)...  3.91 us
    pallas_call x1, Pallas kernels, load(): pl.pallas_call(functools.partial(load_kernel, chunks, len(turned), len(st...  2.96 us
    ppermute x6, waiting for transfers between devices, swap(): return lax.ppermute(array, 'seq', [(i, i ^ shift) for i in range(count)])  1.3 us
    pallas_call x1, Pallas kernels, merge(): pl.pallas_call(merge_kernel, out_shape=jax.ShapeDtypeStruct((rows, width)...  0.9 us
    unnamed x8, local copies, waits for them, and re-layouts  0.45 us
  transfers between devices with their start and end apart: 6, of which 2 were waited for; matrix products, arithmetic and copies ran while one was open for 0% of the time, Pallas kernels for 32%

profile of v6, /device:TPU:0, one launch (start us, length us, event | category | flops | bytes accessed | tf_op | source)
XLA Modules:
  0.0 16.3 jit_solution(17499860211822727533)
XLA Ops:
  0.0 0.5 %collective-permute-start = (bf16[32,1024]{1,0:T(8,128)(2,1)}, bf16[32,1024]{1,0:T(8,128)(2,1)S(1)}, u32[]{:S(2)}, u32[]{:S(2)}) collective-permute-start(bf16[32,1024]{1,0:T(8,128)(2,1)} %refs_0_.3), channel_id=1, source_target_pairs={{0,4},{4,0},{8,12},{12,8},{1,5},{5,1},{9,13},{13,9},{2,6},{6,2},{1... | collective-permute-start | bytes 196616 | tf_op jit(solution)/shard_map/ppermute | solution.py:292
  0.5 2.5 %collective-permute-start.1 = (bf16[32,1024]{1,0:T(8,128)(2,1)}, bf16[32,1024]{1,0:T(8,128)(2,1)S(1)}, u32[]{:S(2)}, u32[]{:S(2)}) collective-permute-start(bf16[32,1024]{1,0:T(8,128)(2,1)} %refs_0_.3), channel_id=1, source_target_pairs={{0,8},{4,12},{8,0},{12,4},{1,9},{5,13},{9,1},{13,5},{2,10},{6,14},... | collective-permute-start | bytes 196616 | tf_op jit(solution)/shard_map/ppermute | solution.py:292
  3.0 3.0 %load.1 = (bf16[1024,1024]{1,0:T(8,128)(2,1)S(1)}, bf16[1024,1024]{1,0:T(8,128)(2,1)S(1)}, bf16[1024,1024]{1,0:T(8,128)(2,1)S(1)}) custom-call(bf16[1024,1024]{1,0:T(8,128)(2,1)} %refs_0_.2, bf16[1024,1024]{1,0:T(8,128)(2,1)} %refs_1_.1, bf16[1024,1024]{1,0:T(8,128)(2,1)} %refs_2_.1), custom_call_target="tpu_custom_call" | custom-call | bytes 6291456 | tf_op jit(solution)/shard_map/load/pallas_call | solution.py:51
  5.9 0.0 copy-start
  5.9 0.0 copy-start.2
  6.0 0.0 copy-start.3
  6.0 0.0 collective-permute-done.refs_2_.refs_1_
  6.0 0.0 collective-permute-done.1.refs_0_
  6.0 0.3 %collective-permute-start.2 = (bf16[32,1024]{1,0:T(8,128)(2,1)S(1)}, bf16[32,1024]{1,0:T(8,128)(2,1)S(1)}, u32[]{:S(2)}, u32[]{:S(2)}) collective-permute-start(bf16[32,1024]{1,0:T(8,128)(2,1)S(1)} %hold.3.refs_1_), channel_id=1, source_target_pairs={{0,4},{4,0},{8,12},{12,8},{1,5},{5,1},{9,13},{13,9},{2,6},{6,2},{1... | collective-permute-start | bytes 196616 | tf_op jit(solution)/shard_map/ppermute | solution.py:292
  7.1 0.4 %copy-done = bf16[1024,1024]{1,0:T(8,128)(2,1)S(1)} copy-done((bf16[1024,1024]{1,0:T(8,128)(2,1)S(1)}, bf16[1024,1024]{1,0:T(8,128)(2,1)}, u32[]{:S(2)}) %copy-start) | copy-done | bytes 2097176
  7.5 0.0 copy-done.2
  7.5 0.0 copy-done.3
  7.5 0.1 tables.1
  7.7 0.0 collective-permute-done.2.refs_0_
  7.7 0.0 copy-start.1
  7.7 2.0 %attend.2 = (bf16[272,128]{1,0:T(8,128)(2,1)S(1)}, bf16[272,128]{1,0:T(8,128)(2,1)S(1)}) custom-call(bf16[32,1024]{1,0:T(8,128)(2,1)S(1)} %collective-permute-done.2.refs_0_, bf16[32,1024]{1,0:T(8,128)(2,1)S(1)} %hold.3.refs_1_, bf16[1024,1024]{1,0:T(8,128)(2,1)S(1)} %get-tuple-element.18.after.refs_1_.refs_2_, ...), custom_call_target="tpu_custom_call" | custom-call | flops 536870912 | bytes 8388608 | tf_op jit(solution)/shard_map/attend/pallas_call | solution.py:185
  9.7 1.3 %collective-permute-start.3 = (bf16[272,128]{1,0:T(8,128)(2,1)S(1)}, bf16[272,128]{1,0:T(8,128)(2,1)S(1)}, u32[]{:S(2)}, u32[]{:S(2)}) collective-permute-start(bf16[272,128]{1,0:T(8,128)(2,1)S(1)} %get-tuple-element.25), channel_id=1, source_target_pairs={{0,8},{4,12},{8,0},{12,4},{1,9},{5,13},{9,1},{13,5},{2,10},{6,14},... | collective-permute-start | bytes 208904 | tf_op jit(solution)/shard_map/ppermute | solution.py:292
  11.0 0.3 %collective-permute-start.4 = (bf16[272,128]{1,0:T(8,128)(2,1)S(1)}, bf16[272,128]{1,0:T(8,128)(2,1)S(1)}, u32[]{:S(2)}, u32[]{:S(2)}) collective-permute-start(bf16[272,128]{1,0:T(8,128)(2,1)S(1)} %get-tuple-element.23.refs_8_), channel_id=1, source_target_pairs={{0,12},{4,8},{8,4},{12,0},{1,13},{5,9},{9,5},{13,1},{2,14},{6,10},... | collective-permute-start | bytes 208904 | tf_op jit(solution)/shard_map/ppermute | solution.py:292
  11.3 0.0 copy-done.1
  11.3 2.0 %attend.3 = (bf16[272,128]{1,0:T(8,128)(2,1)S(1)}, bf16[272,128]{1,0:T(8,128)(2,1)S(1)}) custom-call(bf16[32,1024]{1,0:T(8,128)(2,1)S(1)} %copy-done.1, bf16[32,1024]{1,0:T(8,128)(2,1)S(1)} %collective-permute-done.refs_2_.refs_1_, bf16[1024,1024]{1,0:T(8,128)(2,1)S(1)} %get-tuple-element.18.after.refs_1_.refs_2_, ...), custom_call_target="tpu_custom_call" | custom-call | flops 536870912 | bytes 8388608 | tf_op jit(solution)/shard_map/attend/pallas_call | solution.py:185
  13.3 0.6 %collective-permute-start.5 = (bf16[272,128]{1,0:T(8,128)(2,1)S(1)}, bf16[272,128]{1,0:T(8,128)(2,1)S(1)}, u32[]{:S(2)}, u32[]{:S(2)}) collective-permute-start(bf16[272,128]{1,0:T(8,128)(2,1)S(1)} %get-tuple-element.30), channel_id=1, source_target_pairs={{0,4},{4,0},{8,12},{12,8},{1,5},{5,1},{9,13},{13,9},{2,6},{6,2},{1... | collective-permute-start | bytes 208904 | tf_op jit(solution)/shard_map/ppermute | solution.py:292
  13.9 0.3 %collective-permute-done.3.refs_0_ = bf16[272,128]{1,0:T(8,128)(2,1)S(1)} collective-permute-done((bf16[272,128]{1,0:T(8,128)(2,1)S(1)}, bf16[272,128]{1,0:T(8,128)(2,1)S(1)}, u32[]{:S(2)}, u32[]{:S(2)}) %collective-permute-start.3) | collective-permute-done | bytes 69664 | tf_op jit(solution)/shard_map/ppermute | solution.py:292
  14.2 0.2 %gather.1 = (f32[32,1024]{1,0:T(8,128)S(1)}, f32[32,1024]{1,0:T(8,128)S(1)}, f32[32,1024]{1,0:T(8,128)S(1)}, bf16[128,1024]{1,0:T(8,128)(2,1)S(1)}) custom-call(bf16[272,128]{1,0:T(8,128)(2,1)S(1)} %get-tuple-element.24.refs_0_, bf16[272,128]{1,0:T(8,128)(2,1)S(1)} %hold.4.refs_1_), custom_call_target="tpu_custom_call" | custom-call | bytes 1048576 | tf_op jit(solution)/shard_map/gather/pallas_call | solution.py:251
  14.4 1.0 %collective-permute-done.4.refs_0_ = bf16[272,128]{1,0:T(8,128)(2,1)S(1)} collective-permute-done((bf16[272,128]{1,0:T(8,128)(2,1)S(1)}, bf16[272,128]{1,0:T(8,128)(2,1)S(1)}, u32[]{:S(2)}, u32[]{:S(2)}) %collective-permute-start.4) | collective-permute-done | bytes 69664 | tf_op jit(solution)/shard_map/ppermute | solution.py:292
  15.4 0.0 collective-permute-done.5.refs_1_
  15.4 0.9 %merge.1 = bf16[32,1024]{1,0:T(8,128)(2,1)} custom-call(f32[32,1024]{1,0:T(8,128)S(1)} %get-tuple-element.26.refs_1_.mixed, f32[32,1024]{1,0:T(8,128)S(1)} %get-tuple-element.27.total, f32[32,1024]{1,0:T(8,128)S(1)} %get-tuple-element.28.top, bf16[128,1024]{1,0:T(8,128)(2,1)S(1)} %get-tuple-element.29.spread, bf16[272,128]{1,0:T(8,128)(2,1)S(1)} %hold.5.refs_0_, ...), custom_call_target="tpu_custom_call" | custom-call | tf_op jit(solution)/shard_map/merge/pallas_call | solution.py:277
  (3 shorter events, 0.0 us)
Async XLA Ops:
  0.0 6.0 %collective-permute-start = (bf16[32,1024]{1,0:T(8,128)(2,1)}, bf16[32,1024]{1,0:T(8,128)(2,1)S(1)}, u32[]{:S(2)}, u32[]{:S(2)}) collective-permute-start(bf16[32,1024]{1,0:T(8,128)(2,1)} %refs_0_.3), channel_id=1, source_target_pairs={{0,4},{4,0},{8,12},{12,8},{1,5},{5,1},{9,13},{13,9},{2,6},{6,2},{1... | collective-permute-start | bytes 196616 | tf_op jit(solution)/shard_map/ppermute | solution.py:292
  0.5 5.5 %collective-permute-start.1 = (bf16[32,1024]{1,0:T(8,128)(2,1)}, bf16[32,1024]{1,0:T(8,128)(2,1)S(1)}, u32[]{:S(2)}, u32[]{:S(2)}) collective-permute-start(bf16[32,1024]{1,0:T(8,128)(2,1)} %refs_0_.3), channel_id=1, source_target_pairs={{0,8},{4,12},{8,0},{12,4},{1,9},{5,13},{9,1},{13,5},{2,10},{6,14},... | collective-permute-start | bytes 196616 | tf_op jit(solution)/shard_map/ppermute | solution.py:292
  5.9 1.6 %copy-start = (bf16[1024,1024]{1,0:T(8,128)(2,1)S(1)}, bf16[1024,1024]{1,0:T(8,128)(2,1)}, u32[]{:S(2)}) copy-start(bf16[1024,1024]{1,0:T(8,128)(2,1)} %refs_5_.3) | copy-start | bytes 6291460
  5.9 1.6 %copy-start.2 = (f32[8]{0:T(128)S(1)}, f32[8]{0:T(128)}, u32[]{:S(2)}) copy-start(f32[8]{0:T(128)} %slopes.1) | copy-start | bytes 100
  6.0 1.6 %copy-start.3 = (s32[128]{0:T(128)S(1)}, s32[128]{0:T(128)}, u32[]{:S(2)}) copy-start(s32[128]{0:T(128)} %ids.1) | copy-start | bytes 1540
  6.0 1.7 %collective-permute-start.2 = (bf16[32,1024]{1,0:T(8,128)(2,1)S(1)}, bf16[32,1024]{1,0:T(8,128)(2,1)S(1)}, u32[]{:S(2)}, u32[]{:S(2)}) collective-permute-start(bf16[32,1024]{1,0:T(8,128)(2,1)S(1)} %hold.3.refs_1_), channel_id=1, source_target_pairs={{0,4},{4,0},{8,12},{12,8},{1,5},{5,1},{9,13},{13,9},{2,6},{6,2},{1... | collective-permute-start | bytes 196616 | tf_op jit(solution)/shard_map/ppermute | solution.py:292
  7.7 3.6 %copy-start.1 = (bf16[32,1024]{1,0:T(8,128)(2,1)S(1)}, bf16[32,1024]{1,0:T(8,128)(2,1)}, u32[]{:S(2)}) copy-start(bf16[32,1024]{1,0:T(8,128)(2,1)} %refs_0_.3) | copy-start | bytes 196612
  9.7 4.5 %collective-permute-start.3 = (bf16[272,128]{1,0:T(8,128)(2,1)S(1)}, bf16[272,128]{1,0:T(8,128)(2,1)S(1)}, u32[]{:S(2)}, u32[]{:S(2)}) collective-permute-start(bf16[272,128]{1,0:T(8,128)(2,1)S(1)} %get-tuple-element.25), channel_id=1, source_target_pairs={{0,8},{4,12},{8,0},{12,4},{1,9},{5,13},{9,1},{13,5},{2,10},{6,14},... | collective-permute-start | bytes 208904 | tf_op jit(solution)/shard_map/ppermute | solution.py:292
  11.0 4.4 %collective-permute-start.4 = (bf16[272,128]{1,0:T(8,128)(2,1)S(1)}, bf16[272,128]{1,0:T(8,128)(2,1)S(1)}, u32[]{:S(2)}, u32[]{:S(2)}) collective-permute-start(bf16[272,128]{1,0:T(8,128)(2,1)S(1)} %get-tuple-element.23.refs_8_), channel_id=1, source_target_pairs={{0,12},{4,8},{8,4},{12,0},{1,13},{5,9},{9,5},{13,1},{2,14},{6,10},... | collective-permute-start | bytes 208904 | tf_op jit(solution)/shard_map/ppermute | solution.py:292
  13.3 2.1 %collective-permute-start.5 = (bf16[272,128]{1,0:T(8,128)(2,1)S(1)}, bf16[272,128]{1,0:T(8,128)(2,1)S(1)}, u32[]{:S(2)}, u32[]{:S(2)}) collective-permute-start(bf16[272,128]{1,0:T(8,128)(2,1)S(1)} %get-tuple-element.30), channel_id=1, source_target_pairs={{0,4},{4,0},{8,12},{12,8},{1,5},{5,1},{9,13},{13,9},{2,6},{6,2},{1... | collective-permute-start | bytes 208904 | tf_op jit(solution)/shard_map/ppermute | solution.py:292

commit v7 on v6

--- a/solution.py
+++ b/solution.py
@@ -31,11 +31,14 @@
             )
     for i in range(turned, turned + straight):
         copies.append(pltpu.make_async_copy(sources[i], outs[i], sems.at[turned * chunks + i - turned]))
-    for copy in copies:
+    for copy in copies[: turned * chunks]:
         copy.start()
     for i in range(turned):
         for j in range(chunks):
             copies[i * chunks + j].wait()
+            if i == j == 0:
+                for copy in copies[turned * chunks :]:
+                    copy.start()
             part = slice(j * rows, (j + 1) * rows)
             for col in range(0, width, LANES):
                 outs[i][col : col + LANES, part] = refs[-2][i, part, col : col + LANES].T

time: 16.5 us -> 16.4 us (level)
  waiting for transfers between devices: 1.3 us -> 1.06 us
  Pallas kernels: 8.09 us -> 8.31 us
    ppermute x6, waiting for transfers between devices: 1.3 us -> 1.06 us  [swap(): return lax.ppermute(array, 'seq', [(i, i ^ shift) for i in range(count)])]
    pallas_call x1, Pallas kernels: 2.96 us -> 3.17 us  [load(): pl.pallas_call(functools.partial(load_kernel, chunks, len(turned), len(st...]
  transfers between devices with their start and end apart: 6 -> 6, of which waited for: 2 -> 2; matrix products, arithmetic and copies ran while one was open for 0% -> 0% of each run, Pallas kernels for 32% -> 33%
where the time goes in v7:
time: 16.4 us; the launch traced here: 16.3 us
  Pallas kernels  8.31 us (51%)
  starting transfers between devices  5.53 us (34%)
  waiting for transfers between devices  1.06 us (6%)
  between operations  0.93 us (6%)
  local copies, waits for them, and re-layouts  0.45 us (3%)
    ppermute x6, starting transfers between devices, swap(): return lax.ppermute(array, 'seq', [(i, i ^ shift) for i in range(count)])  5.53 us
    pallas_call x2, Pallas kernels, attend(): pl.pallas_call(functools.partial(attend_kernel, tuple(shifts), len(after)...  3.91 us
    pallas_call x1, Pallas kernels, load(): pl.pallas_call(functools.partial(load_kernel, chunks, len(turned), len(st...  3.17 us
    ppermute x6, waiting for transfers between devices, swap(): return lax.ppermute(array, 'seq', [(i, i ^ shift) for i in range(count)])  1.06 us
    pallas_call x1, Pallas kernels, merge(): pl.pallas_call(merge_kernel, out_shape=jax.ShapeDtypeStruct((rows, width)...  0.9 us
    unnamed x8, local copies, waits for them, and re-layouts  0.45 us
  transfers between devices with their start and end apart: 6, of which 2 were waited for; matrix products, arithmetic and copies ran while one was open for 0% of the time, Pallas kernels for 33%

profile of v7, /device:TPU:0, one launch (start us, length us, event | category | flops | bytes accessed | tf_op | source)
XLA Modules:
  0.0 16.3 jit_solution(7285317756383604952)
XLA Ops:
  0.0 0.5 %collective-permute-start = (bf16[32,1024]{1,0:T(8,128)(2,1)}, bf16[32,1024]{1,0:T(8,128)(2,1)S(1)}, u32[]{:S(2)}, u32[]{:S(2)}) collective-permute-start(bf16[32,1024]{1,0:T(8,128)(2,1)} %refs_0_.3), channel_id=1, source_target_pairs={{0,4},{4,0},{8,12},{12,8},{1,5},{5,1},{9,13},{13,9},{2,6},{6,2},{1... | collective-permute-start | bytes 196616 | tf_op jit(solution)/shard_map/ppermute | solution.py:295
  0.5 2.5 %collective-permute-start.1 = (bf16[32,1024]{1,0:T(8,128)(2,1)}, bf16[32,1024]{1,0:T(8,128)(2,1)S(1)}, u32[]{:S(2)}, u32[]{:S(2)}) collective-permute-start(bf16[32,1024]{1,0:T(8,128)(2,1)} %refs_0_.3), channel_id=1, source_target_pairs={{0,8},{4,12},{8,0},{12,4},{1,9},{5,13},{9,1},{13,5},{2,10},{6,14},... | collective-permute-start | bytes 196616 | tf_op jit(solution)/shard_map/ppermute | solution.py:295
  3.0 3.2 %load.1 = (bf16[1024,1024]{1,0:T(8,128)(2,1)S(1)}, bf16[1024,1024]{1,0:T(8,128)(2,1)S(1)}, bf16[1024,1024]{1,0:T(8,128)(2,1)S(1)}) custom-call(bf16[1024,1024]{1,0:T(8,128)(2,1)} %refs_0_.2, bf16[1024,1024]{1,0:T(8,128)(2,1)} %refs_1_.1, bf16[1024,1024]{1,0:T(8,128)(2,1)} %refs_2_.1), custom_call_target="tpu_custom_call" | custom-call | bytes 6291456 | tf_op jit(solution)/shard_map/load/pallas_call | solution.py:54
  6.2 0.0 copy-start
  6.2 0.0 copy-start.2
  6.2 0.0 copy-start.3
  6.2 0.0 collective-permute-done.refs_2_.refs_1_
  6.2 0.0 collective-permute-done.1.refs_0_
  6.2 0.3 %collective-permute-start.2 = (bf16[32,1024]{1,0:T(8,128)(2,1)S(1)}, bf16[32,1024]{1,0:T(8,128)(2,1)S(1)}, u32[]{:S(2)}, u32[]{:S(2)}) collective-permute-start(bf16[32,1024]{1,0:T(8,128)(2,1)S(1)} %hold.3.refs_1_), channel_id=1, source_target_pairs={{0,4},{4,0},{8,12},{12,8},{1,5},{5,1},{9,13},{13,9},{2,6},{6,2},{1... | collective-permute-start | bytes 196616 | tf_op jit(solution)/shard_map/ppermute | solution.py:295
  7.3 0.4 %copy-done = bf16[1024,1024]{1,0:T(8,128)(2,1)S(1)} copy-done((bf16[1024,1024]{1,0:T(8,128)(2,1)S(1)}, bf16[1024,1024]{1,0:T(8,128)(2,1)}, u32[]{:S(2)}) %copy-start) | copy-done | bytes 2097176
  7.8 0.0 copy-done.2
  7.8 0.0 copy-done.3
  7.8 0.1 tables.1
  7.9 0.0 collective-permute-done.2.refs_0_
  7.9 0.0 copy-start.1
  7.9 2.0 %attend.2 = (bf16[272,128]{1,0:T(8,128)(2,1)S(1)}, bf16[272,128]{1,0:T(8,128)(2,1)S(1)}) custom-call(bf16[32,1024]{1,0:T(8,128)(2,1)S(1)} %collective-permute-done.2.refs_0_, bf16[32,1024]{1,0:T(8,128)(2,1)S(1)} %hold.3.refs_1_, bf16[1024,1024]{1,0:T(8,128)(2,1)S(1)} %get-tuple-element.18.after.refs_1_.refs_2_, ...), custom_call_target="tpu_custom_call" | custom-call | flops 536870912 | bytes 8388608 | tf_op jit(solution)/shard_map/attend/pallas_call | solution.py:188
  9.9 1.1 %collective-permute-start.3 = (bf16[272,128]{1,0:T(8,128)(2,1)S(1)}, bf16[272,128]{1,0:T(8,128)(2,1)S(1)}, u32[]{:S(2)}, u32[]{:S(2)}) collective-permute-start(bf16[272,128]{1,0:T(8,128)(2,1)S(1)} %get-tuple-element.25), channel_id=1, source_target_pairs={{0,8},{4,12},{8,0},{12,4},{1,9},{5,13},{9,1},{13,5},{2,10},{6,14},... | collective-permute-start | bytes 208904 | tf_op jit(solution)/shard_map/ppermute | solution.py:295
  11.0 0.5 %collective-permute-start.4 = (bf16[272,128]{1,0:T(8,128)(2,1)S(1)}, bf16[272,128]{1,0:T(8,128)(2,1)S(1)}, u32[]{:S(2)}, u32[]{:S(2)}) collective-permute-start(bf16[272,128]{1,0:T(8,128)(2,1)S(1)} %get-tuple-element.23.refs_8_), channel_id=1, source_target_pairs={{0,12},{4,8},{8,4},{12,0},{1,13},{5,9},{9,5},{13,1},{2,14},{6,10},... | collective-permute-start | bytes 208904 | tf_op jit(solution)/shard_map/ppermute | solution.py:295
  11.5 0.0 copy-done.1
  11.5 2.0 %attend.3 = (bf16[272,128]{1,0:T(8,128)(2,1)S(1)}, bf16[272,128]{1,0:T(8,128)(2,1)S(1)}) custom-call(bf16[32,1024]{1,0:T(8,128)(2,1)S(1)} %copy-done.1, bf16[32,1024]{1,0:T(8,128)(2,1)S(1)} %collective-permute-done.refs_2_.refs_1_, bf16[1024,1024]{1,0:T(8,128)(2,1)S(1)} %get-tuple-element.18.after.refs_1_.refs_2_, ...), custom_call_target="tpu_custom_call" | custom-call | flops 536870912 | bytes 8388608 | tf_op jit(solution)/shard_map/attend/pallas_call | solution.py:188
  13.5 0.6 %collective-permute-start.5 = (bf16[272,128]{1,0:T(8,128)(2,1)S(1)}, bf16[272,128]{1,0:T(8,128)(2,1)S(1)}, u32[]{:S(2)}, u32[]{:S(2)}) collective-permute-start(bf16[272,128]{1,0:T(8,128)(2,1)S(1)} %get-tuple-element.30), channel_id=1, source_target_pairs={{0,4},{4,0},{8,12},{12,8},{1,5},{5,1},{9,13},{13,9},{2,6},{6,2},{1... | collective-permute-start | bytes 208904 | tf_op jit(solution)/shard_map/ppermute | solution.py:295
  14.1 0.5 %collective-permute-done.3.refs_0_ = bf16[272,128]{1,0:T(8,128)(2,1)S(1)} collective-permute-done((bf16[272,128]{1,0:T(8,128)(2,1)S(1)}, bf16[272,128]{1,0:T(8,128)(2,1)S(1)}, u32[]{:S(2)}, u32[]{:S(2)}) %collective-permute-start.3) | collective-permute-done | bytes 69664 | tf_op jit(solution)/shard_map/ppermute | solution.py:295
  14.6 0.2 %gather.1 = (f32[32,1024]{1,0:T(8,128)S(1)}, f32[32,1024]{1,0:T(8,128)S(1)}, f32[32,1024]{1,0:T(8,128)S(1)}, bf16[128,1024]{1,0:T(8,128)(2,1)S(1)}) custom-call(bf16[272,128]{1,0:T(8,128)(2,1)S(1)} %get-tuple-element.24.refs_0_, bf16[272,128]{1,0:T(8,128)(2,1)S(1)} %hold.4.refs_1_), custom_call_target="tpu_custom_call" | custom-call | bytes 1048576 | tf_op jit(solution)/shard_map/gather/pallas_call | solution.py:254
  14.8 0.5 %collective-permute-done.4.refs_0_ = bf16[272,128]{1,0:T(8,128)(2,1)S(1)} collective-permute-done((bf16[272,128]{1,0:T(8,128)(2,1)S(1)}, bf16[272,128]{1,0:T(8,128)(2,1)S(1)}, u32[]{:S(2)}, u32[]{:S(2)}) %collective-permute-start.4) | collective-permute-done | bytes 69664 | tf_op jit(solution)/shard_map/ppermute | solution.py:295
  15.4 0.0 collective-permute-done.5.refs_1_
  15.4 0.9 %merge.1 = bf16[32,1024]{1,0:T(8,128)(2,1)} custom-call(f32[32,1024]{1,0:T(8,128)S(1)} %get-tuple-element.26.refs_1_.mixed, f32[32,1024]{1,0:T(8,128)S(1)} %get-tuple-element.27.total, f32[32,1024]{1,0:T(8,128)S(1)} %get-tuple-element.28.top, bf16[128,1024]{1,0:T(8,128)(2,1)S(1)} %get-tuple-element.29.spread, bf16[272,128]{1,0:T(8,128)(2,1)S(1)} %hold.5.refs_0_, ...), custom_call_target="tpu_custom_call" | custom-call | tf_op jit(solution)/shard_map/merge/pallas_call | solution.py:280
  (3 shorter events, 0.0 us)
Async XLA Ops:
  0.0 6.2 %collective-permute-start = (bf16[32,1024]{1,0:T(8,128)(2,1)}, bf16[32,1024]{1,0:T(8,128)(2,1)S(1)}, u32[]{:S(2)}, u32[]{:S(2)}) collective-permute-start(bf16[32,1024]{1,0:T(8,128)(2,1)} %refs_0_.3), channel_id=1, source_target_pairs={{0,4},{4,0},{8,12},{12,8},{1,5},{5,1},{9,13},{13,9},{2,6},{6,2},{1... | collective-permute-start | bytes 196616 | tf_op jit(solution)/shard_map/ppermute | solution.py:295
  0.5 5.7 %collective-permute-start.1 = (bf16[32,1024]{1,0:T(8,128)(2,1)}, bf16[32,1024]{1,0:T(8,128)(2,1)S(1)}, u32[]{:S(2)}, u32[]{:S(2)}) collective-permute-start(bf16[32,1024]{1,0:T(8,128)(2,1)} %refs_0_.3), channel_id=1, source_target_pairs={{0,8},{4,12},{8,0},{12,4},{1,9},{5,13},{9,1},{13,5},{2,10},{6,14},... | collective-permute-start | bytes 196616 | tf_op jit(solution)/shard_map/ppermute | solution.py:295
  6.2 1.6 %copy-start = (bf16[1024,1024]{1,0:T(8,128)(2,1)S(1)}, bf16[1024,1024]{1,0:T(8,128)(2,1)}, u32[]{:S(2)}) copy-start(bf16[1024,1024]{1,0:T(8,128)(2,1)} %refs_5_.3) | copy-start | bytes 6291460
  6.2 1.6 %copy-start.2 = (f32[8]{0:T(128)S(1)}, f32[8]{0:T(128)}, u32[]{:S(2)}) copy-start(f32[8]{0:T(128)} %slopes.1) | copy-start | bytes 100
  6.2 1.6 %copy-start.3 = (s32[128]{0:T(128)S(1)}, s32[128]{0:T(128)}, u32[]{:S(2)}) copy-start(s32[128]{0:T(128)} %ids.1) | copy-start | bytes 1540
  6.2 1.7 %collective-permute-start.2 = (bf16[32,1024]{1,0:T(8,128)(2,1)S(1)}, bf16[32,1024]{1,0:T(8,128)(2,1)S(1)}, u32[]{:S(2)}, u32[]{:S(2)}) collective-permute-start(bf16[32,1024]{1,0:T(8,128)(2,1)S(1)} %hold.3.refs_1_), channel_id=1, source_target_pairs={{0,4},{4,0},{8,12},{12,8},{1,5},{5,1},{9,13},{13,9},{2,6},{6,2},{1... | collective-permute-start | bytes 196616 | tf_op jit(solution)/shard_map/ppermute | solution.py:295
  7.9 3.6 %copy-start.1 = (bf16[32,1024]{1,0:T(8,128)(2,1)S(1)}, bf16[32,1024]{1,0:T(8,128)(2,1)}, u32[]{:S(2)}) copy-start(bf16[32,1024]{1,0:T(8,128)(2,1)} %refs_0_.3) | copy-start | bytes 196612
  9.9 4.7 %collective-permute-start.3 = (bf16[272,128]{1,0:T(8,128)(2,1)S(1)}, bf16[272,128]{1,0:T(8,128)(2,1)S(1)}, u32[]{:S(2)}, u32[]{:S(2)}) collective-permute-start(bf16[272,128]{1,0:T(8,128)(2,1)S(1)} %get-tuple-element.25), channel_id=1, source_target_pairs={{0,8},{4,12},{8,0},{12,4},{1,9},{5,13},{9,1},{13,5},{2,10},{6,14},... | collective-permute-start | bytes 208904 | tf_op jit(solution)/shard_map/ppermute | solution.py:295
  11.0 4.4 %collective-permute-start.4 = (bf16[272,128]{1,0:T(8,128)(2,1)S(1)}, bf16[272,128]{1,0:T(8,128)(2,1)S(1)}, u32[]{:S(2)}, u32[]{:S(2)}) collective-permute-start(bf16[272,128]{1,0:T(8,128)(2,1)S(1)} %get-tuple-element.23.refs_8_), channel_id=1, source_target_pairs={{0,12},{4,8},{8,4},{12,0},{1,13},{5,9},{9,5},{13,1},{2,14},{6,10},... | collective-permute-start | bytes 208904 | tf_op jit(solution)/shard_map/ppermute | solution.py:295
  13.5 1.9 %collective-permute-start.5 = (bf16[272,128]{1,0:T(8,128)(2,1)S(1)}, bf16[272,128]{1,0:T(8,128)(2,1)S(1)}, u32[]{:S(2)}, u32[]{:S(2)}) collective-permute-start(bf16[272,128]{1,0:T(8,128)(2,1)S(1)} %get-tuple-element.30), channel_id=1, source_target_pairs={{0,4},{4,0},{8,12},{12,8},{1,5},{5,1},{9,13},{13,9},{2,6},{6,2},{1... | collective-permute-start | bytes 208904 | tf_op jit(solution)/shard_map/ppermute | solution.py:295

commit v8 on v7

--- a/solution.py
+++ b/solution.py
@@ -47,7 +47,7 @@
 
 
 def load(turned, straight, after, limit):
-    chunks = 4
+    chunks = 8
     arrays = (*turned, *straight)
     keys, width = arrays[0].shape
     kind = arrays[0].dtype

time: 16.4 us -> 16.4 us (level)
  transfers between devices with their start and end apart: 6 -> 6, of which waited for: 2 -> 2; matrix products, arithmetic and copies ran while one was open for 0% -> 0% of each run, Pallas kernels for 33% -> 34%
where the time goes in v8:
time: 16.4 us; the launch traced here: 16.3 us
  Pallas kernels  8.4 us (51%)
  starting transfers between devices  5.53 us (34%)
  waiting for transfers between devices  0.96 us (6%)
  between operations  0.93 us (6%)
  local copies, waits for them, and re-layouts  0.45 us (3%)
    ppermute x6, starting transfers between devices, swap(): return lax.ppermute(array, 'seq', [(i, i ^ shift) for i in range(count)])  5.53 us
    pallas_call x2, Pallas kernels, attend(): pl.pallas_call(functools.partial(attend_kernel, tuple(shifts), len(after)...  3.91 us
    pallas_call x1, Pallas kernels, load(): pl.pallas_call(functools.partial(load_kernel, chunks, len(turned), len(st...  3.26 us
    ppermute x6, waiting for transfers between devices, swap(): return lax.ppermute(array, 'seq', [(i, i ^ shift) for i in range(count)])  0.96 us
    pallas_call x1, Pallas kernels, merge(): pl.pallas_call(merge_kernel, out_shape=jax.ShapeDtypeStruct((rows, width)...  0.9 us
    unnamed x8, local copies, waits for them, and re-layouts  0.45 us
  transfers between devices with their start and end apart: 6, of which 2 were waited for; matrix products, arithmetic and copies ran while one was open for 0% of the time, Pallas kernels for 34%

profile of v8, /device:TPU:0, one launch (start us, length us, event | category | flops | bytes accessed | tf_op | source)
XLA Modules:
  0.0 16.3 jit_solution(9793408568431318143)
XLA Ops:
  0.0 0.5 %collective-permute-start = (bf16[32,1024]{1,0:T(8,128)(2,1)}, bf16[32,1024]{1,0:T(8,128)(2,1)S(1)}, u32[]{:S(2)}, u32[]{:S(2)}) collective-permute-start(bf16[32,1024]{1,0:T(8,128)(2,1)} %refs_0_.3), channel_id=1, source_target_pairs={{0,4},{4,0},{8,12},{12,8},{1,5},{5,1},{9,13},{13,9},{2,6},{6,2},{1... | collective-permute-start | bytes 196616 | tf_op jit(solution)/shard_map/ppermute | solution.py:295
  0.5 2.5 %collective-permute-start.1 = (bf16[32,1024]{1,0:T(8,128)(2,1)}, bf16[32,1024]{1,0:T(8,128)(2,1)S(1)}, u32[]{:S(2)}, u32[]{:S(2)}) collective-permute-start(bf16[32,1024]{1,0:T(8,128)(2,1)} %refs_0_.3), channel_id=1, source_target_pairs={{0,8},{4,12},{8,0},{12,4},{1,9},{5,13},{9,1},{13,5},{2,10},{6,14},... | collective-permute-start | bytes 196616 | tf_op jit(solution)/shard_map/ppermute | solution.py:295
  3.0 3.3 %load.1 = (bf16[1024,1024]{1,0:T(8,128)(2,1)S(1)}, bf16[1024,1024]{1,0:T(8,128)(2,1)S(1)}, bf16[1024,1024]{1,0:T(8,128)(2,1)S(1)}) custom-call(bf16[1024,1024]{1,0:T(8,128)(2,1)} %refs_0_.2, bf16[1024,1024]{1,0:T(8,128)(2,1)} %refs_1_.1, bf16[1024,1024]{1,0:T(8,128)(2,1)} %refs_2_.1), custom_call_target="tpu_custom_call" | custom-call | bytes 6291456 | tf_op jit(solution)/shard_map/load/pallas_call | solution.py:54
  6.2 0.0 copy-start
  6.3 0.0 copy-start.2
  6.3 0.0 copy-start.3
  6.3 0.0 collective-permute-done.refs_2_.refs_1_
  6.3 0.0 collective-permute-done.1.refs_0_
  6.3 0.3 %collective-permute-start.2 = (bf16[32,1024]{1,0:T(8,128)(2,1)S(1)}, bf16[32,1024]{1,0:T(8,128)(2,1)S(1)}, u32[]{:S(2)}, u32[]{:S(2)}) collective-permute-start(bf16[32,1024]{1,0:T(8,128)(2,1)S(1)} %hold.3.refs_1_), channel_id=1, source_target_pairs={{0,4},{4,0},{8,12},{12,8},{1,5},{5,1},{9,13},{13,9},{2,6},{6,2},{1... | collective-permute-start | bytes 196616 | tf_op jit(solution)/shard_map/ppermute | solution.py:295
  7.4 0.4 %copy-done = bf16[1024,1024]{1,0:T(8,128)(2,1)S(1)} copy-done((bf16[1024,1024]{1,0:T(8,128)(2,1)S(1)}, bf16[1024,1024]{1,0:T(8,128)(2,1)}, u32[]{:S(2)}) %copy-start) | copy-done | bytes 2097176
  7.9 0.0 copy-done.2
  7.9 0.0 copy-done.3
  7.9 0.1 tables.1
  8.0 0.0 collective-permute-done.2.refs_0_
  8.0 0.0 copy-start.1
  8.0 2.0 %attend.2 = (bf16[272,128]{1,0:T(8,128)(2,1)S(1)}, bf16[272,128]{1,0:T(8,128)(2,1)S(1)}) custom-call(bf16[32,1024]{1,0:T(8,128)(2,1)S(1)} %collective-permute-done.2.refs_0_, bf16[32,1024]{1,0:T(8,128)(2,1)S(1)} %hold.3.refs_1_, bf16[1024,1024]{1,0:T(8,128)(2,1)S(1)} %get-tuple-element.18.after.refs_1_.refs_2_, ...), custom_call_target="tpu_custom_call" | custom-call | flops 536870912 | bytes 8388608 | tf_op jit(solution)/shard_map/attend/pallas_call | solution.py:188
  10.0 1.0 %collective-permute-start.3 = (bf16[272,128]{1,0:T(8,128)(2,1)S(1)}, bf16[272,128]{1,0:T(8,128)(2,1)S(1)}, u32[]{:S(2)}, u32[]{:S(2)}) collective-permute-start(bf16[272,128]{1,0:T(8,128)(2,1)S(1)} %get-tuple-element.25), channel_id=1, source_target_pairs={{0,8},{4,12},{8,0},{12,4},{1,9},{5,13},{9,1},{13,5},{2,10},{6,14},... | collective-permute-start | bytes 208904 | tf_op jit(solution)/shard_map/ppermute | solution.py:295
  11.0 0.6 %collective-permute-start.4 = (bf16[272,128]{1,0:T(8,128)(2,1)S(1)}, bf16[272,128]{1,0:T(8,128)(2,1)S(1)}, u32[]{:S(2)}, u32[]{:S(2)}) collective-permute-start(bf16[272,128]{1,0:T(8,128)(2,1)S(1)} %get-tuple-element.23.refs_8_), channel_id=1, source_target_pairs={{0,12},{4,8},{8,4},{12,0},{1,13},{5,9},{9,5},{13,1},{2,14},{6,10},... | collective-permute-start | bytes 208904 | tf_op jit(solution)/shard_map/ppermute | solution.py:295
  11.6 0.0 copy-done.1
  11.6 2.0 %attend.3 = (bf16[272,128]{1,0:T(8,128)(2,1)S(1)}, bf16[272,128]{1,0:T(8,128)(2,1)S(1)}) custom-call(bf16[32,1024]{1,0:T(8,128)(2,1)S(1)} %copy-done.1, bf16[32,1024]{1,0:T(8,128)(2,1)S(1)} %collective-permute-done.refs_2_.refs_1_, bf16[1024,1024]{1,0:T(8,128)(2,1)S(1)} %get-tuple-element.18.after.refs_1_.refs_2_, ...), custom_call_target="tpu_custom_call" | custom-call | flops 536870912 | bytes 8388608 | tf_op jit(solution)/shard_map/attend/pallas_call | solution.py:188
  13.6 0.6 %collective-permute-start.5 = (bf16[272,128]{1,0:T(8,128)(2,1)S(1)}, bf16[272,128]{1,0:T(8,128)(2,1)S(1)}, u32[]{:S(2)}, u32[]{:S(2)}) collective-permute-start(bf16[272,128]{1,0:T(8,128)(2,1)S(1)} %get-tuple-element.30), channel_id=1, source_target_pairs={{0,4},{4,0},{8,12},{12,8},{1,5},{5,1},{9,13},{13,9},{2,6},{6,2},{1... | collective-permute-start | bytes 208904 | tf_op jit(solution)/shard_map/ppermute | solution.py:295
  14.2 0.6 %collective-permute-done.3.refs_0_ = bf16[272,128]{1,0:T(8,128)(2,1)S(1)} collective-permute-done((bf16[272,128]{1,0:T(8,128)(2,1)S(1)}, bf16[272,128]{1,0:T(8,128)(2,1)S(1)}, u32[]{:S(2)}, u32[]{:S(2)}) %collective-permute-start.3) | collective-permute-done | bytes 69664 | tf_op jit(solution)/shard_map/ppermute | solution.py:295
  14.8 0.2 %gather.1 = (f32[32,1024]{1,0:T(8,128)S(1)}, f32[32,1024]{1,0:T(8,128)S(1)}, f32[32,1024]{1,0:T(8,128)S(1)}, bf16[128,1024]{1,0:T(8,128)(2,1)S(1)}) custom-call(bf16[272,128]{1,0:T(8,128)(2,1)S(1)} %get-tuple-element.24.refs_0_, bf16[272,128]{1,0:T(8,128)(2,1)S(1)} %hold.4.refs_1_), custom_call_target="tpu_custom_call" | custom-call | bytes 1048576 | tf_op jit(solution)/shard_map/gather/pallas_call | solution.py:254
  15.0 0.3 %collective-permute-done.4.refs_0_ = bf16[272,128]{1,0:T(8,128)(2,1)S(1)} collective-permute-done((bf16[272,128]{1,0:T(8,128)(2,1)S(1)}, bf16[272,128]{1,0:T(8,128)(2,1)S(1)}, u32[]{:S(2)}, u32[]{:S(2)}) %collective-permute-start.4) | collective-permute-done | bytes 69664 | tf_op jit(solution)/shard_map/ppermute | solution.py:295
  15.4 0.0 collective-permute-done.5.refs_1_
  15.4 0.9 %merge.1 = bf16[32,1024]{1,0:T(8,128)(2,1)} custom-call(f32[32,1024]{1,0:T(8,128)S(1)} %get-tuple-element.26.refs_1_.mixed, f32[32,1024]{1,0:T(8,128)S(1)} %get-tuple-element.27.total, f32[32,1024]{1,0:T(8,128)S(1)} %get-tuple-element.28.top, bf16[128,1024]{1,0:T(8,128)(2,1)S(1)} %get-tuple-element.29.spread, bf16[272,128]{1,0:T(8,128)(2,1)S(1)} %hold.5.refs_0_, ...), custom_call_target="tpu_custom_call" | custom-call | tf_op jit(solution)/shard_map/merge/pallas_call | solution.py:280
  (3 shorter events, 0.0 us)
Async XLA Ops:
  0.0 6.3 %collective-permute-start = (bf16[32,1024]{1,0:T(8,128)(2,1)}, bf16[32,1024]{1,0:T(8,128)(2,1)S(1)}, u32[]{:S(2)}, u32[]{:S(2)}) collective-permute-start(bf16[32,1024]{1,0:T(8,128)(2,1)} %refs_0_.3), channel_id=1, source_target_pairs={{0,4},{4,0},{8,12},{12,8},{1,5},{5,1},{9,13},{13,9},{2,6},{6,2},{1... | collective-permute-start | bytes 196616 | tf_op jit(solution)/shard_map/ppermute | solution.py:295
  0.5 5.8 %collective-permute-start.1 = (bf16[32,1024]{1,0:T(8,128)(2,1)}, bf16[32,1024]{1,0:T(8,128)(2,1)S(1)}, u32[]{:S(2)}, u32[]{:S(2)}) collective-permute-start(bf16[32,1024]{1,0:T(8,128)(2,1)} %refs_0_.3), channel_id=1, source_target_pairs={{0,8},{4,12},{8,0},{12,4},{1,9},{5,13},{9,1},{13,5},{2,10},{6,14},... | collective-permute-start | bytes 196616 | tf_op jit(solution)/shard_map/ppermute | solution.py:295
  6.2 1.6 %copy-start = (bf16[1024,1024]{1,0:T(8,128)(2,1)S(1)}, bf16[1024,1024]{1,0:T(8,128)(2,1)}, u32[]{:S(2)}) copy-start(bf16[1024,1024]{1,0:T(8,128)(2,1)} %refs_5_.3) | copy-start | bytes 6291460
  6.3 1.6 %copy-start.2 = (f32[8]{0:T(128)S(1)}, f32[8]{0:T(128)}, u32[]{:S(2)}) copy-start(f32[8]{0:T(128)} %slopes.1) | copy-start | bytes 100
  6.3 1.6 %copy-start.3 = (s32[128]{0:T(128)S(1)}, s32[128]{0:T(128)}, u32[]{:S(2)}) copy-start(s32[128]{0:T(128)} %ids.1) | copy-start | bytes 1540
  6.3 1.7 %collective-permute-start.2 = (bf16[32,1024]{1,0:T(8,128)(2,1)S(1)}, bf16[32,1024]{1,0:T(8,128)(2,1)S(1)}, u32[]{:S(2)}, u32[]{:S(2)}) collective-permute-start(bf16[32,1024]{1,0:T(8,128)(2,1)S(1)} %hold.3.refs_1_), channel_id=1, source_target_pairs={{0,4},{4,0},{8,12},{12,8},{1,5},{5,1},{9,13},{13,9},{2,6},{6,2},{1... | collective-permute-start | bytes 196616 | tf_op jit(solution)/shard_map/ppermute | solution.py:295
  8.0 3.6 %copy-start.1 = (bf16[32,1024]{1,0:T(8,128)(2,1)S(1)}, bf16[32,1024]{1,0:T(8,128)(2,1)}, u32[]{:S(2)}) copy-start(bf16[32,1024]{1,0:T(8,128)(2,1)} %refs_0_.3) | copy-start | bytes 196612
  10.0 4.8 %collective-permute-start.3 = (bf16[272,128]{1,0:T(8,128)(2,1)S(1)}, bf16[272,128]{1,0:T(8,128)(2,1)S(1)}, u32[]{:S(2)}, u32[]{:S(2)}) collective-permute-start(bf16[272,128]{1,0:T(8,128)(2,1)S(1)} %get-tuple-element.25), channel_id=1, source_target_pairs={{0,8},{4,12},{8,0},{12,4},{1,9},{5,13},{9,1},{13,5},{2,10},{6,14},... | collective-permute-start | bytes 208904 | tf_op jit(solution)/shard_map/ppermute | solution.py:295
  11.0 4.4 %collective-permute-start.4 = (bf16[272,128]{1,0:T(8,128)(2,1)S(1)}, bf16[272,128]{1,0:T(8,128)(2,1)S(1)}, u32[]{:S(2)}, u32[]{:S(2)}) collective-permute-start(bf16[272,128]{1,0:T(8,128)(2,1)S(1)} %get-tuple-element.23.refs_8_), channel_id=1, source_target_pairs={{0,12},{4,8},{8,4},{12,0},{1,13},{5,9},{9,5},{13,1},{2,14},{6,10},... | collective-permute-start | bytes 208904 | tf_op jit(solution)/shard_map/ppermute | solution.py:295
  13.6 1.8 %collective-permute-start.5 = (bf16[272,128]{1,0:T(8,128)(2,1)S(1)}, bf16[272,128]{1,0:T(8,128)(2,1)S(1)}, u32[]{:S(2)}, u32[]{:S(2)}) collective-permute-start(bf16[272,128]{1,0:T(8,128)(2,1)S(1)} %get-tuple-element.30), channel_id=1, source_target_pairs={{0,4},{4,0},{8,12},{12,8},{1,5},{5,1},{9,13},{13,9},{2,6},{6,2},{1... | collective-permute-start | bytes 208904 | tf_op jit(solution)/shard_map/ppermute | solution.py:295

commit v9 on v8

--- a/solution.py
+++ b/solution.py
@@ -47,7 +47,7 @@
 
 
 def load(turned, straight, after, limit):
-    chunks = 8
+    chunks = 2
     arrays = (*turned, *straight)
     keys, width = arrays[0].shape
     kind = arrays[0].dtype

time: 16.4 us -> 16.4 us (level)
  transfers between devices with their start and end apart: 6 -> 6, of which waited for: 2 -> 2; matrix products, arithmetic and copies ran while one was open for 0% -> 0% of each run, Pallas kernels for 34% -> 33%
where the time goes in v9:
time: 16.4 us; the launch traced here: 16.3 us
  Pallas kernels  8.26 us (50%)
  starting transfers between devices  5.53 us (34%)
  waiting for transfers between devices  1.11 us (7%)
  between operations  0.93 us (6%)
  local copies, waits for them, and re-layouts  0.45 us (3%)
    ppermute x6, starting transfers between devices, swap(): return lax.ppermute(array, 'seq', [(i, i ^ shift) for i in range(count)])  5.53 us
    pallas_call x2, Pallas kernels, attend(): pl.pallas_call(functools.partial(attend_kernel, tuple(shifts), len(after)...  3.91 us
    pallas_call x1, Pallas kernels, load(): pl.pallas_call(functools.partial(load_kernel, chunks, len(turned), len(st...  3.13 us
    ppermute x6, waiting for transfers between devices, swap(): return lax.ppermute(array, 'seq', [(i, i ^ shift) for i in range(count)])  1.11 us
    pallas_call x1, Pallas kernels, merge(): pl.pallas_call(merge_kernel, out_shape=jax.ShapeDtypeStruct((rows, width)...  0.9 us
    unnamed x8, local copies, waits for them, and re-layouts  0.45 us
  transfers between devices with their start and end apart: 6, of which 2 were waited for; matrix products, arithmetic and copies ran while one was open for 0% of the time, Pallas kernels for 33%

profile of v9, /device:TPU:0, one launch (start us, length us, event | category | flops | bytes accessed | tf_op | source)
XLA Modules:
  0.0 16.3 jit_solution(5085911210378321367)
XLA Ops:
  0.0 0.5 %collective-permute-start = (bf16[32,1024]{1,0:T(8,128)(2,1)}, bf16[32,1024]{1,0:T(8,128)(2,1)S(1)}, u32[]{:S(2)}, u32[]{:S(2)}) collective-permute-start(bf16[32,1024]{1,0:T(8,128)(2,1)} %refs_0_.3), channel_id=1, source_target_pairs={{0,4},{4,0},{8,12},{12,8},{1,5},{5,1},{9,13},{13,9},{2,6},{6,2},{1... | collective-permute-start | bytes 196616 | tf_op jit(solution)/shard_map/ppermute | solution.py:295
  0.5 2.5 %collective-permute-start.1 = (bf16[32,1024]{1,0:T(8,128)(2,1)}, bf16[32,1024]{1,0:T(8,128)(2,1)S(1)}, u32[]{:S(2)}, u32[]{:S(2)}) collective-permute-start(bf16[32,1024]{1,0:T(8,128)(2,1)} %refs_0_.3), channel_id=1, source_target_pairs={{0,8},{4,12},{8,0},{12,4},{1,9},{5,13},{9,1},{13,5},{2,10},{6,14},... | collective-permute-start | bytes 196616 | tf_op jit(solution)/shard_map/ppermute | solution.py:295
  3.0 3.1 %load.1 = (bf16[1024,1024]{1,0:T(8,128)(2,1)S(1)}, bf16[1024,1024]{1,0:T(8,128)(2,1)S(1)}, bf16[1024,1024]{1,0:T(8,128)(2,1)S(1)}) custom-call(bf16[1024,1024]{1,0:T(8,128)(2,1)} %refs_0_.2, bf16[1024,1024]{1,0:T(8,128)(2,1)} %refs_1_.1, bf16[1024,1024]{1,0:T(8,128)(2,1)} %refs_2_.1), custom_call_target="tpu_custom_call" | custom-call | bytes 6291456 | tf_op jit(solution)/shard_map/load/pallas_call | solution.py:54
  6.1 0.0 copy-start
  6.1 0.0 copy-start.2
  6.1 0.0 copy-start.3
  6.1 0.0 collective-permute-done.refs_2_.refs_1_
  6.2 0.0 collective-permute-done.1.refs_0_
  6.2 0.3 %collective-permute-start.2 = (bf16[32,1024]{1,0:T(8,128)(2,1)S(1)}, bf16[32,1024]{1,0:T(8,128)(2,1)S(1)}, u32[]{:S(2)}, u32[]{:S(2)}) collective-permute-start(bf16[32,1024]{1,0:T(8,128)(2,1)S(1)} %hold.3.refs_1_), channel_id=1, source_target_pairs={{0,4},{4,0},{8,12},{12,8},{1,5},{5,1},{9,13},{13,9},{2,6},{6,2},{1... | collective-permute-start | bytes 196616 | tf_op jit(solution)/shard_map/ppermute | solution.py:295
  7.3 0.4 %copy-done = bf16[1024,1024]{1,0:T(8,128)(2,1)S(1)} copy-done((bf16[1024,1024]{1,0:T(8,128)(2,1)S(1)}, bf16[1024,1024]{1,0:T(8,128)(2,1)}, u32[]{:S(2)}) %copy-start) | copy-done | bytes 2097176
  7.7 0.0 copy-done.2
  7.7 0.0 copy-done.3
  7.7 0.1 tables.1
  7.8 0.0 collective-permute-done.2.refs_0_
  7.9 0.0 copy-start.1
  7.9 2.0 %attend.2 = (bf16[272,128]{1,0:T(8,128)(2,1)S(1)}, bf16[272,128]{1,0:T(8,128)(2,1)S(1)}) custom-call(bf16[32,1024]{1,0:T(8,128)(2,1)S(1)} %collective-permute-done.2.refs_0_, bf16[32,1024]{1,0:T(8,128)(2,1)S(1)} %hold.3.refs_1_, bf16[1024,1024]{1,0:T(8,128)(2,1)S(1)} %get-tuple-element.18.after.refs_1_.refs_2_, ...), custom_call_target="tpu_custom_call" | custom-call | flops 536870912 | bytes 8388608 | tf_op jit(solution)/shard_map/attend/pallas_call | solution.py:188
  9.8 1.1 %collective-permute-start.3 = (bf16[272,128]{1,0:T(8,128)(2,1)S(1)}, bf16[272,128]{1,0:T(8,128)(2,1)S(1)}, u32[]{:S(2)}, u32[]{:S(2)}) collective-permute-start(bf16[272,128]{1,0:T(8,128)(2,1)S(1)} %get-tuple-element.25), channel_id=1, source_target_pairs={{0,8},{4,12},{8,0},{12,4},{1,9},{5,13},{9,1},{13,5},{2,10},{6,14},... | collective-permute-start | bytes 208904 | tf_op jit(solution)/shard_map/ppermute | solution.py:295
  11.0 0.5 %collective-permute-start.4 = (bf16[272,128]{1,0:T(8,128)(2,1)S(1)}, bf16[272,128]{1,0:T(8,128)(2,1)S(1)}, u32[]{:S(2)}, u32[]{:S(2)}) collective-permute-start(bf16[272,128]{1,0:T(8,128)(2,1)S(1)} %get-tuple-element.23.refs_8_), channel_id=1, source_target_pairs={{0,12},{4,8},{8,4},{12,0},{1,13},{5,9},{9,5},{13,1},{2,14},{6,10},... | collective-permute-start | bytes 208904 | tf_op jit(solution)/shard_map/ppermute | solution.py:295
  11.5 0.0 copy-done.1
  11.5 2.0 %attend.3 = (bf16[272,128]{1,0:T(8,128)(2,1)S(1)}, bf16[272,128]{1,0:T(8,128)(2,1)S(1)}) custom-call(bf16[32,1024]{1,0:T(8,128)(2,1)S(1)} %copy-done.1, bf16[32,1024]{1,0:T(8,128)(2,1)S(1)} %collective-permute-done.refs_2_.refs_1_, bf16[1024,1024]{1,0:T(8,128)(2,1)S(1)} %get-tuple-element.18.after.refs_1_.refs_2_, ...), custom_call_target="tpu_custom_call" | custom-call | flops 536870912 | bytes 8388608 | tf_op jit(solution)/shard_map/attend/pallas_call | solution.py:188
  13.4 0.6 %collective-permute-start.5 = (bf16[272,128]{1,0:T(8,128)(2,1)S(1)}, bf16[272,128]{1,0:T(8,128)(2,1)S(1)}, u32[]{:S(2)}, u32[]{:S(2)}) collective-permute-start(bf16[272,128]{1,0:T(8,128)(2,1)S(1)} %get-tuple-element.30), channel_id=1, source_target_pairs={{0,4},{4,0},{8,12},{12,8},{1,5},{5,1},{9,13},{13,9},{2,6},{6,2},{1... | collective-permute-start | bytes 208904 | tf_op jit(solution)/shard_map/ppermute | solution.py:295
  14.1 0.5 %collective-permute-done.3.refs_0_ = bf16[272,128]{1,0:T(8,128)(2,1)S(1)} collective-permute-done((bf16[272,128]{1,0:T(8,128)(2,1)S(1)}, bf16[272,128]{1,0:T(8,128)(2,1)S(1)}, u32[]{:S(2)}, u32[]{:S(2)}) %collective-permute-start.3) | collective-permute-done | bytes 69664 | tf_op jit(solution)/shard_map/ppermute | solution.py:295
  14.5 0.2 %gather.1 = (f32[32,1024]{1,0:T(8,128)S(1)}, f32[32,1024]{1,0:T(8,128)S(1)}, f32[32,1024]{1,0:T(8,128)S(1)}, bf16[128,1024]{1,0:T(8,128)(2,1)S(1)}) custom-call(bf16[272,128]{1,0:T(8,128)(2,1)S(1)} %get-tuple-element.24.refs_0_, bf16[272,128]{1,0:T(8,128)(2,1)S(1)} %hold.4.refs_1_), custom_call_target="tpu_custom_call" | custom-call | bytes 1048576 | tf_op jit(solution)/shard_map/gather/pallas_call | solution.py:254
  14.7 0.6 %collective-permute-done.4.refs_0_ = bf16[272,128]{1,0:T(8,128)(2,1)S(1)} collective-permute-done((bf16[272,128]{1,0:T(8,128)(2,1)S(1)}, bf16[272,128]{1,0:T(8,128)(2,1)S(1)}, u32[]{:S(2)}, u32[]{:S(2)}) %collective-permute-start.4) | collective-permute-done | bytes 69664 | tf_op jit(solution)/shard_map/ppermute | solution.py:295
  15.4 0.0 collective-permute-done.5.refs_1_
  15.4 0.9 %merge.1 = bf16[32,1024]{1,0:T(8,128)(2,1)} custom-call(f32[32,1024]{1,0:T(8,128)S(1)} %get-tuple-element.26.refs_1_.mixed, f32[32,1024]{1,0:T(8,128)S(1)} %get-tuple-element.27.total, f32[32,1024]{1,0:T(8,128)S(1)} %get-tuple-element.28.top, bf16[128,1024]{1,0:T(8,128)(2,1)S(1)} %get-tuple-element.29.spread, bf16[272,128]{1,0:T(8,128)(2,1)S(1)} %hold.5.refs_0_, ...), custom_call_target="tpu_custom_call" | custom-call | tf_op jit(solution)/shard_map/merge/pallas_call | solution.py:280
  (3 shorter events, 0.0 us)
Async XLA Ops:
  0.0 6.1 %collective-permute-start = (bf16[32,1024]{1,0:T(8,128)(2,1)}, bf16[32,1024]{1,0:T(8,128)(2,1)S(1)}, u32[]{:S(2)}, u32[]{:S(2)}) collective-permute-start(bf16[32,1024]{1,0:T(8,128)(2,1)} %refs_0_.3), channel_id=1, source_target_pairs={{0,4},{4,0},{8,12},{12,8},{1,5},{5,1},{9,13},{13,9},{2,6},{6,2},{1... | collective-permute-start | bytes 196616 | tf_op jit(solution)/shard_map/ppermute | solution.py:295
  0.5 5.7 %collective-permute-start.1 = (bf16[32,1024]{1,0:T(8,128)(2,1)}, bf16[32,1024]{1,0:T(8,128)(2,1)S(1)}, u32[]{:S(2)}, u32[]{:S(2)}) collective-permute-start(bf16[32,1024]{1,0:T(8,128)(2,1)} %refs_0_.3), channel_id=1, source_target_pairs={{0,8},{4,12},{8,0},{12,4},{1,9},{5,13},{9,1},{13,5},{2,10},{6,14},... | collective-permute-start | bytes 196616 | tf_op jit(solution)/shard_map/ppermute | solution.py:295
  6.1 1.6 %copy-start = (bf16[1024,1024]{1,0:T(8,128)(2,1)S(1)}, bf16[1024,1024]{1,0:T(8,128)(2,1)}, u32[]{:S(2)}) copy-start(bf16[1024,1024]{1,0:T(8,128)(2,1)} %refs_5_.3) | copy-start | bytes 6291460
  6.1 1.6 %copy-start.2 = (f32[8]{0:T(128)S(1)}, f32[8]{0:T(128)}, u32[]{:S(2)}) copy-start(f32[8]{0:T(128)} %slopes.1) | copy-start | bytes 100
  6.1 1.6 %copy-start.3 = (s32[128]{0:T(128)S(1)}, s32[128]{0:T(128)}, u32[]{:S(2)}) copy-start(s32[128]{0:T(128)} %ids.1) | copy-start | bytes 1540
  6.2 1.7 %collective-permute-start.2 = (bf16[32,1024]{1,0:T(8,128)(2,1)S(1)}, bf16[32,1024]{1,0:T(8,128)(2,1)S(1)}, u32[]{:S(2)}, u32[]{:S(2)}) collective-permute-start(bf16[32,1024]{1,0:T(8,128)(2,1)S(1)} %hold.3.refs_1_), channel_id=1, source_target_pairs={{0,4},{4,0},{8,12},{12,8},{1,5},{5,1},{9,13},{13,9},{2,6},{6,2},{1... | collective-permute-start | bytes 196616 | tf_op jit(solution)/shard_map/ppermute | solution.py:295
  7.9 3.6 %copy-start.1 = (bf16[32,1024]{1,0:T(8,128)(2,1)S(1)}, bf16[32,1024]{1,0:T(8,128)(2,1)}, u32[]{:S(2)}) copy-start(bf16[32,1024]{1,0:T(8,128)(2,1)} %refs_0_.3) | copy-start | bytes 196612
  9.8 4.7 %collective-permute-start.3 = (bf16[272,128]{1,0:T(8,128)(2,1)S(1)}, bf16[272,128]{1,0:T(8,128)(2,1)S(1)}, u32[]{:S(2)}, u32[]{:S(2)}) collective-permute-start(bf16[272,128]{1,0:T(8,128)(2,1)S(1)} %get-tuple-element.25), channel_id=1, source_target_pairs={{0,8},{4,12},{8,0},{12,4},{1,9},{5,13},{9,1},{13,5},{2,10},{6,14},... | collective-permute-start | bytes 208904 | tf_op jit(solution)/shard_map/ppermute | solution.py:295
  11.0 4.4 %collective-permute-start.4 = (bf16[272,128]{1,0:T(8,128)(2,1)S(1)}, bf16[272,128]{1,0:T(8,128)(2,1)S(1)}, u32[]{:S(2)}, u32[]{:S(2)}) collective-permute-start(bf16[272,128]{1,0:T(8,128)(2,1)S(1)} %get-tuple-element.23.refs_8_), channel_id=1, source_target_pairs={{0,12},{4,8},{8,4},{12,0},{1,13},{5,9},{9,5},{13,1},{2,14},{6,10},... | collective-permute-start | bytes 208904 | tf_op jit(solution)/shard_map/ppermute | solution.py:295
  13.4 1.9 %collective-permute-start.5 = (bf16[272,128]{1,0:T(8,128)(2,1)S(1)}, bf16[272,128]{1,0:T(8,128)(2,1)S(1)}, u32[]{:S(2)}, u32[]{:S(2)}) collective-permute-start(bf16[272,128]{1,0:T(8,128)(2,1)S(1)} %get-tuple-element.30), channel_id=1, source_target_pairs={{0,4},{4,0},{8,12},{12,8},{1,5},{5,1},{9,13},{13,9},{2,6},{6,2},{1... | collective-permute-start | bytes 208904 | tf_op jit(solution)/shard_map/ppermute | solution.py:295
